TPU v7x, 32 devices: a whole 2x2x4 slice. The times are simulated.
32 devices in a mesh: fsdp: 8 (over z, x), rep: 4 (over y, core).
Axes of the slice: x: 2, y: 2, z: 4, core: 2. Of those that a mesh axis runs over, the one named last changes fastest.
Arguments:
- tokens: bfloat16 [16384, 2048], P(('fsdp', 'rep')), may hold values from -6 to 6
- segments: int32 [16384], P(('fsdp', 'rep')), may hold values from 0 to 255, never falling along the last dimension, each value on 1 to 128 neighbouring positions
- cotangent: bfloat16 [16384, 2048], P(('fsdp', 'rep')), may hold values from -6 to 6
- gain_one: bfloat16 [2048], P(('fsdp', 'rep')), may hold values from 0.5 to 1.5
- w_query: bfloat16 [2048, 2048], P(('fsdp', 'rep')), may hold values from -0.125 to 0.125
- w_key: bfloat16 [2048, 2048], P(('fsdp', 'rep')), may hold values from -0.125 to 0.125
- w_value: bfloat16 [2048, 4096], P(('fsdp', 'rep')), may hold values from -0.125 to 0.125
- w_gate: bfloat16 [2048, 4096], P(('fsdp', 'rep')), may hold values from -0.125 to 0.125
- w_beta: bfloat16 [2048, 16], P(('fsdp', 'rep')), may hold values from -0.125 to 0.125
- w_alpha: bfloat16 [2048, 16], P(('fsdp', 'rep')), may hold values from -0.125 to 0.125
- conv_q: bfloat16 [4, 2048], P(None, ('fsdp', 'rep')), may hold values from -3 to 3
- conv_k: bfloat16 [4, 2048], P(None, ('fsdp', 'rep')), may hold values from -3 to 3
- conv_v: bfloat16 [4, 4096], P(None, ('fsdp', 'rep')), may hold values from -3 to 3
- a_log: float32 [16], replicated, may hold values from 0 to 2.77
- dt_bias: float32 [16], replicated, may hold values from -6 to -2
- norm_gain: bfloat16 [256], P(('fsdp', 'rep')), may hold values from 0.5 to 1.5
- w_out: bfloat16 [4096, 2048], P(None, ('fsdp', 'rep')), may hold values from -0.1875 to 0.1875
- gain_two: bfloat16 [2048], P(('fsdp', 'rep')), may hold values from 0.5 to 1.5
- w_ffgate: bfloat16 [2048, 5632], P(('fsdp', 'rep')), may hold values from -0.125 to 0.125
- w_ffup: bfloat16 [2048, 5632], P(('fsdp', 'rep')), may hold values from -0.125 to 0.125
- w_down: bfloat16 [5632, 2048], P(None, ('fsdp', 'rep')), may hold values from -0.15625 to 0.15625
Outputs:
- output: bfloat16 [16384, 2048], P(('fsdp', 'rep'))
- grad_tokens: float32 [16384, 2048], P(('fsdp', 'rep'))
- grad_gain_one: float32 [2048], P(('fsdp', 'rep'))
- grad_w_query: float32 [2048, 2048], P(('fsdp', 'rep'))
- grad_w_key: float32 [2048, 2048], P(('fsdp', 'rep'))
- grad_w_value: float32 [2048, 4096], P(('fsdp', 'rep'))
- grad_w_gate: float32 [2048, 4096], P(('fsdp', 'rep'))
- grad_w_beta: float32 [2048, 16], P(('fsdp', 'rep'))
- grad_w_alpha: float32 [2048, 16], P(('fsdp', 'rep'))
- grad_conv_q: float32 [4, 2048], P(None, ('fsdp', 'rep'))
- grad_conv_k: float32 [4, 2048], P(None, ('fsdp', 'rep'))
- grad_conv_v: float32 [4, 4096], P(None, ('fsdp', 'rep'))
- grad_a_log: float32 [16], replicated
- grad_dt_bias: float32 [16], replicated
- grad_norm_gain: float32 [256], P(('fsdp', 'rep'))
- grad_w_out: float32 [4096, 2048], P(None, ('fsdp', 'rep'))
- grad_gain_two: float32 [2048], P(('fsdp', 'rep'))
- grad_w_ffgate: float32 [2048, 5632], P(('fsdp', 'rep'))
- grad_w_ffup: float32 [2048, 5632], P(('fsdp', 'rep'))
- grad_w_down: float32 [5632, 2048], P(None, ('fsdp', 'rep'))
Inputs may be any that keep to these rules, and one draw needn't show every extreme that they name: `segments`: document numbers never fall along the tokens; a document covers 1 to 128 consecutive tokens.
All inputs are finite; a program needn't handle non-finite values.
Results may differ from a plain program's by a relative error of at most 0.011.
Values may be sent and summed in bfloat16 or wider, within the bound.
No kernel may reach another device: no remote copies, remote signals or barrier semaphores. Data moves between devices by JAX's collectives and lax.ppermute only.
A program may use at most 640 MiB of HBM per device.

v0:
```python
import jax
import jax.numpy as jnp
from jax import lax
from jax.sharding import PartitionSpec as P

HEADS = 16
SPAN = 64
SEQ = 256
MB = 2
HK = 2048
HV = 4096


def rms_norm(values, gain):
    return values * lax.rsqrt(jnp.mean(values * values, axis=-1, keepdims=True) + 1e-06) * gain


def short_conv(signal, conv_taps, doc_ids):
    width = conv_taps.shape[0]
    summed = signal * conv_taps[width - 1]
    for offset in range(1, width):
        shifted = jnp.pad(signal, ((0, 0), (offset, 0), (0, 0)))[:, :-offset]
        shifted_ids = jnp.pad(doc_ids, ((0, 0), (offset, 0)), constant_values=-1)[:, :-offset]
        same_doc = (shifted_ids == doc_ids).astype(signal.dtype)[..., None]
        summed = summed + shifted * same_doc * conv_taps[width - 1 - offset]
    return jax.nn.silu(summed)


def span_step(state_mat, block_in):
    query_part, key_part, value_part, beta_part, decay_part, start_part = block_in
    block_len = query_part.shape[2]
    highest = lax.Precision.HIGHEST
    log_decay = jnp.cumsum(decay_part, axis=-1)
    doc_count = jnp.cumsum(start_part, axis=-1)
    same_doc = doc_count[:, :, None] == doc_count[:, None, :]
    positions = jnp.arange(block_len)
    lower_incl = positions[:, None] >= positions[None, :]
    lower_strict = (positions[:, None] > positions[None, :]).astype(decay_part.dtype)
    linked = (same_doc & lower_incl)[:, None].astype(decay_part.dtype)
    log_gap = log_decay[..., :, None] - log_decay[..., None, :]
    decay_mat = jnp.exp(log_gap * linked) * linked
    carry_in = jnp.exp(log_decay) * (doc_count == 0)[:, None, :].astype(decay_part.dtype)
    key_gram = jnp.einsum("bhid,bhjd->bhij", key_part, key_part, precision=highest)
    nilpotent = -beta_part[..., :, None] * (decay_mat * key_gram * lower_strict)
    inverse = jnp.eye(block_len, dtype=decay_part.dtype) + nilpotent
    power_mat = nilpotent
    for section_num in range(block_len.bit_length() - 2):
        power_mat = jnp.matmul(power_mat, power_mat, precision=highest)
        inverse = inverse + jnp.matmul(inverse, power_mat, precision=highest)
    recalled = jnp.einsum("bhid,bhed->bhie", key_part, state_mat, precision=highest)
    target = beta_part[..., None] * (value_part - carry_in[..., None] * recalled)
    update = jnp.matmul(inverse, target, precision=highest)
    scores = jnp.einsum("bhid,bhjd->bhij", query_part, key_part, precision=highest) * decay_mat
    output = carry_in[..., None] * jnp.einsum(
        "bhid,bhed->bhie", query_part, state_mat, precision=highest
    )
    output = output + jnp.matmul(scores, update, precision=highest)
    weighted = decay_mat[..., -1, :][..., None] * update
    new_state = carry_in[..., -1][..., None, None] * state_mat
    new_state = new_state + jnp.einsum("bhje,bhjd->bhed", weighted, key_part, precision=highest)
    return (new_state, output)


def mixer(
    projected, conv_q, conv_k, conv_v, a_log, dt_bias, norm_gain, doc_ids, head_count, block_size
):
    batch_n = projected.shape[0]
    length = projected.shape[1]
    key_width = conv_q.shape[1]
    value_width = conv_v.shape[1]
    key_head = key_width // head_count
    value_head = value_width // head_count
    base = 2 * key_width + 2 * value_width
    queries = short_conv(projected[..., :key_width], conv_q, doc_ids).reshape(
        batch_n, length, head_count, key_head
    )
    key_vecs = short_conv(projected[..., key_width : 2 * key_width], conv_k, doc_ids).reshape(
        batch_n, length, head_count, key_head
    )
    values = short_conv(
        projected[..., 2 * key_width : 2 * key_width + value_width], conv_v, doc_ids
    ).reshape(batch_n, length, head_count, value_head)
    out_gate = projected[..., 2 * key_width + value_width : base].reshape(
        batch_n, length, head_count, value_head
    )
    beta_rate = jax.nn.sigmoid(projected[..., base : base + head_count])
    decay = -jnp.exp(a_log) * jax.nn.softplus(projected[..., base + head_count :] + dt_bias)
    queries = (
        queries
        * lax.rsqrt(jnp.sum(queries * queries, axis=-1, keepdims=True) + 1e-06)
        * key_head ** (-0.5)
    )
    key_vecs = key_vecs * lax.rsqrt(jnp.sum(key_vecs * key_vecs, axis=-1, keepdims=True) + 1e-06)
    previous = jnp.pad(doc_ids, ((0, 0), (1, 0)), constant_values=-1)[:, :-1]
    doc_start = (doc_ids != previous).astype(decay.dtype)
    num_blocks = length // block_size

    def split_heads(array):
        return array.reshape(
            batch_n, num_blocks, block_size, head_count, array.shape[-1]
        ).transpose(1, 0, 3, 2, 4)

    def split_rates(array):
        return array.reshape(batch_n, num_blocks, block_size, head_count).transpose(1, 0, 3, 2)

    starts = doc_start.reshape(batch_n, num_blocks, block_size).transpose(1, 0, 2)
    state_mat = jnp.zeros((batch_n, head_count, value_head, key_head), decay.dtype)
    final, outputs = lax.scan(
        jax.checkpoint(span_step),
        state_mat,
        (
            split_heads(queries),
            split_heads(key_vecs),
            split_heads(values),
            split_rates(beta_rate),
            split_rates(decay),
            starts,
        ),
    )
    recur = outputs.transpose(1, 0, 3, 2, 4).reshape(batch_n, length, head_count, value_head)
    recur = (
        recur
        * lax.rsqrt(jnp.mean(recur * recur, axis=-1, keepdims=True) + 1e-05)
        * norm_gain
        * jax.nn.silu(out_gate)
    )
    return recur.reshape(batch_n, length, value_width)


def pinned(values, anchor):
    return lax.optimization_barrier((values, anchor))[0]


def cross(left, right):
    return lax.dot_general(
        left, right, (((0,), (0,)), ((), ())), preferred_element_type=jnp.float32
    )


def against(grad_rows, weight):
    return lax.dot_general(
        grad_rows, weight, (((1,), (1,)), ((), ())), preferred_element_type=jnp.float32
    )


def swish_product(first, second):
    return jax.nn.silu(first) * second


def on_device(
    tokens,
    segments,
    cotangent,
    gain_one,
    w_query,
    w_key,
    w_value,
    w_gate,
    w_beta,
    w_alpha,
    conv_q,
    conv_k,
    conv_v,
    a_log,
    dt_bias,
    norm_gain,
    w_out,
    gain_two,
    w_ffgate,
    w_ffup,
    w_down,
):
    mixer_shards = (
        gain_one,
        w_query,
        w_key,
        w_value,
        w_gate,
        w_beta,
        w_alpha,
        conv_q,
        conv_k,
        conv_v,
        norm_gain,
        w_out,
    )
    ffn_shards = (gain_two, w_ffgate, w_ffup, w_down)
    batch_rows = tokens.shape[0] // MB
    seq_count = batch_rows // SEQ
    widths = (HK, HK, HV, HV, HEADS, HEADS)
    mixer_full = (
        lax.all_gather(mixer_shards[0], ("fsdp", "rep"), axis=0, tiled=True),
        lax.all_gather(mixer_shards[1], ("fsdp", "rep"), axis=0, tiled=True),
        lax.all_gather(mixer_shards[2], ("fsdp", "rep"), axis=0, tiled=True),
        lax.all_gather(mixer_shards[3], ("fsdp", "rep"), axis=0, tiled=True),
        lax.all_gather(mixer_shards[4], ("fsdp", "rep"), axis=0, tiled=True),
        lax.all_gather(mixer_shards[5], ("fsdp", "rep"), axis=0, tiled=True),
        lax.all_gather(mixer_shards[6], ("fsdp", "rep"), axis=0, tiled=True),
        lax.all_gather(mixer_shards[7], ("fsdp", "rep"), axis=1, tiled=True),
        lax.all_gather(mixer_shards[8], ("fsdp", "rep"), axis=1, tiled=True),
        lax.all_gather(mixer_shards[9], ("fsdp", "rep"), axis=1, tiled=True),
        lax.all_gather(mixer_shards[10], ("fsdp", "rep"), axis=0, tiled=True),
        lax.all_gather(mixer_shards[11], ("fsdp", "rep"), axis=1, tiled=True),
    )
    ffn_full = (
        lax.all_gather(ffn_shards[0], ("fsdp", "rep"), axis=0, tiled=True),
        lax.all_gather(ffn_shards[1], ("fsdp", "rep"), axis=0, tiled=True),
        lax.all_gather(ffn_shards[2], ("fsdp", "rep"), axis=0, tiled=True),
        lax.all_gather(ffn_shards[3], ("fsdp", "rep"), axis=1, tiled=True),
    )
    gain_first = mixer_full[0].astype(jnp.float32)
    gain_second = ffn_full[0].astype(jnp.float32)
    taps_q32 = mixer_full[7].astype(jnp.float32)
    taps_k32 = mixer_full[8].astype(jnp.float32)
    taps_v32 = mixer_full[9].astype(jnp.float32)
    gain_out32 = mixer_full[10].astype(jnp.float32)
    results = []
    pulls = []
    kept_normed_one = []
    kept_mixed = []
    kept_middle = []
    kept_normed_two = []
    kept_gate = []
    kept_up = []
    kept_hidden = []
    for micro in range(MB):
        row_start = micro * batch_rows
        input_rows = tokens[row_start : row_start + batch_rows]
        doc_ids = segments[row_start : row_start + batch_rows].reshape(seq_count, SEQ)
        inputs = input_rows.astype(jnp.float32)
        normed_one = rms_norm(inputs, gain_first).astype(jnp.bfloat16)
        projected = jnp.concatenate(
            [
                jnp.dot(normed_one, mixer_full[slot], preferred_element_type=jnp.float32)
                for slot in range(1, 7)
            ],
            axis=1,
        )

        def mix_local(
            proj_in, taps_q, taps_k, taps_v, log_scale, step_bias, gain_out, doc_ids=doc_ids
        ):
            mixed_seq = mixer(
                proj_in.reshape(seq_count, SEQ, -1),
                taps_q,
                taps_k,
                taps_v,
                log_scale,
                step_bias,
                gain_out,
                doc_ids,
                HEADS,
                SPAN,
            )
            return mixed_seq.reshape(batch_rows, -1)

        mixed, mix_pull = jax.vjp(
            mix_local, projected, taps_q32, taps_k32, taps_v32, a_log, dt_bias, gain_out32
        )
        mixed_low = mixed.astype(jnp.bfloat16)
        middle = inputs + jnp.dot(mixed_low, mixer_full[11], preferred_element_type=jnp.float32)
        normed_two = rms_norm(middle, gain_second).astype(jnp.bfloat16)
        gate_pre = jnp.dot(normed_two, ffn_full[1], preferred_element_type=jnp.float32)
        up_pre = jnp.dot(normed_two, ffn_full[2], preferred_element_type=jnp.float32)
        hidden = swish_product(gate_pre, up_pre).astype(jnp.bfloat16)
        layer_out = (
            middle + jnp.dot(hidden, ffn_full[3], preferred_element_type=jnp.float32)
        ).astype(jnp.bfloat16)
        results.append(layer_out)
        pulls.append(mix_pull)
        kept_normed_one.append(normed_one)
        kept_mixed.append(mixed_low)
        kept_middle.append(middle)
        kept_normed_two.append(normed_two)
        kept_gate.append(gate_pre)
        kept_up.append(up_pre)
        kept_hidden.append(hidden)
    all_out = jnp.concatenate(results, axis=0)
    again = pinned(mixer_shards, all_out)
    mixer_back = (
        lax.all_gather(again[0], ("fsdp", "rep"), axis=0, tiled=True),
        lax.all_gather(again[1], ("fsdp", "rep"), axis=0, tiled=True),
        lax.all_gather(again[2], ("fsdp", "rep"), axis=0, tiled=True),
        lax.all_gather(again[3], ("fsdp", "rep"), axis=0, tiled=True),
        lax.all_gather(again[4], ("fsdp", "rep"), axis=0, tiled=True),
        lax.all_gather(again[5], ("fsdp", "rep"), axis=0, tiled=True),
        lax.all_gather(again[6], ("fsdp", "rep"), axis=0, tiled=True),
        lax.all_gather(again[7], ("fsdp", "rep"), axis=1, tiled=True),
        lax.all_gather(again[8], ("fsdp", "rep"), axis=1, tiled=True),
        lax.all_gather(again[9], ("fsdp", "rep"), axis=1, tiled=True),
        lax.all_gather(again[10], ("fsdp", "rep"), axis=0, tiled=True),
        lax.all_gather(again[11], ("fsdp", "rep"), axis=1, tiled=True),
    )
    again_ffn = pinned(ffn_shards, all_out)
    ffn_back = (
        lax.all_gather(again_ffn[0], ("fsdp", "rep"), axis=0, tiled=True),
        lax.all_gather(again_ffn[1], ("fsdp", "rep"), axis=0, tiled=True),
        lax.all_gather(again_ffn[2], ("fsdp", "rep"), axis=0, tiled=True),
        lax.all_gather(again_ffn[3], ("fsdp", "rep"), axis=1, tiled=True),
    )
    inputs = tokens.astype(jnp.float32)
    normed_one = jnp.concatenate(kept_normed_one, axis=0)
    mixed_low = jnp.concatenate(kept_mixed, axis=0)
    middle = jnp.concatenate(kept_middle, axis=0)
    normed_two = jnp.concatenate(kept_normed_two, axis=0)
    gate_pre = jnp.concatenate(kept_gate, axis=0)
    up_pre = jnp.concatenate(kept_up, axis=0)
    hidden = jnp.concatenate(kept_hidden, axis=0)
    incoming = cotangent.astype(jnp.float32)
    grad_down = cross(hidden, cotangent)
    dhidden = against(cotangent, ffn_back[3])
    unused_value, glu_pull = jax.vjp(swish_product, gate_pre, up_pre)
    dgate, dup = glu_pull(dhidden)
    dgate_low = dgate.astype(jnp.bfloat16)
    dup_low = dup.astype(jnp.bfloat16)
    grad_ffgate = cross(normed_two, dgate_low)
    grad_ffup = cross(normed_two, dup_low)
    dnormed_two = against(dgate_low, ffn_back[1]) + against(dup_low, ffn_back[2])
    unused_norm, second_pull = jax.vjp(rms_norm, middle, gain_second)
    dmiddle_part, grad_gain_second = second_pull(dnormed_two)
    dmiddle = incoming + dmiddle_part
    dmiddle_low = dmiddle.astype(jnp.bfloat16)
    grad_out = cross(mixed_low, dmiddle_low)
    dmixed = against(dmiddle_low, mixer_back[11])
    dproj_parts = []
    mix_totals = None
    for micro in range(MB):
        row_start = micro * batch_rows
        pulled = pulls[micro](dmixed[row_start : row_start + batch_rows])
        dproj_parts.append(pulled[0])
        if micro == 0:
            mix_totals = pulled[1:]
        else:
            mix_totals = tuple((total + grad for total, grad in zip(mix_totals, pulled[1:])))
    grad_taps_q, grad_taps_k, grad_taps_v, grad_log_scale, grad_step_bias, grad_gain_out = (
        mix_totals
    )
    dprojected_low = jnp.concatenate(dproj_parts, axis=0).astype(jnp.bfloat16)
    proj_grads = []
    dnormed_one = jnp.zeros(inputs.shape, jnp.float32)
    column = 0
    for slot in range(6):
        piece = dprojected_low[:, column : column + widths[slot]]
        proj_grads.append(cross(normed_one, piece))
        dnormed_one = dnormed_one + against(piece, mixer_back[slot + 1])
        column = column + widths[slot]
    unused_first, first_pull = jax.vjp(rms_norm, inputs, gain_first)
    dinput_part, grad_gain_first = first_pull(dnormed_one)
    grad_inputs = dmiddle + dinput_part
    mixer_grads = (
        lax.psum_scatter(grad_gain_first, ("fsdp", "rep"), scatter_dimension=0, tiled=True),
        lax.psum_scatter(proj_grads[0], ("fsdp", "rep"), scatter_dimension=0, tiled=True),
        lax.psum_scatter(proj_grads[1], ("fsdp", "rep"), scatter_dimension=0, tiled=True),
        lax.psum_scatter(proj_grads[2], ("fsdp", "rep"), scatter_dimension=0, tiled=True),
        lax.psum_scatter(proj_grads[3], ("fsdp", "rep"), scatter_dimension=0, tiled=True),
        lax.psum_scatter(proj_grads[4], ("fsdp", "rep"), scatter_dimension=0, tiled=True),
        lax.psum_scatter(proj_grads[5], ("fsdp", "rep"), scatter_dimension=0, tiled=True),
        lax.psum_scatter(grad_taps_q, ("fsdp", "rep"), scatter_dimension=1, tiled=True),
        lax.psum_scatter(grad_taps_k, ("fsdp", "rep"), scatter_dimension=1, tiled=True),
        lax.psum_scatter(grad_taps_v, ("fsdp", "rep"), scatter_dimension=1, tiled=True),
        lax.psum_scatter(grad_gain_out, ("fsdp", "rep"), scatter_dimension=0, tiled=True),
        lax.psum_scatter(grad_out, ("fsdp", "rep"), scatter_dimension=1, tiled=True),
    )
    ffn_grads = (
        lax.psum_scatter(grad_gain_second, ("fsdp", "rep"), scatter_dimension=0, tiled=True),
        lax.psum_scatter(grad_ffgate, ("fsdp", "rep"), scatter_dimension=0, tiled=True),
        lax.psum_scatter(grad_ffup, ("fsdp", "rep"), scatter_dimension=0, tiled=True),
        lax.psum_scatter(grad_down, ("fsdp", "rep"), scatter_dimension=1, tiled=True),
    )
    head_grads = lax.psum((grad_log_scale, grad_step_bias), ("fsdp", "rep"))
    return (
        all_out,
        grad_inputs,
        mixer_grads[0],
        mixer_grads[1],
        mixer_grads[2],
        mixer_grads[3],
        mixer_grads[4],
        mixer_grads[5],
        mixer_grads[6],
        mixer_grads[7],
        mixer_grads[8],
        mixer_grads[9],
        head_grads[0],
        head_grads[1],
        mixer_grads[10],
        mixer_grads[11],
        ffn_grads[0],
        ffn_grads[1],
        ffn_grads[2],
        ffn_grads[3],
    )


def solution(mesh):
    placed = (
        P(("fsdp", "rep"), None),
        P(("fsdp", "rep")),
        P(("fsdp", "rep"), None),
        P(("fsdp", "rep")),
        P(("fsdp", "rep"), None),
        P(("fsdp", "rep"), None),
        P(("fsdp", "rep"), None),
        P(("fsdp", "rep"), None),
        P(("fsdp", "rep"), None),
        P(("fsdp", "rep"), None),
        P(None, ("fsdp", "rep")),
        P(None, ("fsdp", "rep")),
        P(None, ("fsdp", "rep")),
        P(),
        P(),
        P(("fsdp", "rep")),
        P(None, ("fsdp", "rep")),
        P(("fsdp", "rep")),
        P(("fsdp", "rep"), None),
        P(("fsdp", "rep"), None),
        P(None, ("fsdp", "rep")),
    )
    return jax.shard_map(
        on_device,
        mesh=mesh,
        in_specs=placed,
        out_specs=(
            P(("fsdp", "rep"), None),
            P(("fsdp", "rep"), None),
            P(("fsdp", "rep")),
            P(("fsdp", "rep"), None),
            P(("fsdp", "rep"), None),
            P(("fsdp", "rep"), None),
            P(("fsdp", "rep"), None),
            P(("fsdp", "rep"), None),
            P(("fsdp", "rep"), None),
            P(None, ("fsdp", "rep")),
            P(None, ("fsdp", "rep")),
            P(None, ("fsdp", "rep")),
            P(),
            P(),
            P(("fsdp", "rep")),
            P(None, ("fsdp", "rep")),
            P(("fsdp", "rep")),
            P(("fsdp", "rep"), None),
            P(("fsdp", "rep"), None),
            P(None, ("fsdp", "rep")),
        ),
        check_vma=False,
    )
```

profile of v0, /device:TPU:0, one launch (start us, length us, event | category | flops | bytes accessed | tf_op | source)
XLA Modules:
  0.0 6076.0 jit_solution(2295323409670093408)
XLA Ops:
  13.5 42.5 all-reduce.89
  56.5 42.1 all-gather
  141.8 38.4 all-gather.3
  218.8 38.3 all_gather.86
  298.3 105.4 %all-gather.29.cloned.1.call-done = bf16[2048,4096]{1,0:T(8,128)(2,1)} async-done(((bf16[64,4096]{1,0:T(8,128)(2,1)}), bf16[2048,4096]{1,0:T(8,128)(2,1)}) %all-gather.29.cloned.1.call-update) | async-done | bytes 16777232 | tf_op jit(solution)/shard_map/all_gather | solution.py:196
  555.7 127.0 %while.81 = (s32[]{:T(128)}, f32[1,16,256,128]{3,2,1,0:T(8,128)S(1)}, f32[4,1,16,64,256]{4,3,2,1,0:T(8,128)}, f32[4,1,16,256,128]{4,3,2,1,0:T(8,128)}, f32[4,1,1...) while((s32[]{:T(128)}, ...), condition=%wide.region_15.17_spmd.clone, body=%wide.region_12.16_spmd.clone.sunk | while | flops 2321129472 | bytes 34091984 | solution.py:108
  727.2 127.0 %while.80 = (s32[]{:T(128)}, f32[1,16,256,128]{3,2,1,0:T(8,128)S(1)}, f32[4,1,16,64,256]{4,3,2,1,0:T(8,128)}, f32[4,1,16,256,128]{4,3,2,1,0:T(8,128)}, f32[4,1,1...) while((s32[]{:T(128)}, ...), condition=%wide.region_6.8_spmd.clone, body=%wide.region_3.7_spmd.clone.sunk | while | flops 2321129472 | bytes 34091984 | solution.py:108
  1028.6 118.5 %all-gather.39.cloned.1.call-done = bf16[5632,2048]{0,1:T(8,128)(2,1)} async-done(((bf16[5632,64]{0,1:T(8,128)(2,1)}), bf16[5632,2048]{0,1:T(8,128)(2,1)}) %all-gather.39.cloned.1.call-update) | async-done | bytes 23068688 | tf_op jit(solution)/shard_map/all_gather | solution.py:299
  1173.3 119.3 %all-gather.41.cloned.1.call-done = bf16[2048,5632]{1,0:T(8,128)(2,1)} async-done(((bf16[64,5632]{1,0:T(8,128)(2,1)}), bf16[2048,5632]{1,0:T(8,128)(2,1)}) %all-gather.41.cloned.1.call-update) | async-done | bytes 23068688 | tf_op jit(solution)/shard_map/all_gather | solution.py:297
  1312.1 126.2 %all-gather.43.cloned.1.call-done = bf16[2048,5632]{1,0:T(8,128)(2,1)} async-done(((bf16[64,5632]{1,0:T(8,128)(2,1)}), bf16[2048,5632]{1,0:T(8,128)(2,1)}) %all-gather.43.cloned.1.call-update) | async-done | bytes 23068688 | tf_op jit(solution)/shard_map/all_gather | solution.py:298
  1460.7 93.4 %all-gather.45.cloned.1.call-done = bf16[4096,2048]{0,1:T(8,128)(2,1)} async-done(((bf16[4096,64]{0,1:T(8,128)(2,1)}), bf16[4096,2048]{0,1:T(8,128)(2,1)}) %all-gather.45.cloned.1.call-update) | async-done | bytes 16777232 | tf_op jit(solution)/shard_map/all_gather | solution.py:292
  1602.2 372.5 %while.82 = (s32[]{:T(128)}, f32[1,16,256,128]{3,2,1,0:T(8,128)}, f32[4,1,16,64,128]{4,2,3,0,1:T(8,128)}, f32[4,1,16,64,128]{4,2,3,0,1:T(8,128)}, f32[4,1,16,64,...) while((s32[]{:T(128)}, f32[1,16,256,128]{3,2,1,0:T(8,128)}, ...), condition=%wide.region_33.35_spmd.clone, body=%wide.region_21.34_spmd.clone.sunk | while | flops 6358998016 | bytes 192382256 | solution.py:108
  1980.3 381.0 %while.83 = (s32[]{:T(128)}, f32[1,16,256,128]{3,2,1,0:T(8,128)}, f32[4,1,16,64,128]{4,2,3,0,1:T(8,128)}, f32[4,1,16,64,128]{4,2,3,0,1:T(8,128)}, f32[4,1,16,64,...) while((s32[]{:T(128)}, f32[1,16,256,128]{3,2,1,0:T(8,128)}, ...), condition=%wide.region_49.51_spmd.clone, body=%wide.region_37.50_spmd.clone.sunk | while | flops 6358998016 | bytes 192382256 | solution.py:108
  2701.5 38.7 all-gather.4
  2889.7 125.4 %reduce-scatter.40.cloned.1.call-done = f32[64,16]{1,0:T(8,128)} async-done(((f32[2048,16]{1,0:T(8,128)}), f32[64,16]{1,0:T(8,128)}) %reduce-scatter.40.cloned.1.call-update) | async-done | bytes 4112
  3016.5 132.0 %reduce-scatter.42.cloned.1.call-done = f32[64,16]{1,0:T(8,128)} async-done(((f32[2048,16]{1,0:T(8,128)}), f32[64,16]{1,0:T(8,128)}) %reduce-scatter.42.cloned.1.call-update) | async-done | bytes 4112
  3149.9 180.5 %reduce-scatter.24.cloned.1.call-done = f32[64,2048]{1,0:T(8,128)} async-done(((f32[2048,2048]{1,0:T(8,128)}), f32[64,2048]{1,0:T(8,128)}) %reduce-scatter.24.cloned.1.call-update) | async-done | bytes 524304 | tf_op jit(solution)/shard_map/reduce_scatter | solution.py:352
  3330.4 187.6 %reduce-scatter.26.cloned.1.call-done = f32[64,2048]{1,0:T(8,128)} async-done(((f32[2048,2048]{1,0:T(8,128)}), f32[64,2048]{1,0:T(8,128)}) %reduce-scatter.26.cloned.1.call-update) | async-done | bytes 524304 | tf_op jit(solution)/shard_map/reduce_scatter | solution.py:353
  3517.9 486.9 %reduce-scatter.38.cloned.1.call-done = f32[5632,64]{0,1:T(8,128)} async-done(((f32[5632,2048]{0,1:T(8,128)}), f32[5632,64]{0,1:T(8,128)}) %reduce-scatter.38.cloned.1.call-update) | async-done | bytes 1441808 | tf_op jit(solution)/shard_map/reduce_scatter | solution.py:368
  4004.8 363.2 %reduce-scatter.32.cloned.1.call-done = f32[4096,64]{0,1:T(8,128)} async-done(((f32[4096,2048]{0,1:T(8,128)}), f32[4096,64]{0,1:T(8,128)}) %reduce-scatter.32.cloned.1.call-update) | async-done | bytes 1048592 | tf_op jit(solution)/shard_map/reduce_scatter | solution.py:362
  4368.0 360.3 %reduce-scatter.30.cloned.1.call-done = f32[64,4096]{1,0:T(8,128)} async-done(((f32[2048,4096]{1,0:T(8,128)}), f32[64,4096]{1,0:T(8,128)}) %reduce-scatter.30.cloned.1.call-update) | async-done | bytes 1048592 | tf_op jit(solution)/shard_map/reduce_scatter | solution.py:355
  4728.3 360.4 %reduce-scatter.28.cloned.1.call-done = f32[64,4096]{1,0:T(8,128)} async-done(((f32[2048,4096]{1,0:T(8,128)}), f32[64,4096]{1,0:T(8,128)}) %reduce-scatter.28.cloned.1.call-update) | async-done | bytes 1048592 | tf_op jit(solution)/shard_map/reduce_scatter | solution.py:354
  5088.7 489.1 %reduce-scatter.36.cloned.1.call-done = f32[64,5632]{1,0:T(8,128)} async-done(((f32[2048,5632]{1,0:T(8,128)}), f32[64,5632]{1,0:T(8,128)}) %reduce-scatter.36.cloned.1.call-update) | async-done | bytes 1441808 | tf_op jit(solution)/shard_map/reduce_scatter | solution.py:367
  5577.8 491.4 %reduce-scatter.34.cloned.1.call-done = f32[64,5632]{1,0:T(8,128)} async-done(((f32[2048,5632]{1,0:T(8,128)}), f32[64,5632]{1,0:T(8,128)}) %reduce-scatter.34.cloned.1.call-update) | async-done | bytes 1441808 | tf_op jit(solution)/shard_map/reduce_scatter | solution.py:366
  (1971 shorter events, 2097.8 us)
Async XLA Ops:
  10.1 871.4 %all-gather.31.cloned.1.call-start = ((), (), s32[]{:S(2)}) async-start(), calls=%async_computation.17 | async-start | bytes 17301504 | tf_op jit(solution)/shard_map/all_gather | solution.py:203
  10.6 900.4 %all-gather.33.cloned.1.call-start = ((), (), s32[]{:S(2)}) async-start(), calls=%async_computation.18 | async-start | bytes 23789568 | tf_op jit(solution)/shard_map/all_gather | solution.py:207
  11.2 927.5 %all-gather.35.cloned.1.call-start = ((), (), s32[]{:S(2)}) async-start(), calls=%async_computation.19 | async-start | bytes 23789568 | tf_op jit(solution)/shard_map/all_gather | solution.py:208
  12.0 963.4 %all-gather.37.cloned.1.call-start = ((), (), s32[]{:S(2)}) async-start(), calls=%async_computation.20 | async-start | bytes 23789568 | tf_op jit(solution)/shard_map/all_gather | solution.py:209
  12.7 1134.4 %all-gather.39.cloned.1.call-start = ((), (), s32[]{:S(2)}) async-start(), calls=%async_computation.21 | async-start | bytes 23789568 | tf_op jit(solution)/shard_map/all_gather | solution.py:299
  1003.8 434.6 %all-gather.43.cloned.1.call-start = ((), (), s32[]{:S(2)}) async-start(), calls=%async_computation.23 | async-start | bytes 23789568 | tf_op jit(solution)/shard_map/all_gather | solution.py:298
  1004.5 549.6 %all-gather.45.cloned.1.call-start = ((), (), s32[]{:S(2)}) async-start(), calls=%async_computation.24 | async-start | bytes 17301504 | tf_op jit(solution)/shard_map/all_gather | solution.py:292
  1005.1 1778.3 %all-gather.49.cloned.1.call-start = ((), (), s32[]{:S(2)}) async-start(), calls=%async_computation.26 | async-start | bytes 8650752 | tf_op jit(solution)/shard_map/all_gather | solution.py:283
  1005.9 1788.2 %all-gather.47.cloned.1.call-start = ((), (), s32[]{:S(2)}) async-start(), calls=%async_computation.25 | async-start | bytes 8650752 | tf_op jit(solution)/shard_map/all_gather | solution.py:282
  1006.4 1798.2 %all-gather.51.cloned.1.call-start = ((), (), s32[]{:S(2)}) async-start(), calls=%async_computation.27 | async-start | bytes 17301504 | tf_op jit(solution)/shard_map/all_gather | solution.py:284
  1007.0 1812.8 %all-gather.53.cloned.1.call-start = ((), (), s32[]{:S(2)}) async-start(), calls=%async_computation.28 | async-start | bytes 17301504 | tf_op jit(solution)/shard_map/all_gather | solution.py:285
  1028.6 1856.8 %reduce-scatter.46.cloned.1.call-start = ((), (), s32[]{:S(2)}) async-start(), calls=%async_computation.40 | async-start | bytes 1081344
  2480.2 406.6 %reduce-scatter.44.cloned.1.call-start = ((), (), s32[]{:S(2)}) async-start(), calls=%async_computation.39 | async-start | bytes 1081344
  2481.7 406.5 %reduce-scatter.48.cloned.1.call-start = ((), (), s32[]{:S(2)}) async-start(), calls=%async_computation.41 | async-start | bytes 2162688
  2484.3 530.8 %reduce-scatter.40.cloned.1.call-start = ((), (), s32[]{:S(2)}) async-start(), calls=%async_computation.37 | async-start | bytes 1081344
  2552.5 596.0 %reduce-scatter.42.cloned.1.call-start = ((), (), s32[]{:S(2)}) async-start(), calls=%async_computation.38 | async-start | bytes 1081344
  2559.1 771.2 %reduce-scatter.24.cloned.1.call-start = ((), (), s32[]{:S(2)}) async-start(), calls=%async_computation.29 | async-start | bytes 17301504 | tf_op jit(solution)/shard_map/reduce_scatter | solution.py:352
  2569.1 948.8 %reduce-scatter.26.cloned.1.call-start = ((), (), s32[]{:S(2)}) async-start(), calls=%async_computation.30 | async-start | bytes 17301504 | tf_op jit(solution)/shard_map/reduce_scatter | solution.py:353
  2579.1 1425.7 %reduce-scatter.38.cloned.1.call-start = ((), (), s32[]{:S(2)}) async-start(), calls=%async_computation.36 | async-start | bytes 47579136 | tf_op jit(solution)/shard_map/reduce_scatter | solution.py:368
  2601.6 1766.4 %reduce-scatter.32.cloned.1.call-start = ((), (), s32[]{:S(2)}) async-start(), calls=%async_computation.33 | async-start | bytes 34603008 | tf_op jit(solution)/shard_map/reduce_scatter | solution.py:362
  2620.1 2108.1 %reduce-scatter.30.cloned.1.call-start = ((), (), s32[]{:S(2)}) async-start(), calls=%async_computation.32 | async-start | bytes 34603008 | tf_op jit(solution)/shard_map/reduce_scatter | solution.py:355
  2637.8 2450.9 %reduce-scatter.28.cloned.1.call-start = ((), (), s32[]{:S(2)}) async-start(), calls=%async_computation.31 | async-start | bytes 34603008 | tf_op jit(solution)/shard_map/reduce_scatter | solution.py:354
  2655.9 2921.9 %reduce-scatter.36.cloned.1.call-start = ((), (), s32[]{:S(2)}) async-start(), calls=%async_computation.35 | async-start | bytes 47579136 | tf_op jit(solution)/shard_map/reduce_scatter | solution.py:367
  2678.4 3390.8 %reduce-scatter.34.cloned.1.call-start = ((), (), s32[]{:S(2)}) async-start(), calls=%async_computation.34 | async-start | bytes 47579136 | tf_op jit(solution)/shard_map/reduce_scatter | solution.py:366
  (363 other events, 5577.3 us)
Sparse Core Ops, SparseCore 0:
  174.2 113.5 all-gather.26
  290.6 113.0 all-gather.28
  522.2 142.7 all-gather.32
  667.9 142.8 all-gather.34
  813.6 142.7 all-gather.36
  1003.3 143.7 all-gather.38
  1149.9 142.7 all-gather.40
  1295.6 142.7 all-gather.42
  1441.1 113.0 all-gather.44
  1714.5 113.5 all-gather.50
  1830.8 113.0 all-gather.52
  2480.3 133.1 reduce-scatter.45
  2615.8 130.8 reduce-scatter.43
  2749.0 132.8 reduce-scatter.47
  2884.0 130.9 reduce-scatter.39
  3017.3 131.0 reduce-scatter.41
  3151.4 178.8 reduce-scatter.23
  3333.3 184.5 reduce-scatter.25
  3520.8 483.9 reduce-scatter.37
  4007.8 360.2 reduce-scatter.31
  4370.9 357.3 reduce-scatter.29
  4731.1 357.5 reduce-scatter.27
  5091.7 486.0 reduce-scatter.35
  5580.8 488.4 reduce-scatter.33
  (5 shorter events, 422.1 us)
where the time goes:
time: 6090 us; the launch traced here: 6080 us
  waiting for transfers between devices  3750 us (62%)
  matrix products  1230 us (20%)
  local copies, waits for them, and re-layouts  378 us (6%)
  blocking collectives  349 us (6%)
  other arithmetic  324 us (5%)
    reduce_scatter x1, waiting for transfers between devices, on_device(): lax.psum_scatter(grad_ffgate, ('fsdp', 'rep'), scatter_dimension=0, tiled...  491 us
    reduce_scatter x1, waiting for transfers between devices, on_device(): lax.psum_scatter(grad_ffup, ('fsdp', 'rep'), scatter_dimension=0, tiled=T...  489 us
    reduce_scatter x1, waiting for transfers between devices, on_device(): lax.psum_scatter(grad_down, ('fsdp', 'rep'), scatter_dimension=1, tiled=T...  487 us
    reduce_scatter x1, waiting for transfers between devices, on_device(): lax.psum_scatter(grad_out, ('fsdp', 'rep'), scatter_dimension=1, tiled=True)  363 us
    reduce_scatter x1, waiting for transfers between devices, on_device(): lax.psum_scatter(proj_grads[2], ('fsdp', 'rep'), scatter_dimension=0, til...  360 us
    reduce_scatter x1, waiting for transfers between devices, on_device(): lax.psum_scatter(proj_grads[3], ('fsdp', 'rep'), scatter_dimension=0, til...  360 us
    unnamed x34, waiting for transfers between devices  266 us
    reduce_scatter x1, waiting for transfers between devices, on_device(): lax.psum_scatter(proj_grads[1], ('fsdp', 'rep'), scatter_dimension=0, til...  188 us
  transfers between devices with their start and end apart: 29, of which 16 were waited for; matrix products, arithmetic and copies ran while one was open for 31% of the time, Pallas kernels for 0%

commit v1 on v0

v1 whole, which is shorter than its diff:
```python
import functools

import jax
import jax.numpy as jnp
from jax import lax
from jax.experimental import pallas as pl
from jax.experimental.pallas import tpu as pltpu
from jax.sharding import PartitionSpec as P

SEQ = 256
SPLIT = 2
PAIR = 2
ROWS = PAIR * SEQ

f32 = jnp.float32
bf16 = jnp.bfloat16
NN = (((1,), (0,)), ((), ()))
NT = (((1,), (1,)), ((), ()))
TN = (((0,), (0,)), ((), ()))


def split(a):
    hi = a.astype(bf16)
    return hi, (a - hi.astype(f32)).astype(bf16)


def one(a, b, dims):
    return lax.dot_general(a.astype(bf16), b.astype(bf16), dims, preferred_element_type=f32)


def three(a, b, dims):
    ah, al = split(a)
    bh, bl = split(b)
    out = lax.dot_general(ah, bl, dims, preferred_element_type=f32)
    out = out + lax.dot_general(al, bh, dims, preferred_element_type=f32)
    return out + lax.dot_general(ah, bh, dims, preferred_element_type=f32)


def exact_left(a, b, dims):
    bh, bl = split(b)
    a = a.astype(bf16)
    return lax.dot_general(a, bh, dims, preferred_element_type=f32) + lax.dot_general(a, bl, dims, preferred_element_type=f32)


def exact_right(a, b, dims):
    ah, al = split(a)
    b = b.astype(bf16)
    return lax.dot_general(ah, b, dims, preferred_element_type=f32) + lax.dot_general(al, b, dims, preferred_element_type=f32)


def sigmoid(v):
    return 1.0 / (1.0 + jnp.exp(-v))


def conv(c, taps, pos):
    width = taps.shape[0]
    z = c * taps[width - 1 : width]
    for s in range(1, width):
        z = z + jnp.where(pos >= s, pltpu.roll(c, s, 0), 0.0) * taps[width - 1 - s : width - s]
    return z


def unit(c):
    r = lax.rsqrt(jnp.sum(c * c, axis=-1, keepdims=True) + 1e-6)
    return c * r, r


def inverses(n_list, iota_r, iota_c):
    size = n_list[0].shape[0]
    eye = (iota_r == iota_c).astype(f32)
    xs = None
    b = 1
    while b < size:
        mask = ((iota_r // (2 * b)) == (iota_c // (2 * b))) & ((iota_r // b) % 2 == 1) & ((iota_c // b) % 2 == 0)
        cs = [jnp.where(mask, n, 0.0) for n in n_list]
        if xs is None:
            xs = [eye - c for c in cs]
        else:
            low = [x.astype(bf16) for x in xs]
            t = [one(c, x, NN) for c, x in zip(cs, low)]
            xs = [x - one(y, z, NN) for x, y, z in zip(xs, low, t)]
        b *= 2
    left = [(eye - x) - three(n, x, NN) for n, x in zip(n_list, xs)]
    return [x + one(x, r, NN) for x, r in zip(xs, left)]


def rates(pba, prm, tri):
    beta = sigmoid(pba)
    rate = pba + prm[1:2]
    decay = -prm[0:1] * (jnp.maximum(rate, 0.0) + jnp.log1p(jnp.exp(-jnp.abs(rate))))
    return beta, rate, decay, exact_left(tri, decay, NN), exact_right(decay, tri, (((0,), (1,)), ((), ())))


class Sequence:
    def __init__(self, dims, half, refs, rows, iota_r, iota_c, tri):
        pq_ref, pk_ref, pv_ref, pg_ref, ba_ref, pos_ref, taps_ref, gain_ref, prm_ref = refs
        nh, dk, dv = dims
        hs = nh // SPLIT
        wq = hs * dk
        at = half * hs
        H = range(hs)
        self.rows = rows
        self.pos = pos_ref[rows, :]
        taps = taps_ref[...]
        self.taps = (taps[:, :wq], taps[:, wq : 2 * wq], taps[:, 2 * wq :])
        self.raw = (pq_ref[rows, :], pk_ref[rows, :], pv_ref[rows, :])
        self.beta, self.rate, self.decay, gcol, grow = rates(ba_ref[rows, :], prm_ref[...], tri)
        self.z = tuple(conv(c, t, self.pos) for c, t in zip(self.raw, self.taps))
        self.sig = tuple(sigmoid(z) for z in self.z)
        qc, kc, self.v = (z * g for z, g in zip(self.z, self.sig))
        live = (iota_c <= iota_r) & (iota_c >= iota_r - self.pos.astype(jnp.int32))
        self.bs = [self.beta[:, at + h : at + h + 1] for h in H]
        self.uq = [unit(qc[:, h * dk : (h + 1) * dk]) for h in H]
        self.uk = [unit(kc[:, h * dk : (h + 1) * dk]) for h in H]
        self.qs = [a * dk ** -0.5 for a, _ in self.uq]
        self.ks = [a for a, _ in self.uk]
        lane = nh + at
        self.ls = [
            jnp.where(live, jnp.exp(jnp.where(live, gcol[:, lane + h : lane + h + 1] - grow[lane + h : lane + h + 1, :], 0.0)), 0.0)
            for h in H]


def planes(n):
    iota_r = lax.broadcasted_iota(jnp.int32, (n, n), 0)
    iota_c = lax.broadcasted_iota(jnp.int32, (n, n), 1)
    return iota_r, iota_c, (iota_c <= iota_r).astype(f32), iota_c < iota_r


def fwd_kernel(dims, half, *refs):
    shared, (out_ref, x_ref, u_ref, o_ref) = refs[:9], refs[-4:]
    pg_ref, gain_ref = refs[3], refs[7]
    nh, dk, dv = dims
    hs = nh // SPLIT
    iota_r, iota_c, tri, strict = planes(SEQ)
    gain = gain_ref[...]
    seqs = [Sequence(dims, half, shared, slice(i * SEQ, (i + 1) * SEQ), iota_r, iota_c, tri) for i in range(out_ref.shape[0] // SEQ)]
    units = [(i, h) for i in range(len(seqs)) for h in range(hs)]
    ms = [three(seqs[i].ks[h], seqs[i].ks[h], NT) for i, h in units]
    ns = [jnp.where(strict, seqs[i].bs[h] * seqs[i].ls[h] * m, 0.0) for (i, h), m in zip(units, ms)]
    xs = inverses(ns, iota_r, iota_c)
    us = [three(x, seqs[i].bs[h] * seqs[i].v[:, h * dv : (h + 1) * dv], NN) for (i, h), x in zip(units, xs)]
    ps = [seqs[i].ls[h] * three(seqs[i].qs[h], seqs[i].ks[h], NT) for i, h in units]
    os = [three(p, u, NN) for p, u in zip(ps, us)]
    for (i, h), x, u, o in zip(units, xs, us, os):
        rows, sl = seqs[i].rows, slice(h * dv, (h + 1) * dv)
        x_ref[i * hs + h] = x
        u_ref[rows, sl] = u
        o_ref[rows, sl] = o
        r = lax.rsqrt(jnp.mean(o * o, axis=-1, keepdims=True) + 1e-5)
        pg = pg_ref[rows, sl]
        out_ref[rows, sl] = (o * r * gain * (pg * sigmoid(pg))).astype(bf16)


def bwd_kernel(dims, half, has_before, *refs):
    shared, (x_ref, u_ref, o_ref, dm_ref) = refs[:9], refs[9:13]
    dp_ref, dba_ref, dtaps_ref, dgain_ref, dprm_ref = refs[-5:]
    pg_ref, gain_ref, prm_ref = refs[3], refs[7], refs[8]
    nh, dk, dv = dims
    hs = nh // SPLIT
    wq, wv = hs * dk, hs * dv
    at = half * hs
    iota_r, iota_c, tri, strict = planes(SEQ)
    gain = gain_ref[...]
    prm = prm_ref[...]
    seqs = [Sequence(dims, half, shared, slice(i * SEQ, (i + 1) * SEQ), iota_r, iota_c, tri) for i in range(dm_ref.shape[0] // SEQ)]
    units = [(i, h) for i in range(len(seqs)) for h in range(hs)]
    dgain = jnp.zeros_like(gain)
    dos, us = [], []
    for i, h in units:
        rows, sl = seqs[i].rows, slice(h * dv, (h + 1) * dv)
        o = o_ref[rows, sl]
        pg = pg_ref[rows, sl]
        dm = dm_ref[rows, sl]
        r = lax.rsqrt(jnp.mean(o * o, axis=-1, keepdims=True) + 1e-5)
        nrm = o * r
        sg = sigmoid(pg)
        dp_ref[rows, 2 * wq + wv + h * dv : 2 * wq + wv + (h + 1) * dv] = (dm * nrm * gain * (sg * (1.0 + pg * (1.0 - sg)))).astype(bf16)
        dy = dm * (pg * sg)
        dgain = dgain + jnp.sum(dy * nrm, axis=0, keepdims=True)
        dn = dy * gain
        dos.append(r * (dn - nrm * jnp.mean(nrm * dn, axis=-1, keepdims=True)))
        us.append(u_ref[rows, sl])
    bm = [jnp.where(strict, seqs[i].ls[h] * three(seqs[i].ks[h], seqs[i].ks[h], NT), 0.0) for i, h in units]
    ps = [seqs[i].ls[h] * three(seqs[i].qs[h], seqs[i].ks[h], NT) for i, h in units]
    dps = [three(do, u, NT) for do, u in zip(dos, us)]
    dus = [three(p, do, TN) for p, do in zip(ps, dos)]
    dws = [three(x_ref[i * hs + h], du, TN) for (i, h), du in zip(units, dus)]
    das = [-three(dw, u, NT) for dw, u in zip(dws, us)]

    @pl.when(pl.program_id(0) == 0)
    def _():
        dtaps_ref[...] = jnp.zeros_like(dtaps_ref)
        dgain_ref[...] = jnp.zeros_like(dgain_ref)
        dprm_ref[...] = jnp.zeros_like(dprm_ref)

    dgain_ref[...] += dgain
    lane = lax.broadcasted_iota(jnp.int32, (SEQ, 128), 1)
    ones = jnp.ones((SEQ, 128), f32)
    sc = dk ** -0.5
    for i, q in enumerate(seqs):
        rows, pos = q.rows, q.pos
        dbeta = jnp.zeros((SEQ, 128), f32)
        dlog = jnp.zeros((SEQ, 128), f32)
        dz = ([], [], [])
        for h in range(hs):
            n = i * hs + h
            vh = q.v[:, h * dv : (h + 1) * dv]
            ab = das[n] * bm[n]
            dbeta = jnp.where(lane == at + h, jnp.sum(dws[n] * vh, axis=-1, keepdims=True) + jnp.sum(ab, axis=-1, keepdims=True), dbeta)
            e = q.bs[h] * ab + dps[n] * ps[n]
            dlog = jnp.where(lane == nh + at + h, jnp.sum(e, axis=-1, keepdims=True) - exact_right(e, ones, TN), dlog)
            ds = dps[n] * q.ls[h]
            dmm = jnp.where(strict, q.bs[h] * das[n] * q.ls[h], 0.0)
            dq = sc * three(ds, q.ks[h], NN)
            dkh = three(ds, q.qs[h], TN) + three(dmm, q.ks[h], NN) + three(dmm, q.ks[h], TN)
            qh, rq = q.uq[h]
            kh, rk = q.uk[h]
            dz[0].append(rq * (dq - qh * jnp.sum(qh * dq, axis=-1, keepdims=True)))
            dz[1].append(rk * (dkh - kh * jnp.sum(kh * dkh, axis=-1, keepdims=True)))
            dz[2].append(q.bs[h] * dws[n])
        ddecay = exact_left(tri, dlog, TN)
        drate = -prm[0:1] * ddecay * sigmoid(q.rate)
        dba = dbeta * q.beta * (1.0 - q.beta) + drate
        if has_before:
            dba = dba + refs[13][rows, :]
            dp_ref[rows, 2 * wq + 2 * wv :] = dba.astype(bf16)
        dba_ref[rows, :] = dba
        dprm_ref[0:1, :] += jnp.sum(ddecay * q.decay, axis=0, keepdims=True)
        dprm_ref[1:2, :] += jnp.sum(drate, axis=0, keepdims=True)
        to = 0
        for parts, z, sg, c, tap in zip(dz, q.z, q.sig, q.raw, q.taps):
            d = jnp.concatenate(parts, axis=1) * (sg * (1.0 + z * (1.0 - sg)))
            width = tap.shape[0]
            w = c.shape[1]
            dc = d * tap[width - 1 : width]
            dtaps_ref[width - 1 : width, to : to + w] += jnp.sum(d * c, axis=0, keepdims=True)
            for s in range(1, width):
                m = jnp.where(pos >= s, d, 0.0)
                dc = dc + pltpu.roll(m, SEQ - s, 0) * tap[width - 1 - s : width - s]
                dtaps_ref[width - 1 - s : width - s, to : to + w] += jnp.sum(m * pltpu.roll(c, s, 0), axis=0, keepdims=True)
            dp_ref[rows, to : to + w] = dc.astype(bf16)
            to += w


def shared_specs(dims):
    nh, dk, dv = dims
    wq, wv = nh // SPLIT * dk, nh // SPLIT * dv
    at = (2 * wq) // wv
    small = (2 * wq + 2 * wv) // 128
    return [
        pl.BlockSpec((ROWS, wq), lambda i: (i, 0)),
        pl.BlockSpec((ROWS, wq), lambda i: (i, 1)),
        pl.BlockSpec((ROWS, wv), lambda i: (i, at)),
        pl.BlockSpec((ROWS, wv), lambda i: (i, at + 1)),
        pl.BlockSpec((ROWS, 128), lambda i: (i, small)),
        pl.BlockSpec((ROWS, 1), lambda i: (i, 0)),
        pl.BlockSpec((4, 2 * wq + wv), lambda i: (0, 0)),
        pl.BlockSpec((1, dv), lambda i: (0, 0)),
        pl.BlockSpec((8, 128), lambda i: (0, 0)),
    ]


def cost(us):
    return pl.CostEstimate(flops=int(us * 1.1e9), bytes_accessed=int(us * 1e6), transcendentals=0)


def mixer_fwd(proj, first, pos, taps, gain, prm, dims, half, mixed=None):
    tok = pos.shape[0]
    nh, dk, dv = dims
    hs = nh // SPLIT
    ns = tok // SEQ
    wv = hs * dv
    row = pl.BlockSpec((ROWS, wv), lambda i: (i, 0))
    specs = shared_specs(dims)
    args = [proj, proj, proj, proj, first, pos, taps, gain, prm]
    alias = {}
    if mixed is not None:
        alias = {len(args): 0}
        args.append(mixed)
        specs.append(pl.BlockSpec(memory_space=pl.ANY))
    return pl.pallas_call(
        functools.partial(fwd_kernel, dims, half),
        grid=(ns // PAIR,),
        in_specs=specs,
        out_specs=[
            pl.BlockSpec((ROWS, wv), lambda i: (i, half)),
            pl.BlockSpec((PAIR * hs, SEQ, SEQ), lambda i: (i, 0, 0)),
            row,
            row,
        ],
        out_shape=[
            jax.ShapeDtypeStruct((tok, nh * dv), bf16),
            jax.ShapeDtypeStruct((ns * hs, SEQ, SEQ), f32),
            jax.ShapeDtypeStruct((tok, wv), f32),
            jax.ShapeDtypeStruct((tok, wv), f32),
        ],
        input_output_aliases=alias,
        cost_estimate=cost(45),
        compiler_params=pltpu.CompilerParams(vmem_limit_bytes=48 << 20),
    )(*args)


def mixer_bwd(proj, first, pos, taps, gain, prm, x, u, o, dm, dims, half, before=None):
    tok = pos.shape[0]
    nh, dk, dv = dims
    hs = nh // SPLIT
    ns = tok // SEQ
    wq, wv = hs * dk, hs * dv
    row = pl.BlockSpec((ROWS, wv), lambda i: (i, 0))
    lanes = pl.BlockSpec((ROWS, 128), lambda i: (i, 0))
    specs = shared_specs(dims) + [
        pl.BlockSpec((PAIR * hs, SEQ, SEQ), lambda i: (i, 0, 0)), row, row, pl.BlockSpec((ROWS, wv), lambda i: (i, half))]
    args = [proj, proj, proj, proj, first, pos, taps, gain, prm, x, u, o, dm]
    width = 2 * wq + 2 * wv
    if before is not None:
        args.append(before)
        specs.append(lanes)
        width += 128
    return pl.pallas_call(
        functools.partial(bwd_kernel, dims, half, before is not None),
        grid=(ns // PAIR,),
        in_specs=specs,
        out_specs=[
            pl.BlockSpec((ROWS, width), lambda i: (i, 0)),
            lanes,
            pl.BlockSpec((4, 2 * wq + wv), lambda i: (0, 0)),
            pl.BlockSpec((1, dv), lambda i: (0, 0)),
            pl.BlockSpec((8, 128), lambda i: (0, 0)),
        ],
        out_shape=[
            jax.ShapeDtypeStruct((tok, width), bf16),
            jax.ShapeDtypeStruct((tok, 128), f32),
            jax.ShapeDtypeStruct((4, 2 * wq + wv), f32),
            jax.ShapeDtypeStruct((1, dv), f32),
            jax.ShapeDtypeStruct((8, 128), f32),
        ],
        cost_estimate=cost(50),
        compiler_params=pltpu.CompilerParams(vmem_limit_bytes=56 << 20),
    )(*args)


def xor_send(value, axis, size, step):
    return lax.ppermute(value, axis, [(i, i ^ step) for i in range(size)])


def after(value, *needs):
    return lax.optimization_barrier((value, *needs))[0]


def lines(size):
    return [[low + 2 * i for i in range(size // 2)] for low in range(2)]


def gather_line(rows, size):
    return lax.all_gather(rows, "fsdp", axis=0, tiled=True, axis_index_groups=lines(size))


def gather_side(near, size):
    return jnp.concatenate([near, xor_send(near, "fsdp", size, 1)], axis=0)


def dot(left, right, dims=NN, out=f32):
    return lax.dot_general(left, right, dims, preferred_element_type=f32).astype(out)


class Summed:
    def __init__(self, left, right, size):
        self.size = size
        self.half = left.shape[1] // 2
        self.left, self.right = left, right
        self.sent = dot(left[:, self.half :], right, TN, bf16)
        self.got = xor_send(self.sent, "fsdp", size, 1)

    def side(self, *needs):
        keep = dot(self.left[:, : self.half], after(self.right, *needs) if needs else self.right, TN)
        self.low = (keep + self.got.astype(f32)).astype(bf16)
        self.sum = lax.psum_scatter(self.low, "fsdp", scatter_dimension=0, tiled=True, axis_index_groups=lines(self.size))

    def total(self, ranks):
        return lax.all_to_all(self.sum.reshape(ranks, -1, self.sum.shape[1]), "rep", 0, 0)


def join_tokens(rows, size):
    far = {0: rows}
    step = size // 2
    while step:
        for j in list(far):
            far[j ^ step] = xor_send(far[j], "rep", size, step)
        step //= 2
    return jnp.concatenate([far[j] for j in range(size)], axis=0)


def sum_tokens(product, size):
    half = size // 2
    held = {}
    for lo in range(size - half, -1, -half):
        part = product(lo, lo + half)
        for j, block in enumerate(jnp.split(part, half, axis=0)):
            held[lo + j] = block
        step = 1
        while step < half:
            for j in range(lo, lo + half, 2 * step):
                got = xor_send(held[j + step].astype(bf16), "rep", size, step)
                held[j] = held[j] + got.astype(f32)
            step *= 2
        if lo:
            held[lo] = xor_send(held[lo].astype(bf16), "rep", size, lo)
    return held[0] + held[half].astype(f32)


def rms(values):
    return lax.rsqrt(jnp.mean(values * values, axis=-1, keepdims=True) + 1e-06)


def norm_back(n, r, gain, dout):
    scaled = dout * gain
    return r * (scaled - n * jnp.mean(n * scaled, axis=-1, keepdims=True)), jnp.sum(dout * n, axis=0)


def make(F, R):
    both = ("fsdp", "rep")

    def on_device(tokens, segments, cotangent, gain_one, w_query, w_key, w_value, w_gate, w_beta, w_alpha, conv_q, conv_k,
                  conv_v, a_log, dt_bias, norm_gain, w_out, gain_two, w_ffgate, w_ffup, w_down):
        f = lax.axis_index("fsdp")
        r = lax.axis_index("rep")
        N = F * R
        rows_own, D = tokens.shape
        heads = a_log.shape[0]
        dk = w_query.shape[1] // heads
        dv = w_value.shape[1] // heads
        nh = heads // R
        dims = (nh, dk, dv)
        wq, wv = nh * dk, nh * dv
        hq, hv = wq // SPLIT, wv // SPLIT
        shard = D // N
        block = D // F
        ffq = w_ffgate.shape[1] // R
        tok = rows_own * R
        ns = tok // SEQ
        tiny = dv // N
        per = conv_v.shape[1] // shard

        low_bit = f & 1

        def swap(array, axis):
            half = array.shape[axis] // 2
            return jnp.concatenate(
                [lax.dynamic_slice_in_dim(array, (low_bit ^ j) * half, half, axis=axis) for j in range(2)], axis=axis)

        def mix(array, axis):
            at = [slice(None)] * array.ndim
            parts = []
            for bit in range(2):
                for i in range(F // 2):
                    at[axis] = slice((2 * i + bit) * block, (2 * i + bit + 1) * block)
                    parts.append(array[tuple(at)])
            return swap(jnp.concatenate(parts, axis=axis), axis)

        def unmix(array, axis):
            array = swap(array, axis)
            at = [slice(None)] * array.ndim
            parts = []
            for i in range(F // 2):
                for bit in range(2):
                    p = bit * (F // 2) + i
                    at[axis] = slice(p * block, (p + 1) * block)
                    parts.append(array[tuple(at)])
            return jnp.concatenate(parts, axis=axis)

        def quarter(arrays):
            return jnp.concatenate([a.reshape(shard, R, -1) for a in arrays], axis=2)

        def spread(packed):
            return lax.all_to_all(packed.transpose(1, 0, 2), "rep", 0, 0).reshape(R * shard, -1)

        extra = jnp.concatenate(
            [gain_one[:, None], gain_two[:, None], conv_q.T, conv_k.T,
             conv_v.reshape(4, shard, per).transpose(1, 0, 2).reshape(shard, 4 * per),
             jnp.pad(norm_gain, (0, shard - tiny))[:, None]], axis=1)
        n_extra = extra.shape[1]
        extra = jnp.broadcast_to(extra[:, None], (shard, R, n_extra))
        small = jnp.concatenate([w_beta.reshape(shard, R, nh), w_alpha.reshape(shard, R, nh), extra], axis=2)
        small = jnp.pad(small, ((0, 0), (0, 0), (0, 128 - small.shape[2])))

        def halves(array, width):
            parts = array.reshape(shard, R, SPLIT, width)
            return [parts[:, :, h] for h in range(SPLIT)]

        q_h, k_h, v_h, g_h = halves(w_query, hq), halves(w_key, hq), halves(w_value, hv), halves(w_gate, hv)
        own = mix(tokens, 1)
        part_a = spread(jnp.concatenate([q_h[0], k_h[0], v_h[0], g_h[0], small, q_h[1], k_h[1], v_h[1], g_h[1]], axis=2))
        w1 = 2 * hq + 2 * hv
        part_1, part_2 = part_a[:, : w1 + 128], part_a[:, w1 + 128 :]
        line_1 = gather_line(part_1, F)
        every = join_tokens(own, R)
        ids_all = join_tokens(segments[:, None], R).reshape(ns, SEQ)
        part_r = spread(quarter([after(w_out.T, part_a), w_ffgate, w_ffup, w_down.T]))
        part_b, part_g, part_u, part_d = (
            part_r[:, :wv], part_r[:, wv : wv + ffq], part_r[:, wv + ffq : wv + 2 * ffq], part_r[:, wv + 2 * ffq :])
        line_2 = gather_line(after(part_2, line_1), F)
        wa1 = gather_side(line_1, F)
        cot = mix(cotangent, 1)
        cot_all = join_tokens(after(cot, every), R)
        line_b = gather_line(after(part_b, line_2), F)
        line_g = gather_line(after(part_g, line_b), F)
        line_u = gather_line(after(part_u, line_g), F)
        line_d = gather_line(after(part_d, line_u), F)

        extra_all = wa1[:, w1 + 2 * nh : w1 + 2 * nh + n_extra]
        gain_first, gain_second = extra_all[:, 0].astype(f32)[None], extra_all[:, 1].astype(f32)[None]
        rest = unmix(extra_all[:, 2:], 0)
        cq = lax.dynamic_slice_in_dim(rest[:, 0:4], r * wq, wq, axis=0).astype(f32).T
        ck = lax.dynamic_slice_in_dim(rest[:, 4:8], r * wq, wq, axis=0).astype(f32).T
        cv = rest[:, 8 : 8 + 4 * per].reshape(D, 4, per).transpose(1, 0, 2).reshape(4, D * per)
        cv = lax.dynamic_slice_in_dim(cv, r * wv, wv, axis=1).astype(f32)
        gain_out = rest[:, 8 + 4 * per].reshape(N, shard)[:, :tiny].reshape(1, dv).astype(f32)
        taps = [jnp.concatenate([cq[:, h * hq : (h + 1) * hq], ck[:, h * hq : (h + 1) * hq], cv[:, h * hv : (h + 1) * hv]], axis=1)
                for h in range(SPLIT)]
        prm = jnp.stack([jnp.exp(lax.dynamic_slice_in_dim(a_log, r * nh, nh)), lax.dynamic_slice_in_dim(dt_bias, r * nh, nh)])
        prm = jnp.pad(prm, ((0, 6), (nh, 128 - 2 * nh)))
        place = jnp.arange(SEQ)
        same = (ids_all[:, :, None] == ids_all[:, None, :]) & (place[:, None] >= place[None, :])[None]
        pos = (jnp.sum(same.astype(f32), axis=2) - 1.0).reshape(tok, 1)

        every32 = every.astype(f32)
        normed_one = (every32 * rms(every32) * gain_first).astype(bf16)
        normed_one = after(normed_one, line_2)
        proj_1 = dot(normed_one, wa1)
        mixed, x_1, u_1, o_1 = mixer_fwd(proj_1, proj_1, pos, taps[0], gain_out, prm, dims, 0)
        wa2 = gather_side(line_2, F)
        proj_2 = dot(after(normed_one, mixed, line_b), wa2)
        mixed, x_2, u_2, o_2 = mixer_fwd(proj_2, proj_1, pos, taps[1], gain_out, prm, dims, 1, mixed)
        wb = gather_side(line_b, F)
        mixed = after(mixed, line_g)
        wg = gather_side(line_g, F)
        own32 = own.astype(f32)
        middle = own32 + sum_tokens(lambda lo, hi: dot(mixed[lo * rows_own : hi * rows_own], wb, NT), R)
        r2 = rms(middle)
        n2 = middle * r2
        normed_own = (n2 * gain_second).astype(bf16)
        normed_two = join_tokens(after(normed_own, line_u), R)
        wu = gather_side(line_u, F)
        gate_pre = dot(normed_two, wg)
        up_pre = dot(after(normed_two, gate_pre), wu)
        wd = gather_side(line_d, F)
        gate_sig = jax.nn.sigmoid(gate_pre)
        gate_act = gate_pre * gate_sig
        hidden = (gate_act * up_pre).astype(bf16)

        cot_wd = after(cot_all, hidden)
        g_down = Summed(cot_wd, hidden, F)
        dhidden = dot(after(cot_all, g_down.sent), wd)
        dgate = (dhidden * up_pre * (gate_sig * (1.0 + gate_pre * (1.0 - gate_sig)))).astype(bf16)
        dup = (dhidden * gate_act).astype(bf16)
        dnormed_two = sum_tokens(
            lambda lo, hi: dot(dgate[lo * rows_own : hi * rows_own], wg, NT) + dot(dup[lo * rows_own : hi * rows_own], wu, NT), R)
        g_gate = Summed(normed_two, dgate, F)
        g_down.side(g_gate.sent)
        g_up = Summed(normed_two, after(dup, g_gate.sent), F)
        dinner, dgain_second = norm_back(n2, r2, gain_second, dnormed_two)
        dmiddle = cot.astype(f32) + dinner
        dmiddle_low = join_tokens(dmiddle.astype(bf16), R)
        g_gate.side(g_up.sent)
        dmixed = dot(dmiddle_low, wb)
        before = None
        dprm, dgain_out, dtaps = 0.0, 0.0, {}
        dproj = {}
        dp_2, dba, dtaps[1], dg, dpar = mixer_bwd(proj_2, proj_1, pos, taps[1], gain_out, prm, x_2, u_2, o_2, dmixed, dims, 1)
        g_out = Summed(dmiddle_low, mixed, F)
        g_up.side(g_out.sent)
        g_2 = Summed(normed_one, dp_2, F)
        dp_1, dba, dtaps[0], dg1, dpar1 = mixer_bwd(
            proj_1, proj_1, pos, taps[0], gain_out, prm, x_1, u_1, o_1, after(dmixed, g_2.sent), dims, 0, dba)
        g_out.side()
        g_1 = Summed(normed_one, dp_1, F)
        g_2.side(g_1.sent)
        dnormed_one = sum_tokens(
            lambda lo, hi: dot(dp_1[lo * rows_own : hi * rows_own], wa1, NT) + dot(dp_2[lo * rows_own : hi * rows_own], wa2, NT), R)
        g_1.side()
        dprm = dpar + dpar1
        dgain_out = dg + dg1
        hidden_late = after(hidden, g_1.sent)
        layer_out = (middle + sum_tokens(lambda lo, hi: dot(hidden_late[lo * rows_own : hi * rows_own], wd, NT), R)).astype(bf16)

        n1 = own32 * rms(own32)
        dfirst, dgain_first = norm_back(n1, rms(own32), gain_first, dnormed_one)
        grad_tokens = unmix(dmiddle + dfirst, 1)

        def wide(parts):
            return parts.astype(f32).transpose(1, 0, 2).reshape(shard, -1)

        def tall(parts):
            return parts.astype(f32).transpose(0, 2, 1).reshape(-1, shard)

        t_1, t_2 = g_1.total(R), g_2.total(R)

        def joined(lo, width):
            return jnp.stack([t[:, :, lo : lo + width] for t in (t_1, t_2)], axis=2).astype(f32).transpose(1, 0, 2, 3).reshape(shard, -1)

        grad_query, grad_key = joined(0, hq), joined(hq, hq)
        grad_value, grad_gate_w = joined(2 * hq, hv), joined(2 * hq + hv, hv)
        grad_beta, grad_alpha = wide(t_1[:, :, w1 : w1 + nh]), wide(t_1[:, :, w1 + nh : w1 + 2 * nh])
        grad_down, grad_out = tall(g_down.total(R)), tall(g_out.total(R))
        grad_gate, grad_up = wide(g_gate.total(R)), wide(g_up.total(R))

        def placed(parts, total, width):
            part = jnp.concatenate(parts, axis=1)
            return lax.dynamic_update_slice(jnp.zeros((4, total), f32), part, (0, r * width))

        gq = placed([dtaps[h][:, :hq] for h in range(SPLIT)], R * wq, wq)
        gk = placed([dtaps[h][:, hq : 2 * hq] for h in range(SPLIT)], R * wq, wq)
        gv = placed([dtaps[h][:, 2 * hq :] for h in range(SPLIT)], R * wv, wv)
        heads_part = lax.dynamic_update_slice(jnp.zeros((2, heads), f32), dprm[:2, nh : 2 * nh], (0, r * nh)).reshape(1, -1)
        packed = jnp.concatenate([
            unmix(dgain_first[None], 1).reshape(N, -1),
            unmix(dgain_second[None], 1).reshape(N, -1),
            gq.reshape(4, N, -1).transpose(1, 0, 2).reshape(N, -1),
            gk.reshape(4, N, -1).transpose(1, 0, 2).reshape(N, -1),
            gv.reshape(4, N, -1).transpose(1, 0, 2).reshape(N, -1),
            dgain_out.reshape(N, tiny),
            jnp.broadcast_to(heads_part, (N, 2 * heads))], axis=1)
        summed = jnp.sum(lax.all_to_all(packed, both, 0, 0, tiled=True), axis=0)
        sizes = [shard, shard, 4 * shard, 4 * shard, 4 * shard * per, tiny, heads, heads]
        ends = [0]
        for size in sizes:
            ends.append(ends[-1] + size)
        pick = [summed[ends[i] : ends[i + 1]] for i in range(len(sizes))]
        return (
            unmix(layer_out, 1), grad_tokens, pick[0], grad_query, grad_key, grad_value, grad_gate_w, grad_beta, grad_alpha,
            pick[2].reshape(4, shard), pick[3].reshape(4, shard), pick[4].reshape(4, shard * per), pick[6], pick[7], pick[5],
            grad_out, pick[1], grad_gate, grad_up, grad_down)

    return on_device


def solution(mesh):
    rows, cols, flat = P(("fsdp", "rep"), None), P(None, ("fsdp", "rep")), P(("fsdp", "rep"))
    placed = (rows, flat, rows, flat, rows, rows, rows, rows, rows, rows, cols, cols, cols, P(), P(), flat, cols, flat, rows, rows, cols)
    made = (rows, rows, flat, rows, rows, rows, rows, rows, rows, cols, cols, cols, P(), P(), flat, cols, flat, rows, rows, cols)
    return jax.shard_map(
        make(mesh.shape["fsdp"], mesh.shape["rep"]), mesh=mesh, in_specs=placed, out_specs=made, check_vma=False)
```

time: 6090 us -> 1410 us (0.23)
  waiting for transfers between devices: 3750 us -> 509 us
  matrix products: 1230 us -> 376 us
  blocking collectives: 349 us -> 25 us
  other arithmetic: 324 us -> 84.1 us
  local copies, waits for them, and re-layouts: 378 us -> 163 us
  Pallas kernels: 0 us -> 168 us
    reduce_scatter x8 -> x6, waiting for transfers between devices: 2920 us -> 0.03 us  [side(): lax.psum_scatter(self.low, 'fsdp', scatter_dimension=0, tiled=True, axis_...]
    dot_general x566 -> x30, matrix products: 1230 us -> 376 us  [dot(): lax.dot_general(left, right, dims, preferred_element_type=f32).astype(out)]
    all_gather x16 -> x6, waiting for transfers between devices: 565 us -> 22.7 us  [gather_line(): lax.all_gather(rows, 'fsdp', axis=0, tiled=True, axis_index_groups=lines(...]
    ppermute x0 -> x39, waiting for transfers between devices: none -> 454 us  [xor_send(): return lax.ppermute(value, axis, [(i, i ^ step) for i in range(size)])]
    all_gather x7 -> x0, blocking collectives: 269 us -> none  [the longest x1 42.1 us: on_device(): lax.all_gather(mixer_shards[5], ('fsdp', 'rep'), axis=0, tiled=True)]
    unnamed x34 -> x12, waiting for transfers between devices: 266 us -> 0.2 us
    pallas_call x0 -> x4, Pallas kernels: none -> 168 us  [the longest x2 100 us: mixer_bwd(): pl.pallas_call(functools.partial(bwd_kernel, dims, half, before is not No...]
    unnamed x2 -> x0, blocking collectives: 79.9 us -> none
  transfers between devices with their start and end apart: 29 -> 59, of which waited for: 16 -> 21; matrix products, arithmetic and copies ran while one was open for 31% -> 40% of each run, Pallas kernels for 0% -> 12%
where the time goes in v1:
time: 1410 us; the launch traced here: 1400 us
  waiting for transfers between devices  509 us (36%)
  matrix products  376 us (27%)
  Pallas kernels  168 us (12%)
  local copies, waits for them, and re-layouts  163 us (12%)
  other arithmetic  84.1 us (6%)
  starting transfers between devices  60.8 us (4%)
  blocking collectives  25 us (2%)
  between operations  16.4 us (1%)
    ppermute x39, waiting for transfers between devices, xor_send(): return lax.ppermute(value, axis, [(i, i ^ step) for i in range(size)])  454 us
    dot_general x30, matrix products, dot(): lax.dot_general(left, right, dims, preferred_element_type=f32).astype(out)  376 us
    pallas_call x2, Pallas kernels, mixer_bwd(): pl.pallas_call(functools.partial(bwd_kernel, dims, half, before is not No...  100 us
    unnamed x262, local copies, waits for them, and re-layouts  80.8 us
    pallas_call x2, Pallas kernels, mixer_fwd(): pl.pallas_call(functools.partial(fwd_kernel, dims, half), grid=(ns // PAI...  68.2 us
    all_to_all x6, waiting for transfers between devices, total(): lax.all_to_all(self.sum.reshape(ranks, -1, self.sum.shape[1]), 'rep', 0, 0)  31.9 us
    ppermute x39, starting transfers between devices, xor_send(): return lax.ppermute(value, axis, [(i, i ^ step) for i in range(size)])  30.5 us
  transfers between devices with their start and end apart: 59, of which 21 were waited for; matrix products, arithmetic and copies ran while one was open for 40% of the time, Pallas kernels for 12%

profile of v1, /device:TPU:0, one launch (start us, length us, event | category | flops | bytes accessed | tf_op | source)
XLA Modules:
  0.0 1402.2 jit_solution(13000984498614090884)
XLA Ops:
  21.6 25.0 %all_to_all.49 = bf16[4,64,3200]{2,1,0:T(8,128)(2,1)S(1)} all-to-all(bf16[4,64,3200]{2,1,0:T(8,128)(2,1)} %bitcast.176), channel_id=1, replica_groups=mesh['fsdp'=8,'rep'=4] {'rep'}, dimensions={0} | all-to-all | bytes 3276800 | tf_op jit(solution)/shard_map/all_to_all | solution.py:475
  76.2 24.1 %collective-permute-done.1 = bf16[512,2048]{1,0:T(8,128)(2,1)} collective-permute-done((bf16[512,2048]{1,0:T(8,128)(2,1)}, bf16[512,2048]{1,0:T(8,128)(2,1)}, u32[]{:S(2)}, u32[]{:S(2)}) %collective-permute-start.1) | collective-permute-done | bytes 2097184 | tf_op jit(solution)/shard_map/ppermute | solution.py:343
  102.0 16.1 %all-gather.7.cloned.1.call-done = bf16[1024,1664]{0,1:T(8,128)(2,1)} async-done(((bf16[256,1664]{0,1:T(8,128)(2,1)}), bf16[1024,1664]{0,1:T(8,128)(2,1)}) %all-gather.7.cloned.1.call-update) | async-done | bytes 3407888 | tf_op jit(solution)/shard_map/all_gather | solution.py:355
  147.0 47.1 %collective-permute-done.3 = bf16[1024,1664]{0,1:T(8,128)(2,1)} collective-permute-done((bf16[1024,1664]{0,1:T(8,128)(2,1)}, bf16[1024,1664]{0,1:T(8,128)(2,1)}, u32[]{:S(2)}, u32[]{:S(2)}) %collective-permute-start.3) | collective-permute-done | bytes 3407904 | tf_op jit(solution)/shard_map/ppermute | solution.py:343
  212.0 21.3 %fusion.101.refs_0_.refs_1_.refs_2_.refs_3_.refs_4_ = f32[2048,1664]{1,0:T(8,128)} fusion(bf16[2048,2048]{1,0:T(8,128)(2,1)} %fusion.2, bf16[2048,1664]{0,1:T(8,128)(2,1)} %copy-done.39), kind=kOutput, calls=%fused_computation.279 | convolution fusion | flops 13958643712 | bytes 28835840 | tf_op jit(solution)/shard_map/dot_general | solution.py:363
  238.7 34.2 %shard_map.356 = (bf16[2048,1024]{1,0:T(8,128)(2,1)S(1)}, f32[16,256,256]{2,1,0:T(8,128)}, f32[2048,512]{1,0:T(8,128)}, f32[2048,512]{1,0:T(8,128)}) custom-call(f32[2048,1664]{1,0:T(8,128)} %fusion.101.refs_0_.refs_1_.refs_2_.refs_3_.refs_4_, f32[2048,1664]{1,0:T(8,128)} %fusion.101.refs_0_.refs_1_.refs_2_.refs_3_.refs_4_, ...), custom_call_target="tpu_custom_call" | custom-call | flops 49500000256 | bytes 45000000 | tf_op jit(solution)/shard_map/pallas_call | solution.py:281
  275.3 31.2 %collective-permute-done.7 = bf16[1024,1536]{1,0:T(8,128)(2,1)} collective-permute-done((bf16[1024,1536]{1,0:T(8,128)(2,1)}, bf16[1024,1536]{1,0:T(8,128)(2,1)}, u32[]{:S(2)}, u32[]{:S(2)}) %collective-permute-start.7) | collective-permute-done | bytes 3145760 | tf_op jit(solution)/shard_map/ppermute | solution.py:343
  310.3 19.4 %fusion.102.refs_0_.refs_1_.refs_2_.refs_3_ = f32[2048,1536]{1,0:T(8,128)} fusion(bf16[2048,2048]{1,0:T(8,128)(2,1)} %fusion.2, bf16[2048,1536]{1,0:T(8,128)(2,1)} %constant_dynamic-update-slice_fusion.15), kind=kOutput, calls=%fused_computation.280 | convolution fusion | flops 12884901888 | bytes 27262976 | tf_op jit(solution)/shard_map/dot_general | solution.py:363
  331.4 34.0 %shard_map.357 = (bf16[2048,1024]{1,0:T(8,128)(2,1)S(1)}, f32[16,256,256]{2,1,0:T(8,128)}, f32[2048,512]{1,0:T(8,128)}, f32[2048,512]{1,0:T(8,128)}) custom-call(f32[2048,1536]{1,0:T(8,128)} %fusion.102.refs_0_.refs_1_.refs_2_.refs_3_, f32[2048,1536]{1,0:T(8,128)} %fusion.102.refs_0_.refs_1_.refs_2_.refs_3_, ...), custom_call_target="tpu_custom_call", output_to_operand_aliasing={{0}: (9, {})} | custom-call | flops 49500000256 | bytes 45000000 | tf_op jit(solution)/shard_map/pallas_call | solution.py:281
  408.2 35.3 %collective-permute-done.18 = bf16[512,2048]{1,0:T(8,128)(2,1)} collective-permute-done((bf16[512,2048]{1,0:T(8,128)(2,1)}, bf16[512,2048]{1,0:T(8,128)(2,1)}, u32[]{:S(2)}, u32[]{:S(2)}) %collective-permute-start.18) | collective-permute-done | bytes 2097184 | tf_op jit(solution)/shard_map/ppermute | solution.py:343
  445.3 41.8 %collective-permute-done.11 = bf16[512,2048]{1,0:T(8,128)(2,1)S(1)} collective-permute-done((bf16[512,2048]{1,0:T(8,128)(2,1)S(1)}, bf16[512,2048]{1,0:T(8,128)(2,1)S(1)}, u32[]{:S(2)}, u32[]{:S(2)}) %collective-permute-start.11) | collective-permute-done | bytes 2097184 | tf_op jit(solution)/shard_map/ppermute | solution.py:343
  501.8 36.3 %collective-permute-done.13 = bf16[512,2048]{1,0:T(8,128)(2,1)} collective-permute-done((bf16[512,2048]{1,0:T(8,128)(2,1)S(1)}, bf16[512,2048]{1,0:T(8,128)(2,1)}, u32[]{:S(2)}, u32[]{:S(2)}) %collective-permute-start.13) | collective-permute-done | bytes 2097184 | tf_op jit(solution)/shard_map/ppermute | solution.py:343
  553.1 17.4 %collective-permute-done.16 = bf16[1024,1408]{1,0:T(8,128)(2,1)} collective-permute-done((bf16[1024,1408]{1,0:T(8,128)(2,1)}, bf16[1024,1408]{1,0:T(8,128)(2,1)}, u32[]{:S(2)}, u32[]{:S(2)}) %collective-permute-start.16) | collective-permute-done | bytes 2883616 | tf_op jit(solution)/shard_map/ppermute | solution.py:343
  579.2 17.4 %fusion.103 = f32[2048,1408]{1,0:T(8,128)} fusion(bf16[2048,2048]{1,0:T(8,128)(2,1)S(1)} %constant_dynamic-update-slice_fusion.19, bf16[2048,1408]{1,0:T(8,128)(2,1)} %constant_dynamic-update-slice_fusion.23), kind=kOutput, calls=%fused_computation.281 | convolution fusion | flops 11811160064 | bytes 25690112 | tf_op jit(solution)/shard_map/dot_general | solution.py:363
  604.7 21.7 %multiply_convert_fusion.2 = (bf16[2048,1408]{1,0:T(8,128)(2,1)S(1)}, f32[2048,1408]{1,0:T(8,128)}) fusion(f32[2048,1408]{1,0:T(8,128)} %fusion.103, bf16[2048,2048]{1,0:T(8,128)(2,1)} %copy-done.42, bf16[2048,1408]{1,0:T(8,128)(2,1)} %constant_dynamic-update-slice_fusion.25), kind=kOutput, calls=%fused_computation.7 | convolution fusion | flops 11828461568 | bytes 42991616 | tf_op jit(solution)/shard_map/dot_general | solution.py:363
  638.7 30.1 %collective-permute-done.20 = bf16[1024,1408]{1,0:T(8,128)(2,1)S(1)} collective-permute-done((bf16[1024,1408]{1,0:T(8,128)(2,1)}, bf16[1024,1408]{1,0:T(8,128)(2,1)S(1)}, u32[]{:S(2)}, u32[]{:S(2)}) %collective-permute-start.20) | collective-permute-done | bytes 2883616 | tf_op jit(solution)/shard_map/ppermute | solution.py:343
  671.7 28.4 %multiply_convert_fusion.1 = (bf16[2048,1408]{1,0:T(8,128)(2,1)}, bf16[2048,1408]{1,0:T(8,128)(2,1)}) fusion(f32[2048,1408]{1,0:T(8,128)} %fusion.103, f32[2048,1408]{1,0:T(8,128)} %get-tuple-element.159, bf16[2048,2048]{1,0:T(8,128)(2,1)} %copy-done.41, bf16[2048,1408]{1,0:T(8,128)(2,1)} %copy-done.40), kind=kOutput, calls=%fused_computation.6 | convolution fusion | flops 11848646656 | bytes 48758784 | tf_op jit(solution)/shard_map/dot_general | solution.py:363
  777.1 33.8 %collective-permute-done.23 = bf16[512,2048]{1,0:T(8,128)(2,1)} collective-permute-done((bf16[512,2048]{1,0:T(8,128)(2,1)}, bf16[512,2048]{1,0:T(8,128)(2,1)}, u32[]{:S(2)}, u32[]{:S(2)}) %collective-permute-start.23) | collective-permute-done | bytes 2097184 | tf_op jit(solution)/shard_map/ppermute | solution.py:343
  839.2 32.9 %collective-permute-done.25 = bf16[512,2048]{1,0:T(8,128)(2,1)S(1)} collective-permute-done((bf16[512,2048]{1,0:T(8,128)(2,1)}, bf16[512,2048]{1,0:T(8,128)(2,1)S(1)}, u32[]{:S(2)}, u32[]{:S(2)}) %collective-permute-start.25) | collective-permute-done | bytes 2097184 | tf_op jit(solution)/shard_map/ppermute | solution.py:343
  903.7 49.4 %shard_map.358 = (bf16[2048,1536]{1,0:T(8,128)(2,1)}, f32[2048,128]{1,0:T(8,128)}, f32[4,1024]{1,0:T(4,128)}, f32[1,256]{1,0:T(1,128)}, f32[8,128]{1,0:T(8,128)}) custom-call(f32[2048,1536]{1,0:T(8,128)} %fusion.102.refs_0_.refs_1_.refs_2_.refs_3_, f32[2048,1536]{1,0:T(8,128)} %fusion.102.refs_0_.refs_1_.refs_2_.refs_3_, ...), custom_call_target="tpu_custom_call" | custom-call | flops 54999998464 | bytes 50000000 | tf_op jit(solution)/shard_map/pallas_call | solution.py:319
  966.2 50.6 %shard_map.359 = (bf16[2048,1664]{1,0:T(8,128)(2,1)}, f32[2048,128]{1,0:T(8,128)}, f32[4,1024]{1,0:T(4,128)}, f32[1,256]{1,0:T(1,128)}, f32[8,128]{1,0:T(8,128)}) custom-call(f32[2048,1664]{1,0:T(8,128)} %fusion.101.refs_0_.refs_1_.refs_2_.refs_3_.refs_4_, f32[2048,1664]{1,0:T(8,128)} %fusion.101.refs_0_.refs_1_.refs_2_.refs_3_.refs_4_, ...), custom_call_target="tpu_custom_call" | custom-call | flops 54999998464 | bytes 50000000 | tf_op jit(solution)/shard_map/pallas_call | solution.py:319
  1102.6 51.1 %collective-permute-done.35 = bf16[1024,1024]{1,0:T(8,128)(2,1)} collective-permute-done((bf16[1024,1024]{1,0:T(8,128)(2,1)}, bf16[1024,1024]{1,0:T(8,128)(2,1)}, u32[]{:S(2)}, u32[]{:S(2)}) %collective-permute-start.35) | collective-permute-done | bytes 2097184 | tf_op jit(solution)/shard_map/ppermute | solution.py:343
  1232.6 30.3 %collective-permute-done.32 = bf16[512,2048]{1,0:T(8,128)(2,1)} collective-permute-done((bf16[512,2048]{1,0:T(8,128)(2,1)}, bf16[512,2048]{1,0:T(8,128)(2,1)}, u32[]{:S(2)}, u32[]{:S(2)}) %collective-permute-start.32) | collective-permute-done | bytes 2097184 | tf_op jit(solution)/shard_map/ppermute | solution.py:343
  1273.9 35.1 %collective-permute-done.29 = bf16[512,2048]{1,0:T(8,128)(2,1)} collective-permute-done((bf16[512,2048]{1,0:T(8,128)(2,1)}, bf16[512,2048]{1,0:T(8,128)(2,1)}, u32[]{:S(2)}, u32[]{:S(2)}) %collective-permute-start.29) | collective-permute-done | bytes 2097184 | tf_op jit(solution)/shard_map/ppermute | solution.py:343
  (578 shorter events, 621.7 us)
Async XLA Ops:
  7.2 110.9 %all-gather.7.cloned.1.call-start = ((), (), s32[]{:S(2)}) async-start(), calls=%async_computation.15 | async-start | bytes 4259840 | tf_op jit(solution)/shard_map/all_gather | solution.py:355
  51.8 81.0 %collective-permute-start = (bf16[512,2048]{1,0:T(8,128)(2,1)}, bf16[512,2048]{1,0:T(8,128)(2,1)}, u32[]{:S(2)}, u32[]{:S(2)}) collective-permute-start(bf16[512,2048]{1,0:T(8,128)(2,1)} %pad_maximum_fusion.2), channel_id=1, source_target_pairs={{0,1},{1,0},{2,3},{3,2},{4,5},{5,4},{6,7},{7,6},{8,9},{9,8},{10,11... | collective-permute-start | bytes 6291464 | tf_op jit(solution)/shard_map/ppermute | solution.py:343
  72.6 139.2 %all-gather.9.cloned.1.call-start = ((), (), s32[]{:S(2)}) async-start(), calls=%async_computation.16 | async-start | bytes 3932160 | tf_op jit(solution)/shard_map/all_gather | solution.py:355
  144.6 130.3 %all-gather.11.cloned.1.call-start = ((), (), s32[]{:S(2)}) async-start(), calls=%async_computation.17 | async-start | bytes 2621440 | tf_op jit(solution)/shard_map/all_gather | solution.py:355
  211.8 165.2 %all-gather.13.cloned.1.call-start = ((), (), s32[]{:S(2)}) async-start(), calls=%async_computation.18 | async-start | bytes 3604480 | tf_op jit(solution)/shard_map/all_gather | solution.py:355
  274.9 216.7 %all-gather.15.cloned.1.call-start = ((), (), s32[]{:S(2)}) async-start(), calls=%async_computation.19 | async-start | bytes 3604480 | tf_op jit(solution)/shard_map/all_gather | solution.py:355
  396.5 206.8 %all-gather.17.cloned.1.call-start = ((), (), s32[]{:S(2)}) async-start(), calls=%async_computation.20 | async-start | bytes 3604480 | tf_op jit(solution)/shard_map/all_gather | solution.py:355
  408.1 88.4 %collective-permute-start.17 = (bf16[512,2048]{1,0:T(8,128)(2,1)}, bf16[512,2048]{1,0:T(8,128)(2,1)}, u32[]{:S(2)}, u32[]{:S(2)}) collective-permute-start(bf16[512,2048]{1,0:T(8,128)(2,1)} %pad_maximum_fusion.3), channel_id=1, source_target_pairs={{0,1},{1,0},{2,3},{3,2},{4,5},{5,4},{6,7},{7,6},{8,9},{9,8},{10,11... | collective-permute-start | bytes 6291464 | tf_op jit(solution)/shard_map/ppermute | solution.py:343
  443.5 98.2 %collective-permute-start.15 = (bf16[1024,1408]{1,0:T(8,128)(2,1)}, bf16[1024,1408]{1,0:T(8,128)(2,1)}, u32[]{:S(2)}, u32[]{:S(2)}) collective-permute-start(bf16[1024,1408]{1,0:T(8,128)(2,1)} %all-gather.13.cloned.1.call-done), channel_id=1, source_target_pairs={{0,4},{4,0},{8,12},{12,8},{16,20},{20,16},{24,28},{28,24},{1,5},{5... | collective-permute-start | bytes 8650760 | tf_op jit(solution)/shard_map/ppermute | solution.py:343
  545.4 290.3 %reduce-scatter.17.cloned.1.call-start = ((), (), s32[]{:S(2)}) async-start(), calls=%async_computation.26 | async-start | bytes 3604480 | tf_op jit(solution)/shard_map/reduce_scatter | solution.py:377
  637.9 126.2 %collective-permute-start.38 = (bf16[1024,1408]{1,0:T(8,128)(2,1)}, bf16[1024,1408]{1,0:T(8,128)(2,1)}, u32[]{:S(2)}, u32[]{:S(2)}) collective-permute-start(bf16[1024,1408]{1,0:T(8,128)(2,1)} %fusion.31), channel_id=1, source_target_pairs={{0,4},{4,0},{8,12},{12,8},{16,20},{20,16},{24,28},{28,24},{1,5},{5... | collective-permute-start | bytes 8650760 | tf_op jit(solution)/shard_map/ppermute | solution.py:343
  775.5 96.6 %collective-permute-start.36 = (bf16[1024,1408]{1,0:T(8,128)(2,1)}, bf16[1024,1408]{1,0:T(8,128)(2,1)}, u32[]{:S(2)}, u32[]{:S(2)}) collective-permute-start(bf16[1024,1408]{1,0:T(8,128)(2,1)} %convolution_convert_fusion.1), channel_id=1, source_target_pairs={{0,4},{4,0},{8,12},{12,8},{16,20},{20,16},{24,28},{28,24},{1,5},{5... | collective-permute-start | bytes 8650760 | tf_op jit(solution)/shard_map/ppermute | solution.py:343
  834.2 228.5 %collective-permute-start.37 = (bf16[1024,1408]{1,0:T(8,128)(2,1)}, bf16[1024,1408]{1,0:T(8,128)(2,1)}, u32[]{:S(2)}, u32[]{:S(2)}) collective-permute-start(bf16[1024,1408]{1,0:T(8,128)(2,1)} %convolution_convert_fusion), channel_id=1, source_target_pairs={{0,4},{4,0},{8,12},{12,8},{16,20},{20,16},{24,28},{28,24},{1,5},{5... | collective-permute-start | bytes 8650760 | tf_op jit(solution)/shard_map/ppermute | solution.py:343
  839.2 333.4 %reduce-scatter.13.cloned.1.call-start = ((), (), s32[]{:S(2)}) async-start(), calls=%async_computation.24 | async-start | bytes 3604480 | tf_op jit(solution)/shard_map/reduce_scatter | solution.py:377
  883.9 443.1 %reduce-scatter.15.cloned.1.call-start = ((), (), s32[]{:S(2)}) async-start(), calls=%async_computation.25 | async-start | bytes 3604480 | tf_op jit(solution)/shard_map/reduce_scatter | solution.py:377
  964.7 211.5 %collective-permute-start.34 = (bf16[1024,1536]{1,0:T(8,128)(2,1)}, bf16[1024,1536]{1,0:T(8,128)(2,1)}, u32[]{:S(2)}, u32[]{:S(2)}) collective-permute-start(bf16[1024,1536]{1,0:T(8,128)(2,1)} %convolution_convert_fusion.2), channel_id=1, source_target_pairs={{0,4},{4,0},{8,12},{12,8},{16,20},{20,16},{24,28},{28,24},{1,5},{5... | collective-permute-start | bytes 9437192 | tf_op jit(solution)/shard_map/ppermute | solution.py:343
  1029.9 191.4 %collective-permute-start.33 = (bf16[1024,1664]{1,0:T(8,128)(2,1)}, bf16[1024,1664]{1,0:T(8,128)(2,1)}, u32[]{:S(2)}, u32[]{:S(2)}) collective-permute-start(bf16[1024,1664]{1,0:T(8,128)(2,1)} %convolution_convert_fusion.3), channel_id=1, source_target_pairs={{0,4},{4,0},{8,12},{12,8},{16,20},{20,16},{24,28},{28,24},{1,5},{5... | collective-permute-start | bytes 10223624 | tf_op jit(solution)/shard_map/ppermute | solution.py:343
  1045.1 108.5 %collective-permute-start.35 = (bf16[1024,1024]{1,0:T(8,128)(2,1)}, bf16[1024,1024]{1,0:T(8,128)(2,1)}, u32[]{:S(2)}, u32[]{:S(2)}) collective-permute-start(bf16[1024,1024]{1,0:T(8,128)(2,1)} %fusion.72), channel_id=1, source_target_pairs={{0,4},{4,0},{8,12},{12,8},{16,20},{20,16},{24,28},{28,24},{1,5},{5... | collective-permute-start | bytes 6291464 | tf_op jit(solution)/shard_map/ppermute | solution.py:343
  1047.3 168.4 %collective-permute-start.28 = (bf16[512,2048]{1,0:T(8,128)(2,1)S(1)}, bf16[512,2048]{1,0:T(8,128)(2,1)}, u32[]{:S(2)}, u32[]{:S(2)}) collective-permute-start(bf16[512,2048]{1,0:T(8,128)(2,1)S(1)} %split.140), channel_id=1, source_target_pairs={{0,1},{1,0},{2,3},{3,2},{4,5},{5,4},{6,7},{7,6},{8,9},{9,8},{10,11... | collective-permute-start | bytes 6291464 | tf_op jit(solution)/shard_map/ppermute | solution.py:343
  1062.7 211.2 %collective-permute-start.27 = (bf16[512,2048]{1,0:T(8,128)(2,1)}, bf16[512,2048]{1,0:T(8,128)(2,1)}, u32[]{:S(2)}, u32[]{:S(2)}) collective-permute-start(bf16[512,2048]{1,0:T(8,128)(2,1)} %split.141), channel_id=1, source_target_pairs={{0,1},{1,0},{2,3},{3,2},{4,5},{5,4},{6,7},{7,6},{8,9},{9,8},{10,11... | collective-permute-start | bytes 6291464 | tf_op jit(solution)/shard_map/ppermute | solution.py:343
  1073.3 262.7 %reduce-scatter.11.cloned.1.call-start = ((), (), s32[]{:S(2)}) async-start(), calls=%async_computation.23 | async-start | bytes 2621440 | tf_op jit(solution)/shard_map/reduce_scatter | solution.py:377
  1176.2 177.5 %reduce-scatter.9.cloned.1.call-start = ((), (), s32[]{:S(2)}) async-start(), calls=%async_computation.22 | async-start | bytes 3932160 | tf_op jit(solution)/shard_map/reduce_scatter | solution.py:377
  1188.3 180.5 %reduce-scatter.7.cloned.1.call-start = ((), (), s32[]{:S(2)}) async-start(), calls=%async_computation.21 | async-start | bytes 4259840 | tf_op jit(solution)/shard_map/reduce_scatter | solution.py:377
  1220.6 88.4 %collective-permute-start.29 = (bf16[512,2048]{1,0:T(8,128)(2,1)}, bf16[512,2048]{1,0:T(8,128)(2,1)}, u32[]{:S(2)}, u32[]{:S(2)}) collective-permute-start(bf16[512,2048]{1,0:T(8,128)(2,1)} %fusion.19), channel_id=1, source_target_pairs={{0,2},{1,3},{2,0},{3,1},{4,6},{5,7},{6,4},{7,5},{8,10},{9,11},{10,... | collective-permute-start | bytes 6291464 | tf_op jit(solution)/shard_map/ppermute | solution.py:343
  (129 other events, 4270.0 us)
Sparse Core Ops, SparseCore 0:
  49.3 68.7 all-gather.6
  144.7 64.4 all-gather.8
  211.9 44.1 all-gather.10
  275.0 56.4 all-gather.12
  396.6 56.4 all-gather.14
  545.5 57.7 all-gather.16
  775.6 53.9 reduce-scatter.16
  884.0 55.0 reduce-scatter.12
  1073.4 54.0 reduce-scatter.14
  1160.9 42.5 reduce-scatter.10
  1205.9 59.6 reduce-scatter.8
  1267.8 66.9 reduce-scatter.6

commit v2 on v1

--- a/solution.py
+++ b/solution.py
@@ -242,18 +242,18 @@
             to += w
 
 
-def shared_specs(dims):
+def shared_specs(dims, off=0):
     nh, dk, dv = dims
     wq, wv = nh // SPLIT * dk, nh // SPLIT * dv
     at = (2 * wq) // wv
     small = (2 * wq + 2 * wv) // 128
     return [
-        pl.BlockSpec((ROWS, wq), lambda i: (i, 0)),
-        pl.BlockSpec((ROWS, wq), lambda i: (i, 1)),
-        pl.BlockSpec((ROWS, wv), lambda i: (i, at)),
-        pl.BlockSpec((ROWS, wv), lambda i: (i, at + 1)),
-        pl.BlockSpec((ROWS, 128), lambda i: (i, small)),
-        pl.BlockSpec((ROWS, 1), lambda i: (i, 0)),
+        pl.BlockSpec((ROWS, wq), lambda i: (i + off, 0)),
+        pl.BlockSpec((ROWS, wq), lambda i: (i + off, 1)),
+        pl.BlockSpec((ROWS, wv), lambda i: (i + off, at)),
+        pl.BlockSpec((ROWS, wv), lambda i: (i + off, at + 1)),
+        pl.BlockSpec((ROWS, 128), lambda i: (i + off, small)),
+        pl.BlockSpec((ROWS, 1), lambda i: (i + off, 0)),
         pl.BlockSpec((4, 2 * wq + wv), lambda i: (0, 0)),
         pl.BlockSpec((1, dv), lambda i: (0, 0)),
         pl.BlockSpec((8, 128), lambda i: (0, 0)),
@@ -295,33 +295,40 @@
             jax.ShapeDtypeStruct((tok, wv), f32),
         ],
         input_output_aliases=alias,
-        cost_estimate=cost(45),
+        cost_estimate=cost(4),
         compiler_params=pltpu.CompilerParams(vmem_limit_bytes=48 << 20),
     )(*args)
 
 
-def mixer_bwd(proj, first, pos, taps, gain, prm, x, u, o, dm, dims, half, before=None):
+def mixer_bwd(proj, first, pos, taps, gain, prm, x, u, o, dm, dims, half, part, before=None, filled=None):
     tok = pos.shape[0]
     nh, dk, dv = dims
     hs = nh // SPLIT
     ns = tok // SEQ
     wq, wv = hs * dk, hs * dv
-    row = pl.BlockSpec((ROWS, wv), lambda i: (i, 0))
-    lanes = pl.BlockSpec((ROWS, 128), lambda i: (i, 0))
-    specs = shared_specs(dims) + [
-        pl.BlockSpec((PAIR * hs, SEQ, SEQ), lambda i: (i, 0, 0)), row, row, pl.BlockSpec((ROWS, wv), lambda i: (i, half))]
+    steps = dm.shape[0] // ROWS
+    off = part * steps
+    row = pl.BlockSpec((ROWS, wv), lambda i: (i + off, 0))
+    lanes = pl.BlockSpec((ROWS, 128), lambda i: (i + off, 0))
+    specs = shared_specs(dims, off) + [
+        pl.BlockSpec((PAIR * hs, SEQ, SEQ), lambda i: (i + off, 0, 0)), row, row, pl.BlockSpec((ROWS, wv), lambda i: (i, half))]
     args = [proj, proj, proj, proj, first, pos, taps, gain, prm, x, u, o, dm]
     width = 2 * wq + 2 * wv
     if before is not None:
         args.append(before)
         specs.append(lanes)
         width += 128
+    alias = {}
+    if filled is not None:
+        alias = {len(args): 0, len(args) + 1: 1}
+        args += filled
+        specs += [pl.BlockSpec(memory_space=pl.ANY)] * 2
     return pl.pallas_call(
         functools.partial(bwd_kernel, dims, half, before is not None),
-        grid=(ns // PAIR,),
+        grid=(steps,),
         in_specs=specs,
         out_specs=[
-            pl.BlockSpec((ROWS, width), lambda i: (i, 0)),
+            pl.BlockSpec((ROWS, width), lambda i: (i + off, 0)),
             lanes,
             pl.BlockSpec((4, 2 * wq + wv), lambda i: (0, 0)),
             pl.BlockSpec((1, dv), lambda i: (0, 0)),
@@ -334,7 +341,8 @@
             jax.ShapeDtypeStruct((1, dv), f32),
             jax.ShapeDtypeStruct((8, 128), f32),
         ],
-        cost_estimate=cost(50),
+        input_output_aliases=alias,
+        cost_estimate=cost(26),
         compiler_params=pltpu.CompilerParams(vmem_limit_bytes=56 << 20),
     )(*args)
 
@@ -355,8 +363,9 @@
     return lax.all_gather(rows, "fsdp", axis=0, tiled=True, axis_index_groups=lines(size))
 
 
-def gather_side(near, size):
-    return jnp.concatenate([near, xor_send(near, "fsdp", size, 1)], axis=0)
+def gather_side(near, size, *needs):
+    got = xor_send(after(near, *needs) if needs else near, "fsdp", size, 1)
+    return jnp.concatenate([near, got], axis=0), got
 
 
 def dot(left, right, dims=NN, out=f32):
@@ -364,12 +373,12 @@
 
 
 class Summed:
-    def __init__(self, left, right, size):
+    def __init__(self, left, right, size, *needs):
         self.size = size
         self.half = left.shape[1] // 2
         self.left, self.right = left, right
         self.sent = dot(left[:, self.half :], right, TN, bf16)
-        self.got = xor_send(self.sent, "fsdp", size, 1)
+        self.got = xor_send(after(self.sent, *needs) if needs else self.sent, "fsdp", size, 1)
 
     def side(self, *needs):
         keep = dot(self.left[:, : self.half], after(self.right, *needs) if needs else self.right, TN)
@@ -381,31 +390,39 @@
 
 
 def join_tokens(rows, size):
-    far = {0: rows}
-    step = size // 2
-    while step:
-        for j in list(far):
-            far[j ^ step] = xor_send(far[j], "rep", size, step)
-        step //= 2
-    return jnp.concatenate([far[j] for j in range(size)], axis=0)
-
-
-def sum_tokens(product, size):
     half = size // 2
-    held = {}
-    for lo in range(size - half, -1, -half):
-        part = product(lo, lo + half)
-        for j, block in enumerate(jnp.split(part, half, axis=0)):
-            held[lo + j] = block
+
+    def around(block):
+        held = {0: block}
+        step = half // 2
+        while step:
+            for j in list(held):
+                held[j ^ step] = xor_send(held[j], "rep", size, step)
+            step //= 2
+        return jnp.concatenate([held[j] for j in range(half)], axis=0)
+
+    beyond = xor_send(rows, "rep", size, half)
+    return around(rows), around(beyond)
+
+
+def sum_tokens(far, near, size, *needs):
+    half = size // 2
+
+    def around(part):
+        held = jnp.split(part, half, axis=0)
         step = 1
         while step < half:
-            for j in range(lo, lo + half, 2 * step):
-                got = xor_send(held[j + step].astype(bf16), "rep", size, step)
-                held[j] = held[j] + got.astype(f32)
+            for j in range(0, half, 2 * step):
+                held[j] = held[j] + xor_send(held[j + step].astype(bf16), "rep", size, step).astype(f32)
             step *= 2
-        if lo:
-            held[lo] = xor_send(held[lo].astype(bf16), "rep", size, lo)
-    return held[0] + held[half].astype(f32)
+        return held[0]
+
+    beyond = around(far()).astype(bf16)
+    part = near(beyond)
+    if needs:
+        beyond = after(beyond, *needs)
+    got = xor_send(beyond, "rep", size, half)
+    return around(part) + got.astype(f32), got
 
 
 def rms(values):
@@ -477,11 +494,9 @@
         extra = jnp.concatenate(
             [gain_one[:, None], gain_two[:, None], conv_q.T, conv_k.T,
              conv_v.reshape(4, shard, per).transpose(1, 0, 2).reshape(shard, 4 * per),
-             jnp.pad(norm_gain, (0, shard - tiny))[:, None]], axis=1)
-        n_extra = extra.shape[1]
-        extra = jnp.broadcast_to(extra[:, None], (shard, R, n_extra))
-        small = jnp.concatenate([w_beta.reshape(shard, R, nh), w_alpha.reshape(shard, R, nh), extra], axis=2)
-        small = jnp.pad(small, ((0, 0), (0, 0), (0, 128 - small.shape[2])))
+             jnp.pad(norm_gain, (0, shard - tiny))[:, None]], axis=1).T
+        small = jnp.concatenate([w_beta.reshape(shard, R, nh), w_alpha.reshape(shard, R, nh)], axis=2)
+        small = jnp.pad(small, ((0, 0), (0, 0), (0, 128 - 2 * nh)))
 
         def halves(array, width):
             parts = array.reshape(shard, R, SPLIT, width)
@@ -492,29 +507,30 @@
         part_a = spread(jnp.concatenate([q_h[0], k_h[0], v_h[0], g_h[0], small, q_h[1], k_h[1], v_h[1], g_h[1]], axis=2))
         w1 = 2 * hq + 2 * hv
         part_1, part_2 = part_a[:, : w1 + 128], part_a[:, w1 + 128 :]
+        extra_all = lax.all_to_all(jnp.broadcast_to(after(extra, part_a)[None], (N, *extra.shape)), both, 0, 0)
+        extra_all = extra_all.transpose(1, 0, 2).reshape(-1, D).astype(f32)
         line_1 = gather_line(part_1, F)
-        every = join_tokens(own, R)
-        ids_all = join_tokens(segments[:, None], R).reshape(ns, SEQ)
-        part_r = spread(quarter([after(w_out.T, part_a), w_ffgate, w_ffup, w_down.T]))
+        every = jnp.concatenate(join_tokens(own, R), axis=0)
+        ids_all = jnp.concatenate(join_tokens(segments[:, None], R), axis=0).reshape(ns, SEQ)
+        part_r = spread(quarter([after(w_out.T, extra_all), w_ffgate, w_ffup, w_down.T]))
         part_b, part_g, part_u, part_d = (
             part_r[:, :wv], part_r[:, wv : wv + ffq], part_r[:, wv + ffq : wv + 2 * ffq], part_r[:, wv + 2 * ffq :])
-        line_2 = gather_line(after(part_2, line_1), F)
-        wa1 = gather_side(line_1, F)
+        line_2 = gather_line(after(part_2, extra_all), F)
+        wa1, side_1 = gather_side(line_1, F)
         cot = mix(cotangent, 1)
-        cot_all = join_tokens(after(cot, every), R)
-        line_b = gather_line(after(part_b, line_2), F)
-        line_g = gather_line(after(part_g, line_b), F)
-        line_u = gather_line(after(part_u, line_g), F)
-        line_d = gather_line(after(part_d, line_u), F)
-
-        extra_all = wa1[:, w1 + 2 * nh : w1 + 2 * nh + n_extra]
-        gain_first, gain_second = extra_all[:, 0].astype(f32)[None], extra_all[:, 1].astype(f32)[None]
-        rest = unmix(extra_all[:, 2:], 0)
-        cq = lax.dynamic_slice_in_dim(rest[:, 0:4], r * wq, wq, axis=0).astype(f32).T
-        ck = lax.dynamic_slice_in_dim(rest[:, 4:8], r * wq, wq, axis=0).astype(f32).T
-        cv = rest[:, 8 : 8 + 4 * per].reshape(D, 4, per).transpose(1, 0, 2).reshape(4, D * per)
-        cv = lax.dynamic_slice_in_dim(cv, r * wv, wv, axis=1).astype(f32)
-        gain_out = rest[:, 8 + 4 * per].reshape(N, shard)[:, :tiny].reshape(1, dv).astype(f32)
+        cot_near, cot_far = join_tokens(after(cot, every), R)
+        line_b = gather_line(part_b, F)
+        line_g = gather_line(part_g, F)
+        line_u = gather_line(part_u, F)
+        line_d = gather_line(part_d, F)
+
+        gains = mix(extra_all[:2], 1)
+        gain_first, gain_second = gains[0:1], gains[1:2]
+        cq = lax.dynamic_slice_in_dim(extra_all[2:6], r * wq, wq, axis=1)
+        ck = lax.dynamic_slice_in_dim(extra_all[6:10], r * wq, wq, axis=1)
+        cv = extra_all[10 : 10 + 4 * per].reshape(4, per, D).transpose(0, 2, 1).reshape(4, D * per)
+        cv = lax.dynamic_slice_in_dim(cv, r * wv, wv, axis=1)
+        gain_out = extra_all[10 + 4 * per].reshape(N, shard)[:, :tiny].reshape(1, dv)
         taps = [jnp.concatenate([cq[:, h * hq : (h + 1) * hq], ck[:, h * hq : (h + 1) * hq], cv[:, h * hv : (h + 1) * hv]], axis=1)
                 for h in range(SPLIT)]
         prm = jnp.stack([jnp.exp(lax.dynamic_slice_in_dim(a_log, r * nh, nh)), lax.dynamic_slice_in_dim(dt_bias, r * nh, nh)])
@@ -525,63 +541,91 @@
 
         every32 = every.astype(f32)
         normed_one = (every32 * rms(every32) * gain_first).astype(bf16)
-        normed_one = after(normed_one, line_2)
-        proj_1 = dot(normed_one, wa1)
+        proj_1 = dot(after(normed_one, line_2, cot_near, cot_far, part_r, pos), wa1)
         mixed, x_1, u_1, o_1 = mixer_fwd(proj_1, proj_1, pos, taps[0], gain_out, prm, dims, 0)
-        wa2 = gather_side(line_2, F)
+        wa2, side_2 = gather_side(line_2, F, side_1)
         proj_2 = dot(after(normed_one, mixed, line_b), wa2)
         mixed, x_2, u_2, o_2 = mixer_fwd(proj_2, proj_1, pos, taps[1], gain_out, prm, dims, 1, mixed)
-        wb = gather_side(line_b, F)
+        wb, side_b = gather_side(line_b, F, side_2)
         mixed = after(mixed, line_g)
-        wg = gather_side(line_g, F)
+        wg, side_g = gather_side(line_g, F, side_b)
         own32 = own.astype(f32)
-        middle = own32 + sum_tokens(lambda lo, hi: dot(mixed[lo * rows_own : hi * rows_own], wb, NT), R)
+        mid = tok // 2
+        added, unused = sum_tokens(lambda: dot(mixed[mid:], wb, NT), lambda part: dot(after(mixed, part)[:mid], wb, NT), R)
+        middle = own32 + added
         r2 = rms(middle)
         n2 = middle * r2
         normed_own = (n2 * gain_second).astype(bf16)
-        normed_two = join_tokens(after(normed_own, line_u), R)
-        wu = gather_side(line_u, F)
-        gate_pre = dot(normed_two, wg)
-        up_pre = dot(after(normed_two, gate_pre), wu)
-        wd = gather_side(line_d, F)
-        gate_sig = jax.nn.sigmoid(gate_pre)
-        gate_act = gate_pre * gate_sig
-        hidden = (gate_act * up_pre).astype(bf16)
-
-        cot_wd = after(cot_all, hidden)
-        g_down = Summed(cot_wd, hidden, F)
-        dhidden = dot(after(cot_all, g_down.sent), wd)
-        dgate = (dhidden * up_pre * (gate_sig * (1.0 + gate_pre * (1.0 - gate_sig)))).astype(bf16)
-        dup = (dhidden * gate_act).astype(bf16)
-        dnormed_two = sum_tokens(
-            lambda lo, hi: dot(dgate[lo * rows_own : hi * rows_own], wg, NT) + dot(dup[lo * rows_own : hi * rows_own], wu, NT), R)
-        g_gate = Summed(normed_two, dgate, F)
-        g_down.side(g_gate.sent)
-        g_up = Summed(normed_two, after(dup, g_gate.sent), F)
-        dinner, dgain_second = norm_back(n2, r2, gain_second, dnormed_two)
+        wu, side_u = gather_side(line_u, F, side_g)
+        two = join_tokens(after(normed_own, line_u), R)
+        wd, side_d = gather_side(line_d, F, side_u)
+        gates, ups, acts, sigs, hiddens = [], [], [], [], []
+        for normed in two:
+            gates.append(dot(normed, wg))
+            ups.append(dot(normed, wu))
+            sigs.append(jax.nn.sigmoid(gates[-1]))
+            acts.append(gates[-1] * sigs[-1])
+            hiddens.append((acts[-1] * ups[-1]).astype(bf16))
+        hidden = jnp.concatenate(hiddens, axis=0)
+        normed_two = jnp.concatenate(two, axis=0)
+        cot_all = jnp.concatenate([cot_near, cot_far], axis=0)
+
+        kept = {}
+
+        def keep(name, value):
+            kept[name] = value
+            return value
+
+        g_down = Summed(cot_all, hidden, F)
+        dgates, dups = [None, None], [None, None]
+
+        def back_two(t, *needs):
+            dhidden = dot(after((cot_near, cot_far)[t], *needs), wd)
+            dgates[t] = (dhidden * ups[t] * (sigs[t] * (1.0 + gates[t] * (1.0 - sigs[t])))).astype(bf16)
+            dups[t] = (dhidden * acts[t]).astype(bf16)
+            return dot(dgates[t], wg, NT) + dot(dups[t], wu, NT)
+
+        dnormed_two, far_two = sum_tokens(lambda: back_two(1, g_down.sent), lambda part: keep("two", back_two(0, part)), R)
+        g_gate = Summed(normed_two, after(jnp.concatenate(dgates, axis=0), kept["two"]), F, g_down.got)
+        dinner, dgain_second = norm_back(n2, r2, gain_second, after(dnormed_two, g_gate.sent))
         dmiddle = cot.astype(f32) + dinner
-        dmiddle_low = join_tokens(dmiddle.astype(bf16), R)
+        dmiddle_own = dmiddle.astype(bf16)
+        dlow = join_tokens(dmiddle_own, R)
+        g_down.side(dmiddle_own)
+        dm_near = dot(after(dlow[0], g_down.low), wb)
+        args_2 = (proj_2, proj_1, pos, taps[1], gain_out, prm, x_2, u_2, o_2)
+        args_1 = (proj_1, proj_1, pos, taps[0], gain_out, prm, x_1, u_1, o_1)
+        dp_2, dba, dt_2, dg_2, dr_2 = mixer_bwd(*args_2, dm_near, dims, 1, 0)
+        g_up = Summed(normed_two, after(jnp.concatenate(dups, axis=0), dba), F, g_gate.got)
         g_gate.side(g_up.sent)
-        dmixed = dot(dmiddle_low, wb)
-        before = None
-        dprm, dgain_out, dtaps = 0.0, 0.0, {}
-        dproj = {}
-        dp_2, dba, dtaps[1], dg, dpar = mixer_bwd(proj_2, proj_1, pos, taps[1], gain_out, prm, x_2, u_2, o_2, dmixed, dims, 1)
-        g_out = Summed(dmiddle_low, mixed, F)
-        g_up.side(g_out.sent)
-        g_2 = Summed(normed_one, dp_2, F)
-        dp_1, dba, dtaps[0], dg1, dpar1 = mixer_bwd(
-            proj_1, proj_1, pos, taps[0], gain_out, prm, x_1, u_1, o_1, after(dmixed, g_2.sent), dims, 0, dba)
-        g_out.side()
-        g_1 = Summed(normed_one, dp_1, F)
-        g_2.side(g_1.sent)
-        dnormed_one = sum_tokens(
-            lambda lo, hi: dot(dp_1[lo * rows_own : hi * rows_own], wa1, NT) + dot(dp_2[lo * rows_own : hi * rows_own], wa2, NT), R)
-        g_1.side()
-        dprm = dpar + dpar1
-        dgain_out = dg + dg1
-        hidden_late = after(hidden, g_1.sent)
-        layer_out = (middle + sum_tokens(lambda lo, hi: dot(hidden_late[lo * rows_own : hi * rows_own], wd, NT), R)).astype(bf16)
+        dp_1, dba_1, dt_1, dg_1, dr_1 = mixer_bwd(*args_1, after(dm_near, g_gate.low), dims, 0, 0, dba)
+        t_down = g_down.total(R)
+        dm_far = dot(after(dlow[1], dba_1), wb)
+        dp_2, dba, et_2, eg_2, er_2 = mixer_bwd(*args_2, dm_far, dims, 1, 1, None, [dp_2, dba])
+        g_2 = Summed(normed_one, dp_2, F, g_up.got)
+        g_up.side(g_2.sent)
+        t_gate = g_gate.total(R)
+        dp_1, dba_1, et_1, eg_1, er_1 = mixer_bwd(
+            *args_1, after(dm_far, g_up.low, t_down), dims, 0, 1, dba, [dp_1, dba_1])
+        g_1 = Summed(normed_one, dp_1, F, g_2.got)
+        g_out = Summed(jnp.concatenate(dlow, axis=0), after(mixed, g_1.sent), F, g_1.got)
+        t_up = g_up.total(R)
+        g_2.side(g_out.sent)
+
+        def back_one(lo, hi, *needs):
+            return dot(after(dp_1, *needs)[lo:hi], wa1, NT) + dot(dp_2[lo:hi], wa2, NT)
+
+        dnormed_one, far_one = sum_tokens(
+            lambda: back_one(mid, tok, g_out.sent, t_gate), lambda part: keep("one", back_one(0, mid, part, g_2.low)), R)
+        added, unused = sum_tokens(
+            lambda: dot(after(hiddens[1], kept["one"], t_up), wd, NT), lambda part: dot(after(hiddens[0], part), wd, NT), R)
+        layer_out = (middle + added).astype(bf16)
+        g_1.side(kept["one"])
+        g_out.side(g_1.low)
+        t_out = g_out.total(R)
+        dprm = dr_1 + dr_2 + er_1 + er_2
+        dgain_out = dg_1 + dg_2 + eg_1 + eg_2
+        dtaps = [dt_1 + et_1, dt_2 + et_2]
 
         n1 = own32 * rms(own32)
         dfirst, dgain_first = norm_back(n1, rms(own32), gain_first, dnormed_one)
@@ -593,7 +637,8 @@
         def tall(parts):
             return parts.astype(f32).transpose(0, 2, 1).reshape(-1, shard)
 
-        t_1, t_2 = g_1.total(R), g_2.total(R)
+        t_2 = g_2.total(R)
+        t_1 = g_1.total(R)
 
         def joined(lo, width):
             return jnp.stack([t[:, :, lo : lo + width] for t in (t_1, t_2)], axis=2).astype(f32).transpose(1, 0, 2, 3).reshape(shard, -1)
@@ -601,8 +646,8 @@
         grad_query, grad_key = joined(0, hq), joined(hq, hq)
         grad_value, grad_gate_w = joined(2 * hq, hv), joined(2 * hq + hv, hv)
         grad_beta, grad_alpha = wide(t_1[:, :, w1 : w1 + nh]), wide(t_1[:, :, w1 + nh : w1 + 2 * nh])
-        grad_down, grad_out = tall(g_down.total(R)), tall(g_out.total(R))
-        grad_gate, grad_up = wide(g_gate.total(R)), wide(g_up.total(R))
+        grad_down, grad_out = tall(t_down), tall(t_out)
+        grad_gate, grad_up = wide(t_gate), wide(t_up)
 
         def placed(parts, total, width):
             part = jnp.concatenate(parts, axis=1)

time: 1410 us -> 1350 us (0.957)
  waiting for transfers between devices: 509 us -> 393 us
  local copies, waits for them, and re-layouts: 163 us -> 201 us
  other arithmetic: 84.1 us -> 98.4 us
    ppermute x39, waiting for transfers between devices: 454 us -> 318 us  [xor_send(): return lax.ppermute(value, axis, [(i, i ^ step) for i in range(size)])]
    all_gather x6, waiting for transfers between devices: 22.7 us -> 0.03 us  [gather_line(): lax.all_gather(rows, 'fsdp', axis=0, tiled=True, axis_index_groups=lines(...]
    all_to_all x1, waiting for transfers between devices: 0.01 us -> 21.8 us  [spread(): lax.all_to_all(packed.transpose(1, 0, 2), 'rep', 0, 0)]
    unnamed x262 -> x280, local copies, waits for them, and re-layouts: 80.8 us -> 101 us
    concatenate x2 -> x8, other arithmetic: 4.04 us -> 21.6 us  [the longest x1 6.06 us: on_device(): jnp.concatenate(dlow, axis=0)]
    all_to_all x6, waiting for transfers between devices: 31.9 us -> 47 us  [total(): lax.all_to_all(self.sum.reshape(ranks, -1, self.sum.shape[1]), 'rep', 0, 0)]
    pallas_call x2 -> x4, Pallas kernels: 100 us -> 111 us  [mixer_bwd(): pl.pallas_call(functools.partial(bwd_kernel, dims, half, before is not No...]
    dot_general x30 -> x34, matrix products: 376 us -> 367 us  [dot(): lax.dot_general(left, right, dims, preferred_element_type=f32).astype(out)]
  transfers between devices with their start and end apart: 59 -> 60, of which waited for: 21 -> 19; matrix products, arithmetic and copies ran while one was open for 40% -> 44% of each run, Pallas kernels for 12% -> 13%
where the time goes in v2:
time: 1350 us; the launch traced here: 1340 us
  waiting for transfers between devices  393 us (29%)
  matrix products  367 us (27%)
  local copies, waits for them, and re-layouts  201 us (15%)
  Pallas kernels  180 us (13%)
  other arithmetic  98.4 us (7%)
  starting transfers between devices  56 us (4%)
  blocking collectives  24.8 us (2%)
  between operations  16.4 us (1%)
    dot_general x34, matrix products, dot(): lax.dot_general(left, right, dims, preferred_element_type=f32).astype(out)  367 us
    ppermute x39, waiting for transfers between devices, xor_send(): return lax.ppermute(value, axis, [(i, i ^ step) for i in range(size)])  318 us
    pallas_call x4, Pallas kernels, mixer_bwd(): pl.pallas_call(functools.partial(bwd_kernel, dims, half, before is not No...  111 us
    unnamed x280, local copies, waits for them, and re-layouts  101 us
    pallas_call x2, Pallas kernels, mixer_fwd(): pl.pallas_call(functools.partial(fwd_kernel, dims, half), grid=(ns // PAI...  68.8 us
    all_to_all x6, waiting for transfers between devices, total(): lax.all_to_all(self.sum.reshape(ranks, -1, self.sum.shape[1]), 'rep', 0, 0)  47 us
  transfers between devices with their start and end apart: 60, of which 19 were waited for; matrix products, arithmetic and copies ran while one was open for 44% of the time, Pallas kernels for 13%

profile of v2, /device:TPU:0, one launch (start us, length us, event | category | flops | bytes accessed | tf_op | source)
XLA Modules:
  0.0 1338.0 jit_solution(10869702165287916737)
XLA Ops:
  15.4 24.8 %all_to_all.54 = bf16[4,64,3200]{2,1,0:T(8,128)(2,1)S(1)} all-to-all(bf16[4,64,3200]{2,1,0:T(8,128)(2,1)S(1)} %bitcast.180), channel_id=1, replica_groups=mesh['fsdp'=8,'rep'=4] {'rep'}, dimensions={0} | all-to-all | bytes 3276800 | tf_op jit(solution)/shard_map/all_to_all | solution.py:492
  82.7 21.8 %all-to-all-done.2 = bf16[4,64,5248]{2,1,0:T(8,128)(2,1)} async-done(((bf16[4,64,5248]{2,1,0:T(8,128)(2,1)}), bf16[4,64,5248]{2,1,0:T(8,128)(2,1)}, u32[]{:S(2)}, u32[]{:S(2)}) %all-to-all-start.2) | async-done | bytes 2687008 | tf_op jit(solution)/shard_map/all_to_all | solution.py:492
  116.3 32.7 %collective-permute-done.1 = bf16[512,2048]{1,0:T(8,128)(2,1)} collective-permute-done((bf16[512,2048]{1,0:T(8,128)(2,1)}, bf16[512,2048]{1,0:T(8,128)(2,1)}, u32[]{:S(2)}, u32[]{:S(2)}) %collective-permute-start.1) | collective-permute-done | bytes 2097184 | tf_op jit(solution)/shard_map/ppermute | solution.py:351
  189.3 42.7 %collective-permute-done.4 = bf16[512,2048]{1,0:T(8,128)(2,1)} collective-permute-done((bf16[512,2048]{1,0:T(8,128)(2,1)}, bf16[512,2048]{1,0:T(8,128)(2,1)}, u32[]{:S(2)}, u32[]{:S(2)}) %collective-permute-start.4) | collective-permute-done | bytes 2097184 | tf_op jit(solution)/shard_map/ppermute | solution.py:351
  267.7 40.7 %collective-permute-done.9 = bf16[1024,1664]{1,0:T(8,128)(2,1)} collective-permute-done((bf16[1024,1664]{1,0:T(8,128)(2,1)}, bf16[1024,1664]{1,0:T(8,128)(2,1)}, u32[]{:S(2)}, u32[]{:S(2)}) %collective-permute-start.9) | collective-permute-done | bytes 3407904 | tf_op jit(solution)/shard_map/ppermute | solution.py:351
  313.3 21.2 %fusion.81.refs_0_.refs_1_.refs_2_.refs_3_.refs_4_ = f32[2048,1664]{1,0:T(8,128)} fusion(bf16[2048,2048]{1,0:T(8,128)(2,1)S(1)} %bitcast.174, bf16[2048,1664]{1,0:T(8,128)(2,1)} %constant_dynamic-update-slice_fusion.17), kind=kOutput, calls=%fused_computation.282 | convolution fusion | flops 13958643712 | bytes 28835840 | tf_op jit(solution)/shard_map/dot_general | solution.py:372
  334.6 34.6 %shard_map.356 = (bf16[2048,1024]{1,0:T(8,128)(2,1)S(1)}, f32[16,256,256]{2,1,0:T(8,128)}, f32[2048,512]{1,0:T(8,128)}, f32[2048,512]{1,0:T(8,128)}) custom-call(f32[2048,1664]{1,0:T(8,128)} %fusion.81.refs_0_.refs_1_.refs_2_.refs_3_.refs_4_, f32[2048,1664]{1,0:T(8,128)} %fusion.81.refs_0_.refs_1_.refs_2_.refs_3_.refs_4_, ...), custom_call_target="tpu_custom_call" | custom-call | flops 4400000000 | bytes 4000000 | tf_op jit(solution)/shard_map/pallas_call | solution.py:281
  383.2 17.5 %fusion.82.refs_0_.refs_1_.refs_2_.refs_3_ = f32[2048,1536]{1,0:T(8,128)} fusion(bf16[2048,2048]{1,0:T(8,128)(2,1)S(1)} %bitcast.174, bf16[2048,1536]{1,0:T(8,128)(2,1)} %constant_dynamic-update-slice_fusion.19), kind=kOutput, calls=%fused_computation.283 | convolution fusion | flops 12884901888 | bytes 27262976 | tf_op jit(solution)/shard_map/dot_general | solution.py:372
  400.7 34.3 %shard_map.357 = (bf16[2048,1024]{1,0:T(8,128)(2,1)S(1)}, f32[16,256,256]{2,1,0:T(8,128)}, f32[2048,512]{1,0:T(8,128)}, f32[2048,512]{1,0:T(8,128)}) custom-call(f32[2048,1536]{1,0:T(8,128)} %fusion.82.refs_0_.refs_1_.refs_2_.refs_3_, f32[2048,1536]{1,0:T(8,128)} %fusion.82.refs_0_.refs_1_.refs_2_.refs_3_, ...), custom_call_target="tpu_custom_call", output_to_operand_aliasing={{0}: (9, {})} | custom-call | flops 4400000000 | bytes 4000000 | tf_op jit(solution)/shard_map/pallas_call | solution.py:281
  463.2 49.0 %collective-permute-done.16 = bf16[1024,1408]{1,0:T(8,128)(2,1)} collective-permute-done((bf16[1024,1408]{1,0:T(8,128)(2,1)}, bf16[1024,1408]{1,0:T(8,128)(2,1)}, u32[]{:S(2)}, u32[]{:S(2)}) %collective-permute-start.16) | collective-permute-done | bytes 2883616 | tf_op jit(solution)/shard_map/ppermute | solution.py:351
  534.0 42.6 %collective-permute-done.17 = bf16[1024,1408]{1,0:T(8,128)(2,1)} collective-permute-done((bf16[1024,1408]{1,0:T(8,128)(2,1)}, bf16[1024,1408]{1,0:T(8,128)(2,1)}, u32[]{:S(2)}, u32[]{:S(2)}) %collective-permute-start.17) | collective-permute-done | bytes 2883616 | tf_op jit(solution)/shard_map/ppermute | solution.py:351
  693.1 14.2 %multiply_convert_fusion.1 = (bf16[1024,1408]{1,0:T(8,128)(2,1)S(1)}, bf16[1024,1408]{1,0:T(8,128)(2,1)S(1)}) fusion(f32[1024,1408]{1,0:T(8,128)} %fusion.83, f32[1024,1408]{1,0:T(8,128)} %get-tuple-element.235, bf16[1024,2048]{1,0:T(8,128)(2,1)} %get-tuple-element.106, bf16[2048,1408]{1,0:T(8,128)(2,1)} %copy-done.44), kind=kOutput, calls=%fused_computation.22 | convolution fusion | flops 5924323328 | bytes 27262976 | tf_op jit(solution)/shard_map/dot_general | solution.py:372
  780.9 27.4 %shard_map.358 = (bf16[2048,1536]{1,0:T(8,128)(2,1)}, f32[2048,128]{1,0:T(8,128)}, f32[4,1024]{1,0:T(4,128)}, f32[1,256]{1,0:T(1,128)}, f32[8,128]{1,0:T(8,128)}) custom-call(f32[2048,1536]{1,0:T(8,128)} %fusion.82.refs_0_.refs_1_.refs_2_.refs_3_, f32[2048,1536]{1,0:T(8,128)} %fusion.82.refs_0_.refs_1_.refs_2_.refs_3_, ...), custom_call_target="tpu_custom_call" | custom-call | flops 28600000512 | bytes 26000000 | tf_op jit(solution)/shard_map/pallas_call | solution.py:326
  836.6 28.2 %shard_map.359 = (bf16[2048,1664]{1,0:T(8,128)(2,1)}, f32[2048,128]{1,0:T(8,128)}, f32[4,1024]{1,0:T(4,128)}, f32[1,256]{1,0:T(1,128)}, f32[8,128]{1,0:T(8,128)}) custom-call(f32[2048,1664]{1,0:T(8,128)} %fusion.81.refs_0_.refs_1_.refs_2_.refs_3_.refs_4_, f32[2048,1664]{1,0:T(8,128)} %fusion.81.refs_0_.refs_1_.refs_2_.refs_3_.refs_4_, ...), custom_call_target="tpu_custom_call" | custom-call | flops 28600000512 | bytes 26000000 | tf_op jit(solution)/shard_map/pallas_call | solution.py:326
  873.8 27.2 %shard_map.360 = (bf16[2048,1536]{1,0:T(8,128)(2,1)}, f32[2048,128]{1,0:T(8,128)}, f32[4,1024]{1,0:T(4,128)}, f32[1,256]{1,0:T(1,128)}, f32[8,128]{1,0:T(8,128)}) custom-call(f32[2048,1536]{1,0:T(8,128)} %fusion.82.refs_0_.refs_1_.refs_2_.refs_3_, ...), custom_call_target="tpu_custom_call", output_to_operand_aliasing={{0}: (13, {}), {1}: (14, {})} | custom-call | flops 28600000512 | bytes 26000000 | tf_op jit(solution)/shard_map/pallas_call | solution.py:326
  955.2 28.7 %shard_map.361 = (bf16[2048,1664]{1,0:T(8,128)(2,1)}, f32[2048,128]{1,0:T(8,128)}, f32[4,1024]{1,0:T(4,128)}, f32[1,256]{1,0:T(1,128)}, f32[8,128]{1,0:T(8,128)}) custom-call(f32[2048,1664]{1,0:T(8,128)} %fusion.81.refs_0_.refs_1_.refs_2_.refs_3_.refs_4_, ...), custom_call_target="tpu_custom_call", output_to_operand_aliasing={{0}: (14, {}), {1}: (15, {})} | custom-call | flops 28600000512 | bytes 26000000 | tf_op jit(solution)/shard_map/pallas_call | solution.py:326
  983.8 13.0 convolution_convert_fusion.3
  1011.3 12.2 convolution_add_fusion.1
  1028.5 12.0 add_convert_fusion.1
  1045.6 40.8 %collective-permute-done.37 = bf16[1024,1664]{1,0:T(8,128)(2,1)} collective-permute-done((bf16[1024,1664]{1,0:T(8,128)(2,1)}, bf16[1024,1664]{1,0:T(8,128)(2,1)}, u32[]{:S(2)}, u32[]{:S(2)}) %collective-permute-start.37) | collective-permute-done | bytes 3407904 | tf_op jit(solution)/shard_map/ppermute | solution.py:351
  1087.1 14.6 %convolution_add_fusion = f32[1024,2048]{1,0:T(8,128)} fusion(f32[1024,2048]{1,0:T(8,128)} %fusion.50, bf16[2048,1664]{1,0:T(8,128)(2,1)} %constant_dynamic-update-slice_fusion.17, bf16[2048,1664]{1,0:T(8,128)(2,1)} %get-tuple-element.148), kind=kOutput, calls=%fused_computation.78 | convolution fusion | flops 6981419008 | bytes 27000832 | tf_op jit(solution)/shard_map/dot_general | solution.py:372
  1113.0 20.9 %collective-permute-done.38 = bf16[1024,1024]{1,0:T(8,128)(2,1)} collective-permute-done((bf16[1024,1024]{1,0:T(8,128)(2,1)}, bf16[1024,1024]{1,0:T(8,128)(2,1)}, u32[]{:S(2)}, u32[]{:S(2)}) %collective-permute-start.38) | collective-permute-done | bytes 2097184 | tf_op jit(solution)/shard_map/ppermute | solution.py:351
  1174.7 29.0 %collective-permute-done.36 = bf16[512,2048]{1,0:T(8,128)(2,1)} collective-permute-done((bf16[512,2048]{1,0:T(8,128)(2,1)}, bf16[512,2048]{1,0:T(8,128)(2,1)}, u32[]{:S(2)}, u32[]{:S(2)}) %collective-permute-start.36) | collective-permute-done | bytes 2097184 | tf_op jit(solution)/shard_map/ppermute | solution.py:351
  1252.1 31.0 %all-to-all-done.8 = bf16[4,64,1536]{2,1,0:T(8,128)(2,1)S(1)} async-done(((bf16[4,64,1536]{2,1,0:T(8,128)(2,1)}), bf16[4,64,1536]{2,1,0:T(8,128)(2,1)S(1)}, u32[]{:S(2)}, u32[]{:S(2)}) %all-to-all-start.8) | async-done | bytes 786464 | tf_op jit(solution)/shard_map/all_to_all | solution.py:389
  (610 shorter events, 660.5 us)
Async XLA Ops:
  7.2 224.8 %all-gather.9.cloned.1.call-start = ((), (), s32[]{:S(2)}) async-start(), calls=%async_computation.17 | async-start | bytes 4259840 | tf_op jit(solution)/shard_map/all_gather | solution.py:363
  47.5 198.4 %all-gather.7.cloned.1.call-start = ((), (), s32[]{:S(2)}) async-start(), calls=%async_computation.16 | async-start | bytes 3932160 | tf_op jit(solution)/shard_map/all_gather | solution.py:363
  56.3 92.7 %collective-permute-start.7 = (s32[512,1]{0,1:T(1,128)S(1)}, s32[512,1]{0,1:T(1,128)S(1)}, u32[]{:S(2)}, u32[]{:S(2)}) collective-permute-start(s32[512,1]{0,1:T(1,128)S(1)} %bitcast.238), channel_id=1, source_target_pairs={{0,2},{1,3},{2,0},{3,1},{4,6},{5,7},{6,4},{7,5},{8,10},{9,11},{10,... | collective-permute-start | bytes 6152 | tf_op jit(solution)/shard_map/ppermute | solution.py:351
  56.8 92.9 %collective-permute-start.6 = (s32[512,1]{0,1:T(1,128)S(1)}, s32[512,1]{0,1:T(1,128)S(1)}, u32[]{:S(2)}, u32[]{:S(2)}) collective-permute-start(s32[512,1]{0,1:T(1,128)S(1)} %bitcast.239), channel_id=1, source_target_pairs={{0,1},{1,0},{2,3},{3,2},{4,5},{5,4},{6,7},{7,6},{8,9},{9,8},{10,11... | collective-permute-start | bytes 6152 | tf_op jit(solution)/shard_map/ppermute | solution.py:351
  71.9 188.3 %all-gather.11.cloned.1.call-start = ((), (), s32[]{:S(2)}) async-start(), calls=%async_computation.18 | async-start | bytes 2621440 | tf_op jit(solution)/shard_map/all_gather | solution.py:363
  80.6 91.5 %collective-permute-start = (bf16[512,2048]{1,0:T(8,128)(2,1)}, bf16[512,2048]{1,0:T(8,128)(2,1)}, u32[]{:S(2)}, u32[]{:S(2)}) collective-permute-start(bf16[512,2048]{1,0:T(8,128)(2,1)} %pad_maximum_fusion.7), channel_id=1, source_target_pairs={{0,1},{1,0},{2,3},{3,2},{4,5},{5,4},{6,7},{7,6},{8,9},{9,8},{10,11... | collective-permute-start | bytes 6291464 | tf_op jit(solution)/shard_map/ppermute | solution.py:351
  81.1 67.9 %collective-permute-start.1 = (bf16[512,2048]{1,0:T(8,128)(2,1)}, bf16[512,2048]{1,0:T(8,128)(2,1)}, u32[]{:S(2)}, u32[]{:S(2)}) collective-permute-start(bf16[512,2048]{1,0:T(8,128)(2,1)} %pad_maximum_fusion.7), channel_id=1, source_target_pairs={{0,2},{1,3},{2,0},{3,1},{4,6},{5,7},{6,4},{7,5},{8,10},{9,11},{10,... | collective-permute-start | bytes 6291464 | tf_op jit(solution)/shard_map/ppermute | solution.py:351
  106.4 330.6 %all-gather.13.cloned.1.call-start = ((), (), s32[]{:S(2)}) async-start(), calls=%async_computation.19 | async-start | bytes 3604480 | tf_op jit(solution)/shard_map/all_gather | solution.py:363
  155.8 307.4 %all-gather.15.cloned.1.call-start = ((), (), s32[]{:S(2)}) async-start(), calls=%async_computation.20 | async-start | bytes 3604480 | tf_op jit(solution)/shard_map/all_gather | solution.py:363
  189.1 335.9 %all-gather.17.cloned.1.call-start = ((), (), s32[]{:S(2)}) async-start(), calls=%async_computation.21 | async-start | bytes 3604480 | tf_op jit(solution)/shard_map/all_gather | solution.py:363
  232.0 76.4 %collective-permute-start.9 = (bf16[1024,1664]{1,0:T(8,128)(2,1)}, bf16[1024,1664]{1,0:T(8,128)(2,1)}, u32[]{:S(2)}, u32[]{:S(2)}) collective-permute-start(bf16[1024,1664]{1,0:T(8,128)(2,1)} %all-gather.9.cloned.1.call-done), channel_id=1, source_target_pairs={{0,4},{4,0},{8,12},{12,8},{16,20},{20,16},{24,28},{28,24},{1,5},{5... | collective-permute-start | bytes 10223624 | tf_op jit(solution)/shard_map/ppermute | solution.py:351
  308.5 70.0 %collective-permute-start.10 = (bf16[1024,1536]{1,0:T(8,128)(2,1)}, bf16[1024,1536]{1,0:T(8,128)(2,1)}, u32[]{:S(2)}, u32[]{:S(2)}) collective-permute-start(bf16[1024,1536]{1,0:T(8,128)(2,1)} %all-gather.7.cloned.1.call-done), channel_id=1, source_target_pairs={{0,4},{4,0},{8,12},{12,8},{16,20},{20,16},{24,28},{28,24},{1,5},{5... | collective-permute-start | bytes 9437192 | tf_op jit(solution)/shard_map/ppermute | solution.py:351
  463.1 476.6 %reduce-scatter.7.cloned.1.call-start = ((), (), s32[]{:S(2)}) async-start(), calls=%async_computation.22 | async-start | bytes 3604480 | tf_op jit(solution)/shard_map/reduce_scatter | solution.py:386
  576.6 67.9 %collective-permute-start.20 = (bf16[1024,1408]{1,0:T(8,128)(2,1)S(1)}, bf16[1024,1408]{1,0:T(8,128)(2,1)S(1)}, u32[]{:S(2)}, u32[]{:S(2)}) collective-permute-start(bf16[1024,1408]{1,0:T(8,128)(2,1)S(1)} %copy-done.31), channel_id=1, source_target_pairs={{0,4},{4,0},{8,12},{12,8},{16,20},{20,16},{24,28},{28,24},{1,5},{5... | collective-permute-start | bytes 8650760 | tf_op jit(solution)/shard_map/ppermute | solution.py:351
  683.8 75.0 %collective-permute-start.27 = (bf16[1024,1408]{1,0:T(8,128)(2,1)}, bf16[1024,1408]{1,0:T(8,128)(2,1)}, u32[]{:S(2)}, u32[]{:S(2)}) collective-permute-start(bf16[1024,1408]{1,0:T(8,128)(2,1)} %fusion.31), channel_id=1, source_target_pairs={{0,4},{4,0},{8,12},{12,8},{16,20},{20,16},{24,28},{28,24},{1,5},{5... | collective-permute-start | bytes 8650760 | tf_op jit(solution)/shard_map/ppermute | solution.py:351
  759.7 76.9 %collective-permute-start.24 = (bf16[512,2048]{1,0:T(8,128)(2,1)S(1)}, bf16[512,2048]{1,0:T(8,128)(2,1)}, u32[]{:S(2)}, u32[]{:S(2)}) collective-permute-start(bf16[512,2048]{1,0:T(8,128)(2,1)S(1)} %get-tuple-element.156), channel_id=1, source_target_pairs={{0,2},{1,3},{2,0},{3,1},{4,6},{5,7},{6,4},{7,5},{8,10},{9,11},{10,... | collective-permute-start | bytes 6291464 | tf_op jit(solution)/shard_map/ppermute | solution.py:351
  772.0 224.9 %reduce-scatter.9.cloned.1.call-start = ((), (), s32[]{:S(2)}) async-start(), calls=%async_computation.23 | async-start | bytes 3604480 | tf_op jit(solution)/shard_map/reduce_scatter | solution.py:386
  835.6 103.1 %collective-permute-start.29 = (bf16[1024,1408]{1,0:T(8,128)(2,1)}, bf16[1024,1408]{1,0:T(8,128)(2,1)}, u32[]{:S(2)}, u32[]{:S(2)}) collective-permute-start(bf16[1024,1408]{1,0:T(8,128)(2,1)} %convolution_convert_fusion.1), channel_id=1, source_target_pairs={{0,4},{4,0},{8,12},{12,8},{16,20},{20,16},{24,28},{28,24},{1,5},{5... | collective-permute-start | bytes 8650760 | tf_op jit(solution)/shard_map/ppermute | solution.py:351
  938.7 71.3 %collective-permute-start.31 = (bf16[1024,1536]{1,0:T(8,128)(2,1)}, bf16[1024,1536]{1,0:T(8,128)(2,1)}, u32[]{:S(2)}, u32[]{:S(2)}) collective-permute-start(bf16[1024,1536]{1,0:T(8,128)(2,1)} %convolution_convert_fusion), channel_id=1, source_target_pairs={{0,4},{4,0},{8,12},{12,8},{16,20},{20,16},{24,28},{28,24},{1,5},{5... | collective-permute-start | bytes 9437192 | tf_op jit(solution)/shard_map/ppermute | solution.py:351
  943.2 201.0 %reduce-scatter.11.cloned.1.call-start = ((), (), s32[]{:S(2)}) async-start(), calls=%async_computation.24 | async-start | bytes 3604480 | tf_op jit(solution)/shard_map/reduce_scatter | solution.py:386
  1000.4 246.4 %reduce-scatter.15.cloned.1.call-start = ((), (), s32[]{:S(2)}) async-start(), calls=%async_computation.26 | async-start | bytes 3932160 | tf_op jit(solution)/shard_map/reduce_scatter | solution.py:386
  1010.0 76.4 %collective-permute-start.37 = (bf16[1024,1664]{1,0:T(8,128)(2,1)}, bf16[1024,1664]{1,0:T(8,128)(2,1)}, u32[]{:S(2)}, u32[]{:S(2)}) collective-permute-start(bf16[1024,1664]{1,0:T(8,128)(2,1)} %convolution_convert_fusion.3), channel_id=1, source_target_pairs={{0,4},{4,0},{8,12},{12,8},{16,20},{20,16},{24,28},{28,24},{1,5},{5... | collective-permute-start | bytes 10223624 | tf_op jit(solution)/shard_map/ppermute | solution.py:351
  1040.5 251.6 %reduce-scatter.17.cloned.1.call-start = ((), (), s32[]{:S(2)}) async-start(), calls=%async_computation.27 | async-start | bytes 2621440 | tf_op jit(solution)/shard_map/reduce_scatter | solution.py:386
  1147.8 156.6 %reduce-scatter.13.cloned.1.call-start = ((), (), s32[]{:S(2)}) async-start(), calls=%async_computation.25 | async-start | bytes 4259840 | tf_op jit(solution)/shard_map/reduce_scatter | solution.py:386
  (139 other events, 4626.5 us)
Sparse Core Ops, SparseCore 0:
  41.4 68.1 all-gather.8
  111.1 62.1 all-gather.6
  175.4 44.5 all-gather.10
  221.4 57.8 all-gather.12
  280.8 57.8 all-gather.14
  463.2 57.6 all-gather.16
  772.1 53.4 reduce-scatter.6
  835.8 54.3 reduce-scatter.8
  955.3 54.3 reduce-scatter.10
  1040.6 58.3 reduce-scatter.14
  1144.1 40.7 reduce-scatter.16
  1187.2 66.4 reduce-scatter.12

commit v3 on v2

--- a/solution.py
+++ b/solution.py
@@ -402,7 +402,7 @@
         return jnp.concatenate([held[j] for j in range(half)], axis=0)
 
     beyond = xor_send(rows, "rep", size, half)
-    return around(rows), around(beyond)
+    return around(rows), around(beyond), beyond
 
 
 def sum_tokens(far, near, size, *needs):
@@ -506,19 +506,21 @@
         own = mix(tokens, 1)
         part_a = spread(jnp.concatenate([q_h[0], k_h[0], v_h[0], g_h[0], small, q_h[1], k_h[1], v_h[1], g_h[1]], axis=2))
         w1 = 2 * hq + 2 * hv
+        part_a = after(part_a, own)
         part_1, part_2 = part_a[:, : w1 + 128], part_a[:, w1 + 128 :]
         extra_all = lax.all_to_all(jnp.broadcast_to(after(extra, part_a)[None], (N, *extra.shape)), both, 0, 0)
         extra_all = extra_all.transpose(1, 0, 2).reshape(-1, D).astype(f32)
         line_1 = gather_line(part_1, F)
-        every = jnp.concatenate(join_tokens(own, R), axis=0)
-        ids_all = jnp.concatenate(join_tokens(segments[:, None], R), axis=0).reshape(ns, SEQ)
-        part_r = spread(quarter([after(w_out.T, extra_all), w_ffgate, w_ffup, w_down.T]))
+        every_near, every_far, every_got = join_tokens(own, R)
+        every = jnp.concatenate([every_near, every_far], axis=0)
+        ids_all = jnp.concatenate(join_tokens(segments[:, None], R)[:2], axis=0).reshape(ns, SEQ)
+        part_r = spread(quarter([after(w_out.T, extra_all, every_got), w_ffgate, w_ffup, w_down.T]))
         part_b, part_g, part_u, part_d = (
             part_r[:, :wv], part_r[:, wv : wv + ffq], part_r[:, wv + ffq : wv + 2 * ffq], part_r[:, wv + 2 * ffq :])
         line_2 = gather_line(after(part_2, extra_all), F)
         wa1, side_1 = gather_side(line_1, F)
         cot = mix(cotangent, 1)
-        cot_near, cot_far = join_tokens(after(cot, every), R)
+        cot_near, cot_far, unused = join_tokens(after(cot, line_1), R)
         line_b = gather_line(part_b, F)
         line_g = gather_line(part_g, F)
         line_u = gather_line(part_u, F)
@@ -541,10 +543,10 @@
 
         every32 = every.astype(f32)
         normed_one = (every32 * rms(every32) * gain_first).astype(bf16)
-        proj_1 = dot(after(normed_one, line_2, cot_near, cot_far, part_r, pos), wa1)
+        proj_1 = dot(after(normed_one, line_2, part_r), wa1)
         mixed, x_1, u_1, o_1 = mixer_fwd(proj_1, proj_1, pos, taps[0], gain_out, prm, dims, 0)
         wa2, side_2 = gather_side(line_2, F, side_1)
-        proj_2 = dot(after(normed_one, mixed, line_b), wa2)
+        proj_2 = dot(after(normed_one, mixed, line_b, cot_near, cot_far), wa2)
         mixed, x_2, u_2, o_2 = mixer_fwd(proj_2, proj_1, pos, taps[1], gain_out, prm, dims, 1, mixed)
         wb, side_b = gather_side(line_b, F, side_2)
         mixed = after(mixed, line_g)
@@ -557,7 +559,7 @@
         n2 = middle * r2
         normed_own = (n2 * gain_second).astype(bf16)
         wu, side_u = gather_side(line_u, F, side_g)
-        two = join_tokens(after(normed_own, line_u), R)
+        two = join_tokens(after(normed_own, line_u), R)[:2]
         wd, side_d = gather_side(line_d, F, side_u)
         gates, ups, acts, sigs, hiddens = [], [], [], [], []
         for normed in two:
@@ -586,13 +588,13 @@
             return dot(dgates[t], wg, NT) + dot(dups[t], wu, NT)
 
         dnormed_two, far_two = sum_tokens(lambda: back_two(1, g_down.sent), lambda part: keep("two", back_two(0, part)), R)
-        g_gate = Summed(normed_two, after(jnp.concatenate(dgates, axis=0), kept["two"]), F, g_down.got)
+        g_down.side(kept["two"])
+        g_gate = Summed(normed_two, after(jnp.concatenate(dgates, axis=0), g_down.low), F, g_down.got)
         dinner, dgain_second = norm_back(n2, r2, gain_second, after(dnormed_two, g_gate.sent))
         dmiddle = cot.astype(f32) + dinner
         dmiddle_own = dmiddle.astype(bf16)
-        dlow = join_tokens(dmiddle_own, R)
-        g_down.side(dmiddle_own)
-        dm_near = dot(after(dlow[0], g_down.low), wb)
+        dlow = join_tokens(dmiddle_own, R)[:2]
+        dm_near = dot(dlow[0], wb)
         args_2 = (proj_2, proj_1, pos, taps[1], gain_out, prm, x_2, u_2, o_2)
         args_1 = (proj_1, proj_1, pos, taps[0], gain_out, prm, x_1, u_1, o_1)
         dp_2, dba, dt_2, dg_2, dr_2 = mixer_bwd(*args_2, dm_near, dims, 1, 0)
@@ -600,28 +602,28 @@
         g_gate.side(g_up.sent)
         dp_1, dba_1, dt_1, dg_1, dr_1 = mixer_bwd(*args_1, after(dm_near, g_gate.low), dims, 0, 0, dba)
         t_down = g_down.total(R)
+        g_out = Summed(jnp.concatenate(dlow, axis=0), after(mixed, dba_1), F, g_up.got)
         dm_far = dot(after(dlow[1], dba_1), wb)
-        dp_2, dba, et_2, eg_2, er_2 = mixer_bwd(*args_2, dm_far, dims, 1, 1, None, [dp_2, dba])
-        g_2 = Summed(normed_one, dp_2, F, g_up.got)
-        g_up.side(g_2.sent)
+        dp_2, dba, et_2, eg_2, er_2 = mixer_bwd(*args_2, after(dm_far, g_out.sent), dims, 1, 1, None, [dp_2, dba])
+        g_up.side(dba)
+        g_2 = Summed(normed_one, after(dp_2, g_up.low), F)
         t_gate = g_gate.total(R)
         dp_1, dba_1, et_1, eg_1, er_1 = mixer_bwd(
-            *args_1, after(dm_far, g_up.low, t_down), dims, 0, 1, dba, [dp_1, dba_1])
+            *args_1, after(dm_far, g_2.sent, t_down), dims, 0, 1, dba, [dp_1, dba_1])
         g_1 = Summed(normed_one, dp_1, F, g_2.got)
-        g_out = Summed(jnp.concatenate(dlow, axis=0), after(mixed, g_1.sent), F, g_1.got)
         t_up = g_up.total(R)
-        g_2.side(g_out.sent)
+        g_out.side(g_1.sent)
+        g_2.side(g_out.low)
 
         def back_one(lo, hi, *needs):
-            return dot(after(dp_1, *needs)[lo:hi], wa1, NT) + dot(dp_2[lo:hi], wa2, NT)
+            return dot(after(dp_1, *needs)[lo:hi], wa1, NT) + dot(after(dp_2, *needs)[lo:hi], wa2, NT)
 
         dnormed_one, far_one = sum_tokens(
-            lambda: back_one(mid, tok, g_out.sent, t_gate), lambda part: keep("one", back_one(0, mid, part, g_2.low)), R)
+            lambda: back_one(mid, tok, g_out.low, t_gate), lambda part: keep("one", back_one(0, mid, part, g_2.low)), R)
         added, unused = sum_tokens(
             lambda: dot(after(hiddens[1], kept["one"], t_up), wd, NT), lambda part: dot(after(hiddens[0], part), wd, NT), R)
         layer_out = (middle + added).astype(bf16)
         g_1.side(kept["one"])
-        g_out.side(g_1.low)
         t_out = g_out.total(R)
         dprm = dr_1 + dr_2 + er_1 + er_2
         dgain_out = dg_1 + dg_2 + eg_1 + eg_2

time: 1350 us -> 1290 us (0.956)
  waiting for transfers between devices: 393 us -> 294 us
    ppermute x39, waiting for transfers between devices: 318 us -> 217 us  [xor_send(): return lax.ppermute(value, axis, [(i, i ^ step) for i in range(size)])]
    all_to_all x1, waiting for transfers between devices: 21.8 us -> 1.38 us  [spread(): lax.all_to_all(packed.transpose(1, 0, 2), 'rep', 0, 0)]
    unnamed x280 -> x265, local copies, waits for them, and re-layouts: 101 us -> 107 us
  transfers between devices with their start and end apart: 60 -> 60, of which waited for: 19 -> 17; matrix products, arithmetic and copies ran while one was open for 44% -> 46% of each run, Pallas kernels for 13% -> 14%
where the time goes in v3:
time: 1290 us; the launch traced here: 1280 us
  matrix products  368 us (29%)
  waiting for transfers between devices  294 us (23%)
  local copies, waits for them, and re-layouts  209 us (16%)
  Pallas kernels  179 us (14%)
  other arithmetic  108 us (8%)
  starting transfers between devices  68.3 us (5%)
  blocking collectives  34.6 us (3%)
  between operations  16.5 us (1%)
    dot_general x34, matrix products, dot(): lax.dot_general(left, right, dims, preferred_element_type=f32).astype(out)  368 us
    ppermute x39, waiting for transfers between devices, xor_send(): return lax.ppermute(value, axis, [(i, i ^ step) for i in range(size)])  217 us
    pallas_call x4, Pallas kernels, mixer_bwd(): pl.pallas_call(functools.partial(bwd_kernel, dims, half, before is not No...  111 us
    unnamed x265, local copies, waits for them, and re-layouts  107 us
    pallas_call x2, Pallas kernels, mixer_fwd(): pl.pallas_call(functools.partial(fwd_kernel, dims, half), grid=(ns // PAI...  68.4 us
    all_to_all x6, waiting for transfers between devices, total(): lax.all_to_all(self.sum.reshape(ranks, -1, self.sum.shape[1]), 'rep', 0, 0)  58.8 us
    all_to_all x1, blocking collectives, spread(): lax.all_to_all(packed.transpose(1, 0, 2), 'rep', 0, 0)  34.6 us
    ppermute x39, starting transfers between devices, xor_send(): return lax.ppermute(value, axis, [(i, i ^ step) for i in range(size)])  29.6 us
  transfers between devices with their start and end apart: 60, of which 17 were waited for; matrix products, arithmetic and copies ran while one was open for 46% of the time, Pallas kernels for 14%

profile of v3, /device:TPU:0, one launch (start us, length us, event | category | flops | bytes accessed | tf_op | source)
XLA Modules:
  0.0 1276.8 jit_solution(2197762859714923736)
XLA Ops:
  72.0 29.6 %collective-permute-done.1 = bf16[512,2048]{1,0:T(8,128)(2,1)} collective-permute-done((bf16[512,2048]{1,0:T(8,128)(2,1)}, bf16[512,2048]{1,0:T(8,128)(2,1)}, u32[]{:S(2)}, u32[]{:S(2)}) %collective-permute-start.1) | collective-permute-done | bytes 2097184 | tf_op jit(solution)/shard_map/ppermute | solution.py:351
  107.6 34.6 %all_to_all.54 = bf16[4,64,5248]{2,1,0:T(8,128)(2,1)S(1)} all-to-all(bf16[4,64,5248]{2,1,0:T(8,128)(2,1)S(1)} %copy.270), channel_id=1, replica_groups=mesh['fsdp'=8,'rep'=4] {'rep'}, dimensions={0} | all-to-all | bytes 5373952 | tf_op jit(solution)/shard_map/all_to_all | solution.py:492
  211.9 13.0 %all-gather.11.cloned.1.call-done = bf16[1024,1024]{1,0:T(8,128)(2,1)} async-done(((bf16[256,1024]{1,0:T(8,128)(2,1)}), bf16[1024,1024]{1,0:T(8,128)(2,1)}) %all-gather.11.cloned.1.call-update) | async-done | bytes 2097168 | tf_op jit(solution)/shard_map/all_gather | solution.py:363
  256.5 18.3 %fusion.86.refs_0_.refs_1_.refs_2_.refs_3_.refs_4_ = f32[2048,1664]{1,0:T(8,128)} fusion(bf16[2048,2048]{1,0:T(8,128)(2,1)S(1)} %bitcast.181, bf16[2048,1664]{1,0:T(8,128)(2,1)S(1)} %constant_dynamic-update-slice_fusion.13), kind=kOutput, calls=%fused_computation.286 | convolution fusion | flops 13958643712 | bytes 28835840 | tf_op jit(solution)/shard_map/dot_general | solution.py:372
  274.8 34.3 %shard_map.356 = (bf16[2048,1024]{1,0:T(8,128)(2,1)S(1)}, f32[16,256,256]{2,1,0:T(8,128)}, f32[2048,512]{1,0:T(8,128)}, f32[2048,512]{1,0:T(8,128)}) custom-call(f32[2048,1664]{1,0:T(8,128)} %fusion.86.refs_0_.refs_1_.refs_2_.refs_3_.refs_4_, f32[2048,1664]{1,0:T(8,128)} %fusion.86.refs_0_.refs_1_.refs_2_.refs_3_.refs_4_, ...), custom_call_target="tpu_custom_call" | custom-call | flops 4400000000 | bytes 4000000 | tf_op jit(solution)/shard_map/pallas_call | solution.py:281
  327.6 17.8 %fusion.87.refs_0_.refs_1_.refs_2_.refs_3_ = f32[2048,1536]{1,0:T(8,128)} fusion(bf16[2048,2048]{1,0:T(8,128)(2,1)S(1)} %bitcast.181, bf16[2048,1536]{1,0:T(8,128)(2,1)} %constant_dynamic-update-slice_fusion.19), kind=kOutput, calls=%fused_computation.287 | convolution fusion | flops 12884901888 | bytes 27262976 | tf_op jit(solution)/shard_map/dot_general | solution.py:372
  345.4 34.0 %shard_map.357 = (bf16[2048,1024]{1,0:T(8,128)(2,1)S(1)}, f32[16,256,256]{2,1,0:T(8,128)}, f32[2048,512]{1,0:T(8,128)}, f32[2048,512]{1,0:T(8,128)}) custom-call(f32[2048,1536]{1,0:T(8,128)} %fusion.87.refs_0_.refs_1_.refs_2_.refs_3_, f32[2048,1536]{1,0:T(8,128)} %fusion.87.refs_0_.refs_1_.refs_2_.refs_3_, ...), custom_call_target="tpu_custom_call", output_to_operand_aliasing={{0}: (9, {})} | custom-call | flops 4400000000 | bytes 4000000 | tf_op jit(solution)/shard_map/pallas_call | solution.py:281
  408.7 47.7 %collective-permute-done.16 = bf16[1024,1408]{1,0:T(8,128)(2,1)} collective-permute-done((bf16[1024,1408]{1,0:T(8,128)(2,1)}, bf16[1024,1408]{1,0:T(8,128)(2,1)}, u32[]{:S(2)}, u32[]{:S(2)}) %collective-permute-start.16) | collective-permute-done | bytes 2883616 | tf_op jit(solution)/shard_map/ppermute | solution.py:351
  478.5 42.2 %collective-permute-done.17 = bf16[1024,1408]{1,0:T(8,128)(2,1)} collective-permute-done((bf16[1024,1408]{1,0:T(8,128)(2,1)}, bf16[1024,1408]{1,0:T(8,128)(2,1)}, u32[]{:S(2)}, u32[]{:S(2)}) %collective-permute-start.17) | collective-permute-done | bytes 2883616 | tf_op jit(solution)/shard_map/ppermute | solution.py:351
  542.7 11.9 multiply_convert_fusion.5
  638.8 14.2 %multiply_convert_fusion.1 = (bf16[1024,1408]{1,0:T(8,128)(2,1)S(1)}, bf16[1024,1408]{1,0:T(8,128)(2,1)S(1)}) fusion(f32[1024,1408]{1,0:T(8,128)} %fusion.88, f32[1024,1408]{1,0:T(8,128)} %get-tuple-element.239, bf16[1024,2048]{1,0:T(8,128)(2,1)} %get-tuple-element.110, bf16[2048,1408]{1,0:T(8,128)(2,1)} %copy-done.48), kind=kOutput, calls=%fused_computation.22 | convolution fusion | flops 5924323328 | bytes 27262976 | tf_op jit(solution)/shard_map/dot_general | solution.py:372
  742.9 27.6 %shard_map.358 = (bf16[2048,1536]{1,0:T(8,128)(2,1)}, f32[2048,128]{1,0:T(8,128)}, f32[4,1024]{1,0:T(4,128)}, f32[1,256]{1,0:T(1,128)}, f32[8,128]{1,0:T(8,128)}) custom-call(f32[2048,1536]{1,0:T(8,128)} %fusion.87.refs_0_.refs_1_.refs_2_.refs_3_, f32[2048,1536]{1,0:T(8,128)} %fusion.87.refs_0_.refs_1_.refs_2_.refs_3_, ...), custom_call_target="tpu_custom_call" | custom-call | flops 28600000512 | bytes 26000000 | tf_op jit(solution)/shard_map/pallas_call | solution.py:326
  805.8 27.7 %shard_map.359 = (bf16[2048,1664]{1,0:T(8,128)(2,1)}, f32[2048,128]{1,0:T(8,128)}, f32[4,1024]{1,0:T(4,128)}, f32[1,256]{1,0:T(1,128)}, f32[8,128]{1,0:T(8,128)}) custom-call(f32[2048,1664]{1,0:T(8,128)} %fusion.86.refs_0_.refs_1_.refs_2_.refs_3_.refs_4_, f32[2048,1664]{1,0:T(8,128)} %fusion.86.refs_0_.refs_1_.refs_2_.refs_3_.refs_4_, ...), custom_call_target="tpu_custom_call" | custom-call | flops 28600000512 | bytes 26000000 | tf_op jit(solution)/shard_map/pallas_call | solution.py:326
  857.0 27.4 %shard_map.360 = (bf16[2048,1536]{1,0:T(8,128)(2,1)}, f32[2048,128]{1,0:T(8,128)}, f32[4,1024]{1,0:T(4,128)}, f32[1,256]{1,0:T(1,128)}, f32[8,128]{1,0:T(8,128)}) custom-call(f32[2048,1536]{1,0:T(8,128)} %fusion.87.refs_0_.refs_1_.refs_2_.refs_3_, ...), custom_call_target="tpu_custom_call", output_to_operand_aliasing={{0}: (13, {}), {1}: (14, {})} | custom-call | flops 28600000512 | bytes 26000000 | tf_op jit(solution)/shard_map/pallas_call | solution.py:326
  886.5 12.0 add_convert_fusion.2
  912.1 28.0 %shard_map.361 = (bf16[2048,1664]{1,0:T(8,128)(2,1)}, f32[2048,128]{1,0:T(8,128)}, f32[4,1024]{1,0:T(4,128)}, f32[1,256]{1,0:T(1,128)}, f32[8,128]{1,0:T(8,128)}) custom-call(f32[2048,1664]{1,0:T(8,128)} %fusion.86.refs_0_.refs_1_.refs_2_.refs_3_.refs_4_, ...), custom_call_target="tpu_custom_call", output_to_operand_aliasing={{0}: (14, {}), {1}: (15, {})} | custom-call | flops 28600000512 | bytes 26000000 | tf_op jit(solution)/shard_map/pallas_call | solution.py:326
  943.2 13.2 %convolution_convert_fusion.3 = bf16[1024,1664]{1,0:T(8,128)(2,1)} fusion(bf16[2048,1664]{1,0:T(8,128)(2,1)} %get-tuple-element.156, bf16[2048,2048]{1,0:T(8,128)(2,1)} %fusion.2), kind=kOutput, calls=%fused_computation.89 | convolution fusion | flops 6981025792 | bytes 14417920 | tf_op jit(solution)/shard_map/dot_general | solution.py:372
  970.1 44.2 %collective-permute-done.32 = bf16[1024,1536]{1,0:T(8,128)(2,1)} collective-permute-done((bf16[1024,1536]{1,0:T(8,128)(2,1)}, bf16[1024,1536]{1,0:T(8,128)(2,1)}, u32[]{:S(2)}, u32[]{:S(2)}) %collective-permute-start.32) | collective-permute-done | bytes 3145760 | tf_op jit(solution)/shard_map/ppermute | solution.py:351
  1014.8 12.0 fusion.56
  1026.8 12.3 convolution_add_fusion.1
  1061.9 12.2 fusion.54
  1077.9 12.3 convolution_add_fusion
  1129.0 20.0 %all-to-all-done.9 = bf16[4,64,1024]{2,1,0:T(8,128)(2,1)S(1)} async-done(((bf16[4,64,1024]{2,1,0:T(8,128)(2,1)}), bf16[4,64,1024]{2,1,0:T(8,128)(2,1)S(1)}, u32[]{:S(2)}, u32[]{:S(2)}) %all-to-all-start.9) | async-done | bytes 524320 | tf_op jit(solution)/shard_map/all_to_all | solution.py:389
  1200.5 31.0 %all-to-all-done.8 = bf16[4,64,1536]{2,1,0:T(8,128)(2,1)S(1)} async-done(((bf16[4,64,1536]{2,1,0:T(8,128)(2,1)}), bf16[4,64,1536]{2,1,0:T(8,128)(2,1)S(1)}, u32[]{:S(2)}, u32[]{:S(2)}) %all-to-all-start.8) | async-done | bytes 786464 | tf_op jit(solution)/shard_map/all_to_all | solution.py:389
  (595 shorter events, 682.6 us)
Async XLA Ops:
  20.9 155.2 %all-gather.9.cloned.1.call-start = ((), (), s32[]{:S(2)}) async-start(), calls=%async_computation.17 | async-start | bytes 4259840 | tf_op jit(solution)/shard_map/all_gather | solution.py:363
  52.5 149.3 %all-gather.7.cloned.1.call-start = ((), (), s32[]{:S(2)}) async-start(), calls=%async_computation.16 | async-start | bytes 3932160 | tf_op jit(solution)/shard_map/all_gather | solution.py:363
  64.6 160.3 %all-gather.11.cloned.1.call-start = ((), (), s32[]{:S(2)}) async-start(), calls=%async_computation.18 | async-start | bytes 2621440 | tf_op jit(solution)/shard_map/all_gather | solution.py:363
  144.6 236.8 %all-gather.13.cloned.1.call-start = ((), (), s32[]{:S(2)}) async-start(), calls=%async_computation.19 | async-start | bytes 3604480 | tf_op jit(solution)/shard_map/all_gather | solution.py:363
  147.7 261.0 %all-gather.15.cloned.1.call-start = ((), (), s32[]{:S(2)}) async-start(), calls=%async_computation.20 | async-start | bytes 3604480 | tf_op jit(solution)/shard_map/all_gather | solution.py:363
  176.0 292.3 %all-gather.17.cloned.1.call-start = ((), (), s32[]{:S(2)}) async-start(), calls=%async_computation.21 | async-start | bytes 3604480 | tf_op jit(solution)/shard_map/all_gather | solution.py:363
  176.1 76.3 %collective-permute-start.3 = (bf16[1024,1664]{1,0:T(8,128)(2,1)}, bf16[1024,1664]{1,0:T(8,128)(2,1)}, u32[]{:S(2)}, u32[]{:S(2)}) collective-permute-start(bf16[1024,1664]{1,0:T(8,128)(2,1)} %all-gather.9.cloned.1.call-done), channel_id=1, source_target_pairs={{0,4},{4,0},{8,12},{12,8},{16,20},{20,16},{24,28},{28,24},{1,5},{5... | collective-permute-start | bytes 10223624 | tf_op jit(solution)/shard_map/ppermute | solution.py:351
  236.4 72.7 %collective-permute-start.9 = (bf16[512,2048]{1,0:T(8,128)(2,1)}, bf16[512,2048]{1,0:T(8,128)(2,1)S(1)}, u32[]{:S(2)}, u32[]{:S(2)}) collective-permute-start(bf16[512,2048]{1,0:T(8,128)(2,1)} %collective-permute-done.8), channel_id=1, source_target_pairs={{0,1},{1,0},{2,3},{3,2},{4,5},{5,4},{6,7},{7,6},{8,9},{9,8},{10,11... | collective-permute-start | bytes 6291464 | tf_op jit(solution)/shard_map/ppermute | solution.py:351
  252.4 69.9 %collective-permute-start.10 = (bf16[1024,1536]{1,0:T(8,128)(2,1)}, bf16[1024,1536]{1,0:T(8,128)(2,1)}, u32[]{:S(2)}, u32[]{:S(2)}) collective-permute-start(bf16[1024,1536]{1,0:T(8,128)(2,1)} %all-gather.7.cloned.1.call-done), channel_id=1, source_target_pairs={{0,4},{4,0},{8,12},{12,8},{16,20},{20,16},{24,28},{28,24},{1,5},{5... | collective-permute-start | bytes 9437192 | tf_op jit(solution)/shard_map/ppermute | solution.py:351
  391.2 65.2 %collective-permute-start.16 = (bf16[1024,1408]{1,0:T(8,128)(2,1)}, bf16[1024,1408]{1,0:T(8,128)(2,1)}, u32[]{:S(2)}, u32[]{:S(2)}) collective-permute-start(bf16[1024,1408]{1,0:T(8,128)(2,1)} %all-gather.13.cloned.1.call-done), channel_id=1, source_target_pairs={{0,4},{4,0},{8,12},{12,8},{16,20},{20,16},{24,28},{28,24},{1,5},{5... | collective-permute-start | bytes 8650760 | tf_op jit(solution)/shard_map/ppermute | solution.py:351
  408.6 424.9 %reduce-scatter.7.cloned.1.call-start = ((), (), s32[]{:S(2)}) async-start(), calls=%async_computation.22 | async-start | bytes 3604480 | tf_op jit(solution)/shard_map/reduce_scatter | solution.py:386
  474.2 65.1 %collective-permute-start.18 = (bf16[512,2048]{1,0:T(8,128)(2,1)S(1)}, bf16[512,2048]{1,0:T(8,128)(2,1)S(1)}, u32[]{:S(2)}, u32[]{:S(2)}) collective-permute-start(bf16[512,2048]{1,0:T(8,128)(2,1)S(1)} %multiply_convert_fusion.6), channel_id=1, source_target_pairs={{0,2},{1,3},{2,0},{3,1},{4,6},{5,7},{6,4},{7,5},{8,10},{9,11},{10,... | collective-permute-start | bytes 6291464 | tf_op jit(solution)/shard_map/ppermute | solution.py:351
  520.8 67.6 %collective-permute-start.20 = (bf16[1024,1408]{1,0:T(8,128)(2,1)S(1)}, bf16[1024,1408]{1,0:T(8,128)(2,1)S(1)}, u32[]{:S(2)}, u32[]{:S(2)}) collective-permute-start(bf16[1024,1408]{1,0:T(8,128)(2,1)S(1)} %copy-done.32), channel_id=1, source_target_pairs={{0,4},{4,0},{8,12},{12,8},{16,20},{20,16},{24,28},{28,24},{1,5},{5... | collective-permute-start | bytes 8650760 | tf_op jit(solution)/shard_map/ppermute | solution.py:351
  628.0 65.2 %collective-permute-start.24 = (bf16[1024,1408]{1,0:T(8,128)(2,1)}, bf16[1024,1408]{1,0:T(8,128)(2,1)}, u32[]{:S(2)}, u32[]{:S(2)}) collective-permute-start(bf16[1024,1408]{1,0:T(8,128)(2,1)} %fusion.35), channel_id=1, source_target_pairs={{0,4},{4,0},{8,12},{12,8},{16,20},{20,16},{24,28},{28,24},{1,5},{5... | collective-permute-start | bytes 8650760 | tf_op jit(solution)/shard_map/ppermute | solution.py:351
  637.1 78.4 %collective-permute-start.23 = (bf16[512,2048]{1,0:T(8,128)(2,1)}, bf16[512,2048]{1,0:T(8,128)(2,1)}, u32[]{:S(2)}, u32[]{:S(2)}) collective-permute-start(bf16[512,2048]{1,0:T(8,128)(2,1)} %fusion.26), channel_id=1, source_target_pairs={{0,2},{1,3},{2,0},{3,1},{4,6},{5,7},{6,4},{7,5},{8,10},{9,11},{10,... | collective-permute-start | bytes 6291464 | tf_op jit(solution)/shard_map/ppermute | solution.py:351
  727.9 228.6 %reduce-scatter.9.cloned.1.call-start = ((), (), s32[]{:S(2)}) async-start(), calls=%async_computation.23 | async-start | bytes 3604480 | tf_op jit(solution)/shard_map/reduce_scatter | solution.py:386
  729.5 76.3 %collective-permute-start.25 = (bf16[512,2048]{1,0:T(8,128)(2,1)S(1)}, bf16[512,2048]{1,0:T(8,128)(2,1)}, u32[]{:S(2)}, u32[]{:S(2)}) collective-permute-start(bf16[512,2048]{1,0:T(8,128)(2,1)S(1)} %get-tuple-element.162), channel_id=1, source_target_pairs={{0,2},{1,3},{2,0},{3,1},{4,6},{5,7},{6,4},{7,5},{8,10},{9,11},{10,... | collective-permute-start | bytes 6291464 | tf_op jit(solution)/shard_map/ppermute | solution.py:351
  804.2 82.2 %collective-permute-start.29 = (bf16[1024,1408]{1,0:T(8,128)(2,1)}, bf16[1024,1408]{1,0:T(8,128)(2,1)}, u32[]{:S(2)}, u32[]{:S(2)}) collective-permute-start(bf16[1024,1408]{1,0:T(8,128)(2,1)} %convolution_convert_fusion.1), channel_id=1, source_target_pairs={{0,4},{4,0},{8,12},{12,8},{16,20},{20,16},{24,28},{28,24},{1,5},{5... | collective-permute-start | bytes 8650760 | tf_op jit(solution)/shard_map/ppermute | solution.py:351
  837.1 237.1 %reduce-scatter.11.cloned.1.call-start = ((), (), s32[]{:S(2)}) async-start(), calls=%async_computation.24 | async-start | bytes 3604480 | tf_op jit(solution)/shard_map/reduce_scatter | solution.py:386
  910.4 103.9 %collective-permute-start.32 = (bf16[1024,1536]{1,0:T(8,128)(2,1)}, bf16[1024,1536]{1,0:T(8,128)(2,1)}, u32[]{:S(2)}, u32[]{:S(2)}) collective-permute-start(bf16[1024,1536]{1,0:T(8,128)(2,1)} %convolution_convert_fusion), channel_id=1, source_target_pairs={{0,4},{4,0},{8,12},{12,8},{16,20},{20,16},{24,28},{28,24},{1,5},{5... | collective-permute-start | bytes 9437192 | tf_op jit(solution)/shard_map/ppermute | solution.py:351
  960.0 137.2 %reduce-scatter.17.cloned.1.call-start = ((), (), s32[]{:S(2)}) async-start(), calls=%async_computation.27 | async-start | bytes 2621440 | tf_op jit(solution)/shard_map/reduce_scatter | solution.py:386
  970.1 225.2 %reduce-scatter.15.cloned.1.call-start = ((), (), s32[]{:S(2)}) async-start(), calls=%async_computation.26 | async-start | bytes 3932160 | tf_op jit(solution)/shard_map/reduce_scatter | solution.py:386
  1014.3 103.2 %collective-permute-start.38 = (bf16[1024,1664]{1,0:T(8,128)(2,1)}, bf16[1024,1664]{1,0:T(8,128)(2,1)}, u32[]{:S(2)}, u32[]{:S(2)}) collective-permute-start(bf16[1024,1664]{1,0:T(8,128)(2,1)} %convolution_convert_fusion.3), channel_id=1, source_target_pairs={{0,4},{4,0},{8,12},{12,8},{16,20},{20,16},{24,28},{28,24},{1,5},{5... | collective-permute-start | bytes 10223624 | tf_op jit(solution)/shard_map/ppermute | solution.py:351
  1100.7 140.5 %reduce-scatter.13.cloned.1.call-start = ((), (), s32[]{:S(2)}) async-start(), calls=%async_computation.25 | async-start | bytes 4259840 | tf_op jit(solution)/shard_map/reduce_scatter | solution.py:386
  (131 other events, 3850.2 us)
Sparse Core Ops, SparseCore 0:
  44.6 69.8 all-gather.8
  116.1 62.1 all-gather.6
  180.4 44.5 all-gather.10
  226.4 57.8 all-gather.12
  285.7 57.8 all-gather.14
  408.7 58.2 all-gather.16
  728.0 57.1 reduce-scatter.6
  804.4 57.1 reduce-scatter.8
  898.6 56.5 reduce-scatter.10
  970.2 44.3 reduce-scatter.16
  1055.8 61.3 reduce-scatter.14
  1129.2 67.8 reduce-scatter.12

commit v4 on v3

--- a/solution.py
+++ b/solution.py
@@ -368,6 +368,13 @@
     return jnp.concatenate([near, got], axis=0), got
 
 
+def gather_side_first(rows, size, *needs):
+    got = xor_send(after(rows, *needs), "fsdp", size, 1)
+    full = gather_line(jnp.concatenate([rows, got], axis=0), size)
+    width = rows.shape[1]
+    return full.reshape(size // 2, 2, -1, width).swapaxes(0, 1).reshape(-1, width), full, got
+
+
 def dot(left, right, dims=NN, out=f32):
     return lax.dot_general(left, right, dims, preferred_element_type=f32).astype(out)
 
@@ -514,17 +521,16 @@
         every_near, every_far, every_got = join_tokens(own, R)
         every = jnp.concatenate([every_near, every_far], axis=0)
         ids_all = jnp.concatenate(join_tokens(segments[:, None], R)[:2], axis=0).reshape(ns, SEQ)
-        part_r = spread(quarter([after(w_out.T, extra_all, every_got), w_ffgate, w_ffup, w_down.T]))
+        part_r = spread(quarter([after(w_out.T, extra_all, every_got, line_1), w_ffgate, w_ffup, w_down.T]))
         part_b, part_g, part_u, part_d = (
             part_r[:, :wv], part_r[:, wv : wv + ffq], part_r[:, wv + ffq : wv + 2 * ffq], part_r[:, wv + 2 * ffq :])
         line_2 = gather_line(after(part_2, extra_all), F)
         wa1, side_1 = gather_side(line_1, F)
         cot = mix(cotangent, 1)
-        cot_near, cot_far, unused = join_tokens(after(cot, line_1), R)
+        cot_near, cot_far, unused = join_tokens(after(cot, side_1), R)
         line_b = gather_line(part_b, F)
         line_g = gather_line(part_g, F)
         line_u = gather_line(part_u, F)
-        line_d = gather_line(part_d, F)
 
         gains = mix(extra_all[:2], 1)
         gain_first, gain_second = gains[0:1], gains[1:2]
@@ -548,8 +554,9 @@
         wa2, side_2 = gather_side(line_2, F, side_1)
         proj_2 = dot(after(normed_one, mixed, line_b, cot_near, cot_far), wa2)
         mixed, x_2, u_2, o_2 = mixer_fwd(proj_2, proj_1, pos, taps[1], gain_out, prm, dims, 1, mixed)
+        wd, line_d, got_d = gather_side_first(part_d, F, side_2)
         wb, side_b = gather_side(line_b, F, side_2)
-        mixed = after(mixed, line_g)
+        mixed = after(mixed, line_g, got_d)
         wg, side_g = gather_side(line_g, F, side_b)
         own32 = own.astype(f32)
         mid = tok // 2
@@ -558,12 +565,13 @@
         r2 = rms(middle)
         n2 = middle * r2
         normed_own = (n2 * gain_second).astype(bf16)
-        wu, side_u = gather_side(line_u, F, side_g)
-        two = join_tokens(after(normed_own, line_u), R)[:2]
-        wd, side_d = gather_side(line_d, F, side_u)
+        side_u = xor_send(after(line_u, side_g), "fsdp", F, 1)
+        two = join_tokens(after(normed_own, line_u, side_g), R)[:2]
         gates, ups, acts, sigs, hiddens = [], [], [], [], []
-        for normed in two:
+        for normed in (two[0], after(two[1], line_d)):
             gates.append(dot(normed, wg))
+            if not ups:
+                wu = jnp.concatenate([line_u, after(side_u, gates[0])], axis=0)
             ups.append(dot(normed, wu))
             sigs.append(jax.nn.sigmoid(gates[-1]))
             acts.append(gates[-1] * sigs[-1])
@@ -585,7 +593,8 @@
             dhidden = dot(after((cot_near, cot_far)[t], *needs), wd)
             dgates[t] = (dhidden * ups[t] * (sigs[t] * (1.0 + gates[t] * (1.0 - sigs[t])))).astype(bf16)
             dups[t] = (dhidden * acts[t]).astype(bf16)
-            return dot(dgates[t], wg, NT) + dot(dups[t], wu, NT)
+            ready = dgates[t] if t else after(dgates[t], g_down.got)
+            return dot(ready, wg, NT) + dot(dups[t], wu, NT)
 
         dnormed_two, far_two = sum_tokens(lambda: back_two(1, g_down.sent), lambda part: keep("two", back_two(0, part)), R)
         g_down.side(kept["two"])
@@ -602,7 +611,7 @@
         g_gate.side(g_up.sent)
         dp_1, dba_1, dt_1, dg_1, dr_1 = mixer_bwd(*args_1, after(dm_near, g_gate.low), dims, 0, 0, dba)
         t_down = g_down.total(R)
-        g_out = Summed(jnp.concatenate(dlow, axis=0), after(mixed, dba_1), F, g_up.got)
+        g_out = Summed(jnp.concatenate(dlow, axis=0), after(mixed, dba_1), F)
         dm_far = dot(after(dlow[1], dba_1), wb)
         dp_2, dba, et_2, eg_2, er_2 = mixer_bwd(*args_2, after(dm_far, g_out.sent), dims, 1, 1, None, [dp_2, dba])
         g_up.side(dba)
@@ -610,21 +619,25 @@
         t_gate = g_gate.total(R)
         dp_1, dba_1, et_1, eg_1, er_1 = mixer_bwd(
             *args_1, after(dm_far, g_2.sent, t_down), dims, 0, 1, dba, [dp_1, dba_1])
-        g_1 = Summed(normed_one, dp_1, F, g_2.got)
+        g_out.side(dp_1)
+        g_1 = Summed(normed_one, after(dp_1, g_out.low), F)
         t_up = g_up.total(R)
-        g_out.side(g_1.sent)
-        g_2.side(g_out.low)
 
         def back_one(lo, hi, *needs):
             return dot(after(dp_1, *needs)[lo:hi], wa1, NT) + dot(after(dp_2, *needs)[lo:hi], wa2, NT)
 
-        dnormed_one, far_one = sum_tokens(
-            lambda: back_one(mid, tok, g_out.low, t_gate), lambda part: keep("one", back_one(0, mid, part, g_2.low)), R)
-        added, unused = sum_tokens(
-            lambda: dot(after(hiddens[1], kept["one"], t_up), wd, NT), lambda part: dot(after(hiddens[0], part), wd, NT), R)
+        g_2.side(g_1.sent)
+
+        def near_one(part):
+            g_1.side(part)
+            kept["out"], unused = sum_tokens(
+                lambda: dot(after(hiddens[1], g_1.low), wd, NT), lambda held: keep("last", dot(after(hiddens[0], held), wd, NT)), R)
+            return back_one(0, mid, kept["last"], t_out)
+
+        t_out = g_out.total(R)
+        dnormed_one, far_one = sum_tokens(lambda: back_one(mid, tok, g_2.low, t_gate, t_up), near_one, R)
+        added = kept["out"]
         layer_out = (middle + added).astype(bf16)
-        g_1.side(kept["one"])
-        t_out = g_out.total(R)
         dprm = dr_1 + dr_2 + er_1 + er_2
         dgain_out = dg_1 + dg_2 + eg_1 + eg_2
         dtaps = [dt_1 + et_1, dt_2 + et_2]

time: 1290 us -> 1310 us (1.016)
  waiting for transfers between devices: 294 us -> 360 us
  blocking collectives: 34.6 us -> 0 us
    ppermute x39, waiting for transfers between devices: 217 us -> 297 us  [xor_send(): return lax.ppermute(value, axis, [(i, i ^ step) for i in range(size)])]
    all_to_all x6, waiting for transfers between devices: 58.8 us -> 19.6 us  [total(): lax.all_to_all(self.sum.reshape(ranks, -1, self.sum.shape[1]), 'rep', 0, 0)]
    all_to_all x1 -> x0, blocking collectives: 34.6 us -> none  [spread(): lax.all_to_all(packed.transpose(1, 0, 2), 'rep', 0, 0)]
    all_to_all x1 -> x2, waiting for transfers between devices: 1.38 us -> 28.5 us  [spread(): lax.all_to_all(packed.transpose(1, 0, 2), 'rep', 0, 0)]
    unnamed x265 -> x294, local copies, waits for them, and re-layouts: 107 us -> 90.5 us
  transfers between devices with their start and end apart: 60 -> 61, of which waited for: 17 -> 21; matrix products, arithmetic and copies ran while one was open for 46% -> 41% of each run, Pallas kernels for 14% -> 14%
where the time goes in v4:
time: 1310 us; the launch traced here: 1300 us
  matrix products  366 us (28%)
  waiting for transfers between devices  360 us (27%)
  local copies, waits for them, and re-layouts  202 us (15%)
  Pallas kernels  180 us (14%)
  other arithmetic  110 us (8%)
  starting transfers between devices  71.3 us (5%)
  between operations  16.3 us (1%)
    dot_general x34, matrix products, dot(): lax.dot_general(left, right, dims, preferred_element_type=f32).astype(out)  366 us
    ppermute x39, waiting for transfers between devices, xor_send(): return lax.ppermute(value, axis, [(i, i ^ step) for i in range(size)])  297 us
    pallas_call x4, Pallas kernels, mixer_bwd(): pl.pallas_call(functools.partial(bwd_kernel, dims, half, before is not No...  111 us
    unnamed x294, local copies, waits for them, and re-layouts  90.5 us
    pallas_call x2, Pallas kernels, mixer_fwd(): pl.pallas_call(functools.partial(fwd_kernel, dims, half), grid=(ns // PAI...  68.6 us
    all_to_all x2, waiting for transfers between devices, spread(): lax.all_to_all(packed.transpose(1, 0, 2), 'rep', 0, 0)  28.5 us
    ppermute x39, starting transfers between devices, xor_send(): return lax.ppermute(value, axis, [(i, i ^ step) for i in range(size)])  28 us
  transfers between devices with their start and end apart: 61, of which 21 were waited for; matrix products, arithmetic and copies ran while one was open for 41% of the time, Pallas kernels for 14%

profile of v4, /device:TPU:0, one launch (start us, length us, event | category | flops | bytes accessed | tf_op | source)
XLA Modules:
  0.0 1304.8 jit_solution(7151868962563626277)
XLA Ops:
  69.7 32.3 %collective-permute-done.5 = s32[512,1]{0,1:T(1,128)S(1)} collective-permute-done((s32[512,1]{0,1:T(1,128)S(1)}, s32[512,1]{0,1:T(1,128)S(1)}, u32[]{:S(2)}, u32[]{:S(2)}) %collective-permute-start.5) | collective-permute-done | bytes 2080 | tf_op jit(solution)/shard_map/ppermute | solution.py:351
  144.9 27.1 %all-to-all-done.2 = bf16[4,64,5248]{2,1,0:T(8,128)(2,1)} async-done(((bf16[4,64,5248]{2,1,0:T(8,128)(2,1)}), bf16[4,64,5248]{2,1,0:T(8,128)(2,1)}, u32[]{:S(2)}, u32[]{:S(2)}) %all-to-all-start.2) | async-done | bytes 2687008 | tf_op jit(solution)/shard_map/all_to_all | solution.py:499
  184.5 20.0 %collective-permute-done.3 = bf16[1024,1664]{1,0:T(8,128)(2,1)} collective-permute-done((bf16[1024,1664]{1,0:T(8,128)(2,1)}, bf16[1024,1664]{1,0:T(8,128)(2,1)}, u32[]{:S(2)}, u32[]{:S(2)}) %collective-permute-start.3) | collective-permute-done | bytes 3407904 | tf_op jit(solution)/shard_map/ppermute | solution.py:351
  231.8 19.7 %collective-permute-done.8 = bf16[512,2048]{1,0:T(8,128)(2,1)} collective-permute-done((bf16[512,2048]{1,0:T(8,128)(2,1)}, bf16[512,2048]{1,0:T(8,128)(2,1)}, u32[]{:S(2)}, u32[]{:S(2)}) %collective-permute-start.8) | collective-permute-done | bytes 2097184 | tf_op jit(solution)/shard_map/ppermute | solution.py:351
  251.5 21.2 %fusion.86.refs_0_.refs_1_.refs_2_.refs_3_.refs_4_ = f32[2048,1664]{1,0:T(8,128)} fusion(bf16[2048,2048]{1,0:T(8,128)(2,1)} %fusion.2, bf16[2048,1664]{1,0:T(8,128)(2,1)} %constant_dynamic-update-slice_fusion.13), kind=kOutput, calls=%fused_computation.284 | convolution fusion | flops 13958643712 | bytes 28835840 | tf_op jit(solution)/shard_map/dot_general | solution.py:379
  276.8 34.5 %shard_map.356 = (bf16[2048,1024]{1,0:T(8,128)(2,1)S(1)}, f32[16,256,256]{2,1,0:T(8,128)}, f32[2048,512]{1,0:T(8,128)}, f32[2048,512]{1,0:T(8,128)}) custom-call(f32[2048,1664]{1,0:T(8,128)} %fusion.86.refs_0_.refs_1_.refs_2_.refs_3_.refs_4_, f32[2048,1664]{1,0:T(8,128)} %fusion.86.refs_0_.refs_1_.refs_2_.refs_3_.refs_4_, ...), custom_call_target="tpu_custom_call" | custom-call | flops 4400000000 | bytes 4000000 | tf_op jit(solution)/shard_map/pallas_call | solution.py:281
  335.8 15.8 %fusion.87.refs_0_.refs_1_.refs_2_.refs_3_ = f32[2048,1536]{1,0:T(8,128)} fusion(bf16[2048,2048]{1,0:T(8,128)(2,1)S(1)} %bitcast.183, bf16[2048,1536]{1,0:T(8,128)(2,1)S(1)} %constant_dynamic-update-slice_fusion.19), kind=kOutput, calls=%fused_computation.285 | convolution fusion | flops 12884901888 | bytes 27262976 | tf_op jit(solution)/shard_map/dot_general | solution.py:379
  351.6 34.0 %shard_map.357 = (bf16[2048,1024]{1,0:T(8,128)(2,1)S(1)}, f32[16,256,256]{2,1,0:T(8,128)}, f32[2048,512]{1,0:T(8,128)}, f32[2048,512]{1,0:T(8,128)}) custom-call(f32[2048,1536]{1,0:T(8,128)} %fusion.87.refs_0_.refs_1_.refs_2_.refs_3_, f32[2048,1536]{1,0:T(8,128)} %fusion.87.refs_0_.refs_1_.refs_2_.refs_3_, ...), custom_call_target="tpu_custom_call", output_to_operand_aliasing={{0}: (9, {})} | custom-call | flops 4400000000 | bytes 4000000 | tf_op jit(solution)/shard_map/pallas_call | solution.py:281
  424.6 34.4 %collective-permute-done.15 = bf16[512,2048]{1,0:T(8,128)(2,1)} collective-permute-done((bf16[512,2048]{1,0:T(8,128)(2,1)}, bf16[512,2048]{1,0:T(8,128)(2,1)}, u32[]{:S(2)}, u32[]{:S(2)}) %collective-permute-start.15) | collective-permute-done | bytes 2097184 | tf_op jit(solution)/shard_map/ppermute | solution.py:351
  466.3 20.8 %collective-permute-done.16 = bf16[1024,1408]{1,0:T(8,128)(2,1)} collective-permute-done((bf16[1024,1408]{1,0:T(8,128)(2,1)}, bf16[1024,1408]{1,0:T(8,128)(2,1)}, u32[]{:S(2)}, u32[]{:S(2)}) %collective-permute-start.16) | collective-permute-done | bytes 2883616 | tf_op jit(solution)/shard_map/ppermute | solution.py:351
  504.4 50.0 %collective-permute-done.18 = bf16[1024,1408]{1,0:T(8,128)(2,1)S(1)} collective-permute-done((bf16[1024,1408]{1,0:T(8,128)(2,1)S(1)}, bf16[1024,1408]{1,0:T(8,128)(2,1)S(1)}, u32[]{:S(2)}, u32[]{:S(2)}) %collective-permute-start.18) | collective-permute-done | bytes 2883616 | tf_op jit(solution)/shard_map/ppermute | solution.py:351
  608.6 12.6 multiply_convert_fusion.3
  630.2 12.8 convolution_add_fusion.3
  692.3 22.9 %collective-permute-done.22 = bf16[1024,1408]{1,0:T(8,128)(2,1)} collective-permute-done((bf16[1024,1408]{1,0:T(8,128)(2,1)}, bf16[1024,1408]{1,0:T(8,128)(2,1)}, u32[]{:S(2)}, u32[]{:S(2)}) %collective-permute-start.22) | collective-permute-done | bytes 2883616 | tf_op jit(solution)/shard_map/ppermute | solution.py:351
  777.1 27.4 %shard_map.358 = (bf16[2048,1536]{1,0:T(8,128)(2,1)}, f32[2048,128]{1,0:T(8,128)}, f32[4,1024]{1,0:T(4,128)}, f32[1,256]{1,0:T(1,128)}, f32[8,128]{1,0:T(8,128)}) custom-call(f32[2048,1536]{1,0:T(8,128)} %fusion.87.refs_0_.refs_1_.refs_2_.refs_3_, f32[2048,1536]{1,0:T(8,128)} %fusion.87.refs_0_.refs_1_.refs_2_.refs_3_, ...), custom_call_target="tpu_custom_call" | custom-call | flops 28600000512 | bytes 26000000 | tf_op jit(solution)/shard_map/pallas_call | solution.py:326
  815.8 13.4 %collective-permute-done.28 = bf16[1024,1408]{1,0:T(8,128)(2,1)S(1)} collective-permute-done((bf16[1024,1408]{1,0:T(8,128)(2,1)}, bf16[1024,1408]{1,0:T(8,128)(2,1)S(1)}, u32[]{:S(2)}, u32[]{:S(2)}) %collective-permute-start.28) | collective-permute-done | bytes 2883616 | tf_op jit(solution)/shard_map/ppermute | solution.py:351
  842.3 28.6 %shard_map.359 = (bf16[2048,1664]{1,0:T(8,128)(2,1)}, f32[2048,128]{1,0:T(8,128)}, f32[4,1024]{1,0:T(4,128)}, f32[1,256]{1,0:T(1,128)}, f32[8,128]{1,0:T(8,128)}) custom-call(f32[2048,1664]{1,0:T(8,128)} %fusion.86.refs_0_.refs_1_.refs_2_.refs_3_.refs_4_, f32[2048,1664]{1,0:T(8,128)} %fusion.86.refs_0_.refs_1_.refs_2_.refs_3_.refs_4_, ...), custom_call_target="tpu_custom_call" | custom-call | flops 28600000512 | bytes 26000000 | tf_op jit(solution)/shard_map/pallas_call | solution.py:326
  894.5 27.3 %shard_map.360 = (bf16[2048,1536]{1,0:T(8,128)(2,1)}, f32[2048,128]{1,0:T(8,128)}, f32[4,1024]{1,0:T(4,128)}, f32[1,256]{1,0:T(1,128)}, f32[8,128]{1,0:T(8,128)}) custom-call(f32[2048,1536]{1,0:T(8,128)} %fusion.87.refs_0_.refs_1_.refs_2_.refs_3_, ...), custom_call_target="tpu_custom_call", output_to_operand_aliasing={{0}: (13, {}), {1}: (14, {})} | custom-call | flops 28600000512 | bytes 26000000 | tf_op jit(solution)/shard_map/pallas_call | solution.py:326
  946.0 27.9 %shard_map.361 = (bf16[2048,1664]{1,0:T(8,128)(2,1)}, f32[2048,128]{1,0:T(8,128)}, f32[4,1024]{1,0:T(4,128)}, f32[1,256]{1,0:T(1,128)}, f32[8,128]{1,0:T(8,128)}) custom-call(f32[2048,1664]{1,0:T(8,128)} %fusion.86.refs_0_.refs_1_.refs_2_.refs_3_.refs_4_, ...), custom_call_target="tpu_custom_call", output_to_operand_aliasing={{0}: (14, {}), {1}: (15, {})} | custom-call | flops 28600000512 | bytes 26000000 | tf_op jit(solution)/shard_map/pallas_call | solution.py:326
  985.9 12.9 convolution_convert_fusion.3
  1002.8 16.0 %collective-permute-done.31 = bf16[1024,1536]{1,0:T(8,128)(2,1)} collective-permute-done((bf16[1024,1536]{1,0:T(8,128)(2,1)}, bf16[1024,1536]{1,0:T(8,128)(2,1)}, u32[]{:S(2)}, u32[]{:S(2)}) %collective-permute-start.31) | collective-permute-done | bytes 3145760 | tf_op jit(solution)/shard_map/ppermute | solution.py:351
  1069.7 20.8 %collective-permute-done.33 = bf16[1024,1664]{1,0:T(8,128)(2,1)} collective-permute-done((bf16[1024,1664]{1,0:T(8,128)(2,1)}, bf16[1024,1664]{1,0:T(8,128)(2,1)}, u32[]{:S(2)}, u32[]{:S(2)}) %collective-permute-start.33) | collective-permute-done | bytes 3407904 | tf_op jit(solution)/shard_map/ppermute | solution.py:351
  1090.5 13.6 %add_convert_fusion = bf16[1024,1664]{1,0:T(8,128)(2,1)} fusion(bf16[1024,1664]{1,0:T(8,128)(2,1)} %collective-permute-done.33, bf16[2048,1664]{1,0:T(8,128)(2,1)} %get-tuple-element.148, bf16[2048,2048]{1,0:T(8,128)(2,1)} %fusion.2), kind=kOutput, calls=%fused_computation.7 | convolution fusion | flops 6984433664 | bytes 17825792 | tf_op jit(solution)/shard_map/dot_general | solution.py:379
  1213.5 37.3 %collective-permute-done.36 = bf16[512,2048]{1,0:T(8,128)(2,1)} collective-permute-done((bf16[512,2048]{1,0:T(8,128)(2,1)}, bf16[512,2048]{1,0:T(8,128)(2,1)}, u32[]{:S(2)}, u32[]{:S(2)}) %collective-permute-start.36) | collective-permute-done | bytes 2097184 | tf_op jit(solution)/shard_map/ppermute | solution.py:351
  (624 shorter events, 705.0 us)
Async XLA Ops:
  20.9 105.3 %all-gather.9.cloned.1.call-start = ((), (), s32[]{:S(2)}) async-start(), calls=%async_computation.17 | async-start | bytes 4259840 | tf_op jit(solution)/shard_map/all_gather | solution.py:363
  52.6 164.8 %all-gather.7.cloned.1.call-start = ((), (), s32[]{:S(2)}) async-start(), calls=%async_computation.16 | async-start | bytes 3932160 | tf_op jit(solution)/shard_map/all_gather | solution.py:363
  65.0 109.0 %collective-permute-start = (bf16[512,2048]{1,0:T(8,128)(2,1)}, bf16[512,2048]{1,0:T(8,128)(2,1)}, u32[]{:S(2)}, u32[]{:S(2)}) collective-permute-start(bf16[512,2048]{1,0:T(8,128)(2,1)} %pad_maximum_fusion.7), channel_id=1, source_target_pairs={{0,1},{1,0},{2,3},{3,2},{4,5},{5,4},{6,7},{7,6},{8,9},{9,8},{10,11... | collective-permute-start | bytes 6291464 | tf_op jit(solution)/shard_map/ppermute | solution.py:351
  128.5 76.0 %collective-permute-start.3 = (bf16[1024,1664]{1,0:T(8,128)(2,1)}, bf16[1024,1664]{1,0:T(8,128)(2,1)}, u32[]{:S(2)}, u32[]{:S(2)}) collective-permute-start(bf16[1024,1664]{1,0:T(8,128)(2,1)} %all-gather.9.cloned.1.call-done), channel_id=1, source_target_pairs={{0,4},{4,0},{8,12},{12,8},{16,20},{20,16},{24,28},{28,24},{1,5},{5... | collective-permute-start | bytes 10223624 | tf_op jit(solution)/shard_map/ppermute | solution.py:351
  140.0 173.3 %all-gather.11.cloned.1.call-start = ((), (), s32[]{:S(2)}) async-start(), calls=%async_computation.18 | async-start | bytes 2621440 | tf_op jit(solution)/shard_map/all_gather | solution.py:363
  173.9 213.6 %all-gather.13.cloned.1.call-start = ((), (), s32[]{:S(2)}) async-start(), calls=%async_computation.19 | async-start | bytes 3604480 | tf_op jit(solution)/shard_map/all_gather | solution.py:363
  226.1 240.2 %all-gather.15.cloned.1.call-start = ((), (), s32[]{:S(2)}) async-start(), calls=%async_computation.20 | async-start | bytes 3604480 | tf_op jit(solution)/shard_map/all_gather | solution.py:363
  226.3 90.3 %collective-permute-start.7 = (bf16[512,2048]{1,0:T(8,128)(2,1)}, bf16[512,2048]{1,0:T(8,128)(2,1)}, u32[]{:S(2)}, u32[]{:S(2)}) collective-permute-start(bf16[512,2048]{1,0:T(8,128)(2,1)} %pad_maximum_fusion.8), channel_id=1, source_target_pairs={{0,1},{1,0},{2,3},{3,2},{4,5},{5,4},{6,7},{7,6},{8,9},{9,8},{10,11... | collective-permute-start | bytes 6291464 | tf_op jit(solution)/shard_map/ppermute | solution.py:351
  226.4 98.1 %collective-permute-start.10 = (bf16[1024,1536]{1,0:T(8,128)(2,1)}, bf16[1024,1536]{1,0:T(8,128)(2,1)}, u32[]{:S(2)}, u32[]{:S(2)}) collective-permute-start(bf16[1024,1536]{1,0:T(8,128)(2,1)} %all-gather.7.cloned.1.call-done), channel_id=1, source_target_pairs={{0,4},{4,0},{8,12},{12,8},{16,20},{20,16},{24,28},{28,24},{1,5},{5... | collective-permute-start | bytes 9437192 | tf_op jit(solution)/shard_map/ppermute | solution.py:351
  251.5 77.3 %collective-permute-start.9 = (bf16[512,2048]{1,0:T(8,128)(2,1)}, bf16[512,2048]{1,0:T(8,128)(2,1)}, u32[]{:S(2)}, u32[]{:S(2)}) collective-permute-start(bf16[512,2048]{1,0:T(8,128)(2,1)} %collective-permute-done.8), channel_id=1, source_target_pairs={{0,1},{1,0},{2,3},{3,2},{4,5},{5,4},{6,7},{7,6},{8,9},{9,8},{10,11... | collective-permute-start | bytes 6291464 | tf_op jit(solution)/shard_map/ppermute | solution.py:351
  401.9 167.3 %all-gather.17.cloned.1.call-start = ((), (), s32[]{:S(2)}) async-start(), calls=%async_computation.21 | async-start | bytes 7208960 | tf_op jit(solution)/shard_map/all_gather | solution.py:363
  424.6 446.3 %reduce-scatter.7.cloned.1.call-start = ((), (), s32[]{:S(2)}) async-start(), calls=%async_computation.22 | async-start | bytes 3604480 | tf_op jit(solution)/shard_map/reduce_scatter | solution.py:393
  661.1 90.5 %collective-permute-start.24 = (bf16[512,2048]{1,0:T(8,128)(2,1)}, bf16[512,2048]{1,0:T(8,128)(2,1)}, u32[]{:S(2)}, u32[]{:S(2)}) collective-permute-start(bf16[512,2048]{1,0:T(8,128)(2,1)} %fusion.26), channel_id=1, source_target_pairs={{0,2},{1,3},{2,0},{3,1},{4,6},{5,7},{6,4},{7,5},{8,10},{9,11},{10,... | collective-permute-start | bytes 6291464 | tf_op jit(solution)/shard_map/ppermute | solution.py:351
  764.1 218.3 %reduce-scatter.9.cloned.1.call-start = ((), (), s32[]{:S(2)}) async-start(), calls=%async_computation.23 | async-start | bytes 3604480 | tf_op jit(solution)/shard_map/reduce_scatter | solution.py:393
  765.7 76.5 %collective-permute-start.25 = (bf16[512,2048]{1,0:T(8,128)(2,1)S(1)}, bf16[512,2048]{1,0:T(8,128)(2,1)}, u32[]{:S(2)}, u32[]{:S(2)}) collective-permute-start(bf16[512,2048]{1,0:T(8,128)(2,1)S(1)} %get-tuple-element.166), channel_id=1, source_target_pairs={{0,2},{1,3},{2,0},{3,1},{4,6},{5,7},{6,4},{7,5},{8,10},{9,11},{10,... | collective-permute-start | bytes 6291464 | tf_op jit(solution)/shard_map/ppermute | solution.py:351
  840.7 81.1 %collective-permute-start.29 = (bf16[1024,1408]{1,0:T(8,128)(2,1)}, bf16[1024,1408]{1,0:T(8,128)(2,1)}, u32[]{:S(2)}, u32[]{:S(2)}) collective-permute-start(bf16[1024,1408]{1,0:T(8,128)(2,1)} %convolution_convert_fusion.1), channel_id=1, source_target_pairs={{0,4},{4,0},{8,12},{12,8},{16,20},{20,16},{24,28},{28,24},{1,5},{5... | collective-permute-start | bytes 8650760 | tf_op jit(solution)/shard_map/ppermute | solution.py:351
  870.9 75.1 %all-to-all-start.3 = ((bf16[4,64,1408]{2,1,0:T(8,128)(2,1)}), bf16[4,64,1408]{2,1,0:T(8,128)(2,1)S(1)}, u32[]{:S(2)}, u32[]{:S(2)}) async-start(bf16[4,64,1408]{2,1,0:T(8,128)(2,1)} %bitcast.207), calls=%async_computation.4 | async-start | bytes 1441792 | tf_op jit(solution)/shard_map/all_to_all | solution.py:396
  874.4 124.8 %reduce-scatter.11.cloned.1.call-start = ((), (), s32[]{:S(2)}) async-start(), calls=%async_computation.24 | async-start | bytes 3604480 | tf_op jit(solution)/shard_map/reduce_scatter | solution.py:393
  894.1 79.8 %collective-permute-start.30 = (bf16[1024,1024]{1,0:T(8,128)(2,1)}, bf16[1024,1024]{1,0:T(8,128)(2,1)}, u32[]{:S(2)}, u32[]{:S(2)}) collective-permute-start(bf16[1024,1024]{1,0:T(8,128)(2,1)} %fusion.64), channel_id=1, source_target_pairs={{0,4},{4,0},{8,12},{12,8},{16,20},{20,16},{24,28},{28,24},{1,5},{5... | collective-permute-start | bytes 6291464 | tf_op jit(solution)/shard_map/ppermute | solution.py:351
  998.9 91.6 %collective-permute-start.33 = (bf16[1024,1664]{1,0:T(8,128)(2,1)}, bf16[1024,1664]{1,0:T(8,128)(2,1)}, u32[]{:S(2)}, u32[]{:S(2)}) collective-permute-start(bf16[1024,1664]{1,0:T(8,128)(2,1)} %convolution_convert_fusion.3), channel_id=1, source_target_pairs={{0,4},{4,0},{8,12},{12,8},{16,20},{20,16},{24,28},{28,24},{1,5},{5... | collective-permute-start | bytes 10223624 | tf_op jit(solution)/shard_map/ppermute | solution.py:351
  1002.7 120.3 %reduce-scatter.13.cloned.1.call-start = ((), (), s32[]{:S(2)}) async-start(), calls=%async_computation.25 | async-start | bytes 2621440 | tf_op jit(solution)/shard_map/reduce_scatter | solution.py:393
  1060.4 121.6 %reduce-scatter.17.cloned.1.call-start = ((), (), s32[]{:S(2)}) async-start(), calls=%async_computation.27 | async-start | bytes 3932160 | tf_op jit(solution)/shard_map/reduce_scatter | solution.py:393
  1127.0 75.1 %collective-permute-start.38 = (bf16[512,2048]{1,0:T(8,128)(2,1)}, bf16[512,2048]{1,0:T(8,128)(2,1)}, u32[]{:S(2)}, u32[]{:S(2)}) collective-permute-start(bf16[512,2048]{1,0:T(8,128)(2,1)} %fusion.19), channel_id=1, source_target_pairs={{0,2},{1,3},{2,0},{3,1},{4,6},{5,7},{6,4},{7,5},{8,10},{9,11},{10,... | collective-permute-start | bytes 6291464 | tf_op jit(solution)/shard_map/ppermute | solution.py:351
  1185.5 86.0 %reduce-scatter.15.cloned.1.call-start = ((), (), s32[]{:S(2)}) async-start(), calls=%async_computation.26 | async-start | bytes 4259840 | tf_op jit(solution)/shard_map/reduce_scatter | solution.py:393
  (146 other events, 3924.8 us)
Sparse Core Ops, SparseCore 0:
  44.7 69.8 all-gather.8
  116.1 62.1 all-gather.6
  180.4 44.5 all-gather.10
  227.0 57.9 all-gather.12
  402.0 59.7 all-gather.14
  463.7 105.3 all-gather.16
  764.2 54.5 reduce-scatter.6
  840.8 54.4 reduce-scatter.8
  933.1 54.9 reduce-scatter.10
  1060.5 42.3 reduce-scatter.12
  1123.1 58.7 reduce-scatter.16
  1188.4 67.4 reduce-scatter.14

commit v5 on v4

--- a/solution.py
+++ b/solution.py
@@ -387,10 +387,11 @@
         self.sent = dot(left[:, self.half :], right, TN, bf16)
         self.got = xor_send(after(self.sent, *needs) if needs else self.sent, "fsdp", size, 1)
 
-    def side(self, *needs):
+    def side(self, *needs, before=()):
         keep = dot(self.left[:, : self.half], after(self.right, *needs) if needs else self.right, TN)
         self.low = (keep + self.got.astype(f32)).astype(bf16)
-        self.sum = lax.psum_scatter(self.low, "fsdp", scatter_dimension=0, tiled=True, axis_index_groups=lines(self.size))
+        ready = after(self.low, *before) if before else self.low
+        self.sum = lax.psum_scatter(ready, "fsdp", scatter_dimension=0, tiled=True, axis_index_groups=lines(self.size))
 
     def total(self, ranks):
         return lax.all_to_all(self.sum.reshape(ranks, -1, self.sum.shape[1]), "rep", 0, 0)
@@ -522,15 +523,13 @@
         every = jnp.concatenate([every_near, every_far], axis=0)
         ids_all = jnp.concatenate(join_tokens(segments[:, None], R)[:2], axis=0).reshape(ns, SEQ)
         part_r = spread(quarter([after(w_out.T, extra_all, every_got, line_1), w_ffgate, w_ffup, w_down.T]))
-        part_b, part_g, part_u, part_d = (
-            part_r[:, :wv], part_r[:, wv : wv + ffq], part_r[:, wv + ffq : wv + 2 * ffq], part_r[:, wv + 2 * ffq :])
+        part_b, part_gu, part_d = part_r[:, :wv], part_r[:, wv : wv + 2 * ffq], part_r[:, wv + 2 * ffq :]
         line_2 = gather_line(after(part_2, extra_all), F)
         wa1, side_1 = gather_side(line_1, F)
         cot = mix(cotangent, 1)
         cot_near, cot_far, unused = join_tokens(after(cot, side_1), R)
         line_b = gather_line(part_b, F)
-        line_g = gather_line(part_g, F)
-        line_u = gather_line(part_u, F)
+        line_gu = gather_line(part_gu, F)
 
         gains = mix(extra_all[:2], 1)
         gain_first, gain_second = gains[0:1], gains[1:2]
@@ -552,12 +551,13 @@
         proj_1 = dot(after(normed_one, line_2, part_r), wa1)
         mixed, x_1, u_1, o_1 = mixer_fwd(proj_1, proj_1, pos, taps[0], gain_out, prm, dims, 0)
         wa2, side_2 = gather_side(line_2, F, side_1)
-        proj_2 = dot(after(normed_one, mixed, line_b, cot_near, cot_far), wa2)
+        proj_2 = dot(after(normed_one, mixed, line_b), wa2)
         mixed, x_2, u_2, o_2 = mixer_fwd(proj_2, proj_1, pos, taps[1], gain_out, prm, dims, 1, mixed)
         wd, line_d, got_d = gather_side_first(part_d, F, side_2)
         wb, side_b = gather_side(line_b, F, side_2)
-        mixed = after(mixed, line_g, got_d)
-        wg, side_g = gather_side(line_g, F, side_b)
+        mixed = after(mixed, line_gu, got_d, cot_near, cot_far)
+        side_gu = xor_send(after(line_gu, side_b), "fsdp", F, 1)
+        wg, wu = (jnp.concatenate([line_gu[:, at : at + ffq], side_gu[:, at : at + ffq]], axis=0) for at in (0, ffq))
         own32 = own.astype(f32)
         mid = tok // 2
         added, unused = sum_tokens(lambda: dot(mixed[mid:], wb, NT), lambda part: dot(after(mixed, part)[:mid], wb, NT), R)
@@ -565,13 +565,10 @@
         r2 = rms(middle)
         n2 = middle * r2
         normed_own = (n2 * gain_second).astype(bf16)
-        side_u = xor_send(after(line_u, side_g), "fsdp", F, 1)
-        two = join_tokens(after(normed_own, line_u, side_g), R)[:2]
+        two = join_tokens(normed_own, R)[:2]
         gates, ups, acts, sigs, hiddens = [], [], [], [], []
         for normed in (two[0], after(two[1], line_d)):
             gates.append(dot(normed, wg))
-            if not ups:
-                wu = jnp.concatenate([line_u, after(side_u, gates[0])], axis=0)
             ups.append(dot(normed, wu))
             sigs.append(jax.nn.sigmoid(gates[-1]))
             acts.append(gates[-1] * sigs[-1])
@@ -593,8 +590,7 @@
             dhidden = dot(after((cot_near, cot_far)[t], *needs), wd)
             dgates[t] = (dhidden * ups[t] * (sigs[t] * (1.0 + gates[t] * (1.0 - sigs[t])))).astype(bf16)
             dups[t] = (dhidden * acts[t]).astype(bf16)
-            ready = dgates[t] if t else after(dgates[t], g_down.got)
-            return dot(ready, wg, NT) + dot(dups[t], wu, NT)
+            return dot(dgates[t], wg, NT) + dot(dups[t], wu, NT)
 
         dnormed_two, far_two = sum_tokens(lambda: back_two(1, g_down.sent), lambda part: keep("two", back_two(0, part)), R)
         g_down.side(kept["two"])
@@ -609,13 +605,13 @@
         dp_2, dba, dt_2, dg_2, dr_2 = mixer_bwd(*args_2, dm_near, dims, 1, 0)
         g_up = Summed(normed_two, after(jnp.concatenate(dups, axis=0), dba), F, g_gate.got)
         g_gate.side(g_up.sent)
-        dp_1, dba_1, dt_1, dg_1, dr_1 = mixer_bwd(*args_1, after(dm_near, g_gate.low), dims, 0, 0, dba)
+        dp_1, dba_1, dt_1, dg_1, dr_1 = mixer_bwd(*args_1, after(dm_near, g_gate.low, g_down.sum), dims, 0, 0, dba)
         t_down = g_down.total(R)
         g_out = Summed(jnp.concatenate(dlow, axis=0), after(mixed, dba_1), F)
         dm_far = dot(after(dlow[1], dba_1), wb)
         dp_2, dba, et_2, eg_2, er_2 = mixer_bwd(*args_2, after(dm_far, g_out.sent), dims, 1, 1, None, [dp_2, dba])
         g_up.side(dba)
-        g_2 = Summed(normed_one, after(dp_2, g_up.low), F)
+        g_2 = Summed(normed_one, after(dp_2, g_up.low, g_gate.sum), F)
         t_gate = g_gate.total(R)
         dp_1, dba_1, et_1, eg_1, er_1 = mixer_bwd(
             *args_1, after(dm_far, g_2.sent, t_down), dims, 0, 1, dba, [dp_1, dba_1])
@@ -626,16 +622,22 @@
         def back_one(lo, hi, *needs):
             return dot(after(dp_1, *needs)[lo:hi], wa1, NT) + dot(after(dp_2, *needs)[lo:hi], wa2, NT)
 
-        g_2.side(g_1.sent)
+        t_out = g_out.total(R)
 
         def near_one(part):
-            g_1.side(part)
-            kept["out"], unused = sum_tokens(
-                lambda: dot(after(hiddens[1], g_1.low), wd, NT), lambda held: keep("last", dot(after(hiddens[0], held), wd, NT)), R)
-            return back_one(0, mid, kept["last"], t_out)
-
-        t_out = g_out.total(R)
-        dnormed_one, far_one = sum_tokens(lambda: back_one(mid, tok, g_2.low, t_gate, t_up), near_one, R)
+            g_2.side(part, before=(g_out.sum,))
+
+            def far_out():
+                return keep("far", dot(after(hiddens[1], g_2.low, t_up), wd, NT))
+
+            def near_out(held):
+                g_1.side(kept["far"], held, before=(g_2.sum,))
+                return keep("last", dot(after(hiddens[0], g_1.low), wd, NT))
+
+            kept["out"], unused = sum_tokens(far_out, near_out, R)
+            return back_one(0, mid, kept["last"], t_out, g_2.sum)
+
+        dnormed_one, far_one = sum_tokens(lambda: back_one(mid, tok, g_1.sent, g_up.sum, t_gate), near_one, R)
         added = kept["out"]
         layer_out = (middle + added).astype(bf16)
         dprm = dr_1 + dr_2 + er_1 + er_2

time: 1310 us -> 1240 us (0.947)
  waiting for transfers between devices: 360 us -> 256 us
  local copies, waits for them, and re-layouts: 202 us -> 221 us
  matrix products: 366 us -> 382 us
    ppermute x39 -> x38, waiting for transfers between devices: 297 us -> 168 us  [xor_send(): return lax.ppermute(value, axis, [(i, i ^ step) for i in range(size)])]
    all_gather x6 -> x5, waiting for transfers between devices: 2.72 us -> 27.3 us  [gather_line(): lax.all_gather(rows, 'fsdp', axis=0, tiled=True, axis_index_groups=lines(...]
    dot_general x34, matrix products: 366 us -> 382 us  [dot(): lax.dot_general(left, right, dims, preferred_element_type=f32).astype(out)]
    ppermute x39 -> x38, starting transfers between devices: 28 us -> 20.7 us  [xor_send(): return lax.ppermute(value, axis, [(i, i ^ step) for i in range(size)])]
    unnamed x294 -> x271, local copies, waits for them, and re-layouts: 90.5 us -> 94.7 us
  transfers between devices with their start and end apart: 61 -> 59, of which waited for: 21 -> 20; matrix products, arithmetic and copies ran while one was open for 41% -> 47% of each run, Pallas kernels for 14% -> 15%
where the time goes in v5:
time: 1240 us
  matrix products  382 us (31%)
  waiting for transfers between devices  256 us (21%)
  local copies, waits for them, and re-layouts  221 us (18%)
  Pallas kernels  179 us (14%)
  other arithmetic  120 us (10%)
  starting transfers between devices  62.3 us (5%)
  between operations  15.8 us (1%)
    dot_general x34, matrix products, dot(): lax.dot_general(left, right, dims, preferred_element_type=f32).astype(out)  382 us
    ppermute x38, waiting for transfers between devices, xor_send(): return lax.ppermute(value, axis, [(i, i ^ step) for i in range(size)])  168 us
    pallas_call x4, Pallas kernels, mixer_bwd(): pl.pallas_call(functools.partial(bwd_kernel, dims, half, before is not No...  111 us
    unnamed x271, local copies, waits for them, and re-layouts  94.7 us
    pallas_call x2, Pallas kernels, mixer_fwd(): pl.pallas_call(functools.partial(fwd_kernel, dims, half), grid=(ns // PAI...  68.4 us
    all_gather x5, waiting for transfers between devices, gather_line(): lax.all_gather(rows, 'fsdp', axis=0, tiled=True, axis_index_groups=lines(...  27.3 us
    all_to_all x2, waiting for transfers between devices, spread(): lax.all_to_all(packed.transpose(1, 0, 2), 'rep', 0, 0)  25.8 us
  transfers between devices with their start and end apart: 59, of which 20 were waited for; matrix products, arithmetic and copies ran while one was open for 47% of the time, Pallas kernels for 15%

profile of v5, /device:TPU:0, one launch (start us, length us, event | category | flops | bytes accessed | tf_op | source)
XLA Modules:
  0.0 1236.2 jit_solution(5745777639379293047)
XLA Ops:
  80.4 32.2 %collective-permute-done.5 = s32[512,1]{0,1:T(1,128)S(1)} collective-permute-done((s32[512,1]{0,1:T(1,128)S(1)}, s32[512,1]{0,1:T(1,128)S(1)}, u32[]{:S(2)}, u32[]{:S(2)}) %collective-permute-start.5) | collective-permute-done | bytes 2080 | tf_op jit(solution)/shard_map/ppermute | solution.py:351
  153.6 24.4 %all-to-all-done.2 = bf16[4,64,5248]{2,1,0:T(8,128)(2,1)} async-done(((bf16[4,64,5248]{2,1,0:T(8,128)(2,1)}), bf16[4,64,5248]{2,1,0:T(8,128)(2,1)}, u32[]{:S(2)}, u32[]{:S(2)}) %all-to-all-start.2) | async-done | bytes 2687008 | tf_op jit(solution)/shard_map/all_to_all | solution.py:500
  213.2 14.0 %collective-permute-done.3 = bf16[1024,1664]{1,0:T(8,128)(2,1)} collective-permute-done((bf16[1024,1664]{1,0:T(8,128)(2,1)}, bf16[1024,1664]{1,0:T(8,128)(2,1)}, u32[]{:S(2)}, u32[]{:S(2)}) %collective-permute-start.3) | collective-permute-done | bytes 3407904 | tf_op jit(solution)/shard_map/ppermute | solution.py:351
  234.4 21.2 %fusion.95.refs_0_.refs_1_.refs_2_.refs_3_.refs_4_ = f32[2048,1664]{1,0:T(8,128)} fusion(bf16[2048,2048]{1,0:T(8,128)(2,1)} %fusion.2, bf16[2048,1664]{1,0:T(8,128)(2,1)} %constant_dynamic-update-slice_fusion.13), kind=kOutput, calls=%fused_computation.287 | convolution fusion | flops 13958643712 | bytes 28835840 | tf_op jit(solution)/shard_map/dot_general | solution.py:379
  258.1 34.3 %shard_map.356 = (bf16[2048,1024]{1,0:T(8,128)(2,1)S(1)}, f32[16,256,256]{2,1,0:T(8,128)}, f32[2048,512]{1,0:T(8,128)}, f32[2048,512]{1,0:T(8,128)}) custom-call(f32[2048,1664]{1,0:T(8,128)} %fusion.95.refs_0_.refs_1_.refs_2_.refs_3_.refs_4_, f32[2048,1664]{1,0:T(8,128)} %fusion.95.refs_0_.refs_1_.refs_2_.refs_3_.refs_4_, ...), custom_call_target="tpu_custom_call" | custom-call | flops 4400000000 | bytes 4000000 | tf_op jit(solution)/shard_map/pallas_call | solution.py:281
  313.1 15.8 %fusion.96.refs_0_.refs_1_.refs_2_.refs_3_ = f32[2048,1536]{1,0:T(8,128)} fusion(bf16[2048,2048]{1,0:T(8,128)(2,1)S(1)} %bitcast.173, bf16[2048,1536]{1,0:T(8,128)(2,1)S(1)} %constant_dynamic-update-slice_fusion.15), kind=kOutput, calls=%fused_computation.288 | convolution fusion | flops 12884901888 | bytes 27262976 | tf_op jit(solution)/shard_map/dot_general | solution.py:379
  328.9 34.1 %shard_map.357 = (bf16[2048,1024]{1,0:T(8,128)(2,1)S(1)}, f32[16,256,256]{2,1,0:T(8,128)}, f32[2048,512]{1,0:T(8,128)}, f32[2048,512]{1,0:T(8,128)}) custom-call(f32[2048,1536]{1,0:T(8,128)} %fusion.96.refs_0_.refs_1_.refs_2_.refs_3_, f32[2048,1536]{1,0:T(8,128)} %fusion.96.refs_0_.refs_1_.refs_2_.refs_3_, ...), custom_call_target="tpu_custom_call", output_to_operand_aliasing={{0}: (9, {})} | custom-call | flops 4400000000 | bytes 4000000 | tf_op jit(solution)/shard_map/pallas_call | solution.py:281
  398.7 40.4 %collective-permute-done.15 = bf16[512,2048]{1,0:T(8,128)(2,1)S(1)} collective-permute-done((bf16[512,2048]{1,0:T(8,128)(2,1)S(1)}, bf16[512,2048]{1,0:T(8,128)(2,1)S(1)}, u32[]{:S(2)}, u32[]{:S(2)}) %collective-permute-start.15) | collective-permute-done | bytes 2097184 | tf_op jit(solution)/shard_map/ppermute | solution.py:351
  449.9 27.3 %all-gather.14.cloned.1.call-done = bf16[2048,1408]{1,0:T(8,128)(2,1)} async-done(((bf16[512,1408]{1,0:T(8,128)(2,1)}), bf16[2048,1408]{1,0:T(8,128)(2,1)}) %all-gather.14.cloned.1.call-update) | async-done | bytes 5767184 | tf_op jit(solution)/shard_map/all_gather | solution.py:363
  480.3 33.3 %collective-permute-done.17 = bf16[1024,2816]{1,0:T(8,128)(2,1)} collective-permute-done((bf16[1024,2816]{1,0:T(8,128)(2,1)}, bf16[1024,2816]{1,0:T(8,128)(2,1)}, u32[]{:S(2)}, u32[]{:S(2)}) %collective-permute-start.17) | collective-permute-done | bytes 5767200 | tf_op jit(solution)/shard_map/ppermute | solution.py:351
  527.4 15.1 %multiply_convert_fusion.5 = (bf16[1024,1408]{1,0:T(8,128)(2,1)}, f32[1024,1408]{1,0:T(8,128)}) fusion(f32[1024,1408]{1,0:T(8,128)} %fusion.59, bf16[1024,1408]{1,0:T(8,128)(2,1)} %get-tuple-element.173, bf16[1024,1408]{1,0:T(8,128)(2,1)} %get-tuple-element.171, bf16[512,2048]{1,0:T(8,128)(2,1)} %collective-permute-done.16, ...), kind=kOutput, calls=%fused_computation.31 | convolution fusion | flops 5934153728 | bytes 24379392 | tf_op jit(solution)/shard_map/dot_general | solution.py:379
  554.4 12.3 multiply_convert_fusion.4
  577.6 13.9 %multiply_convert_fusion.3 = (bf16[1024,1408]{1,0:T(8,128)(2,1)}, bf16[1024,1408]{1,0:T(8,128)(2,1)S(1)}) fusion(f32[1024,1408]{1,0:T(8,128)} %fusion.79, f32[1024,1408]{1,0:T(8,128)} %get-tuple-element.234, bf16[1024,2048]{1,0:T(8,128)(2,1)} %get-tuple-element.108, bf16[2048,1408]{1,0:T(8,128)(2,1)S(1)} %bitcast.176), kind=kOutput, calls=%fused_computation.27 | convolution fusion | flops 5924323328 | bytes 27262976 | tf_op jit(solution)/shard_map/dot_general | solution.py:379
  602.0 13.3 %convolution_add_fusion.3 = f32[1024,2048]{1,0:T(8,128)} fusion(f32[1024,2048]{1,0:T(8,128)} %fusion.77, bf16[1024,1408]{1,0:T(8,128)(2,1)} %get-tuple-element.168, bf16[1024,1408]{1,0:T(8,128)(2,1)} %copy-done.45, bf16[1024,1408]{1,0:T(8,128)(2,1)} %get-tuple-element.170), kind=kOutput, calls=%fused_computation.89 | convolution fusion | flops 5919211520 | bytes 25427968 | tf_op jit(solution)/shard_map/dot_general | solution.py:379
  636.5 14.0 %multiply_convert_fusion.1 = (bf16[1024,1408]{1,0:T(8,128)(2,1)}, bf16[1024,1408]{1,0:T(8,128)(2,1)S(1)}) fusion(f32[1024,1408]{1,0:T(8,128)} %fusion.59, f32[1024,1408]{1,0:T(8,128)} %get-tuple-element.232, bf16[1024,2048]{1,0:T(8,128)(2,1)} %get-tuple-element.109, bf16[2048,1408]{1,0:T(8,128)(2,1)S(1)} %bitcast.177), kind=kOutput, calls=%fused_computation.25 | convolution fusion | flops 5924323328 | bytes 27262976 | tf_op jit(solution)/shard_map/dot_general | solution.py:379
  733.5 27.4 %shard_map.358 = (bf16[2048,1536]{1,0:T(8,128)(2,1)}, f32[2048,128]{1,0:T(8,128)}, f32[4,1024]{1,0:T(4,128)}, f32[1,256]{1,0:T(1,128)}, f32[8,128]{1,0:T(8,128)}) custom-call(f32[2048,1536]{1,0:T(8,128)} %fusion.96.refs_0_.refs_1_.refs_2_.refs_3_, f32[2048,1536]{1,0:T(8,128)} %fusion.96.refs_0_.refs_1_.refs_2_.refs_3_, ...), custom_call_target="tpu_custom_call" | custom-call | flops 28600000512 | bytes 26000000 | tf_op jit(solution)/shard_map/pallas_call | solution.py:326
  808.1 27.9 %shard_map.359 = (bf16[2048,1664]{1,0:T(8,128)(2,1)}, f32[2048,128]{1,0:T(8,128)}, f32[4,1024]{1,0:T(4,128)}, f32[1,256]{1,0:T(1,128)}, f32[8,128]{1,0:T(8,128)}) custom-call(f32[2048,1664]{1,0:T(8,128)} %fusion.95.refs_0_.refs_1_.refs_2_.refs_3_.refs_4_, f32[2048,1664]{1,0:T(8,128)} %fusion.95.refs_0_.refs_1_.refs_2_.refs_3_.refs_4_, ...), custom_call_target="tpu_custom_call" | custom-call | flops 28600000512 | bytes 26000000 | tf_op jit(solution)/shard_map/pallas_call | solution.py:326
  851.3 27.4 %shard_map.360 = (bf16[2048,1536]{1,0:T(8,128)(2,1)}, f32[2048,128]{1,0:T(8,128)}, f32[4,1024]{1,0:T(4,128)}, f32[1,256]{1,0:T(1,128)}, f32[8,128]{1,0:T(8,128)}) custom-call(f32[2048,1536]{1,0:T(8,128)} %fusion.96.refs_0_.refs_1_.refs_2_.refs_3_, ...), custom_call_target="tpu_custom_call", output_to_operand_aliasing={{0}: (13, {}), {1}: (14, {})} | custom-call | flops 28600000512 | bytes 26000000 | tf_op jit(solution)/shard_map/pallas_call | solution.py:326
  906.8 28.4 %shard_map.361 = (bf16[2048,1664]{1,0:T(8,128)(2,1)}, f32[2048,128]{1,0:T(8,128)}, f32[4,1024]{1,0:T(4,128)}, f32[1,256]{1,0:T(1,128)}, f32[8,128]{1,0:T(8,128)}) custom-call(f32[2048,1664]{1,0:T(8,128)} %fusion.95.refs_0_.refs_1_.refs_2_.refs_3_.refs_4_, ...), custom_call_target="tpu_custom_call", output_to_operand_aliasing={{0}: (14, {}), {1}: (15, {})} | custom-call | flops 28600000512 | bytes 26000000 | tf_op jit(solution)/shard_map/pallas_call | solution.py:326
  946.8 12.9 %convolution_convert_fusion.3 = bf16[1024,1664]{1,0:T(8,128)(2,1)} fusion(bf16[2048,1664]{1,0:T(8,128)(2,1)} %get-tuple-element.143, bf16[2048,2048]{1,0:T(8,128)(2,1)} %fusion.2), kind=kOutput, calls=%fused_computation.94 | convolution fusion | flops 6981025792 | bytes 14417920 | tf_op jit(solution)/shard_map/dot_general | solution.py:379
  971.6 12.2 convolution_add_fusion.1
  1002.7 12.3 add_convert_fusion.1
  1069.3 13.7 %add_convert_fusion = bf16[1024,1664]{1,0:T(8,128)(2,1)} fusion(bf16[1024,1664]{1,0:T(8,128)(2,1)} %collective-permute-done.33, bf16[2048,1664]{1,0:T(8,128)(2,1)} %get-tuple-element.143, bf16[2048,2048]{1,0:T(8,128)(2,1)} %fusion.2), kind=kOutput, calls=%fused_computation.8 | convolution fusion | flops 6984433664 | bytes 17825792 | tf_op jit(solution)/shard_map/dot_general | solution.py:379
  1135.0 18.3 %collective-permute-done.35 = bf16[512,2048]{1,0:T(8,128)(2,1)} collective-permute-done((bf16[512,2048]{1,0:T(8,128)(2,1)}, bf16[512,2048]{1,0:T(8,128)(2,1)}, u32[]{:S(2)}, u32[]{:S(2)}) %collective-permute-start.35) | collective-permute-done | bytes 2097184 | tf_op jit(solution)/shard_map/ppermute | solution.py:351
  (597 shorter events, 694.4 us)
Async XLA Ops:
  31.7 102.0 %all-gather.8.cloned.1.call-start = ((), (), s32[]{:S(2)}) async-start(), calls=%async_computation.17 | async-start | bytes 4259840 | tf_op jit(solution)/shard_map/all_gather | solution.py:363
  63.3 138.6 %all-gather.6.cloned.1.call-start = ((), (), s32[]{:S(2)}) async-start(), calls=%async_computation.16 | async-start | bytes 3932160 | tf_op jit(solution)/shard_map/all_gather | solution.py:363
  75.5 104.5 %collective-permute-start = (bf16[512,2048]{1,0:T(8,128)(2,1)}, bf16[512,2048]{1,0:T(8,128)(2,1)}, u32[]{:S(2)}, u32[]{:S(2)}) collective-permute-start(bf16[512,2048]{1,0:T(8,128)(2,1)} %pad_maximum_fusion.13), channel_id=1, source_target_pairs={{0,1},{1,0},{2,3},{3,2},{4,5},{5,4},{6,7},{7,6},{8,9},{9,8},{10,11... | collective-permute-start | bytes 6291464 | tf_op jit(solution)/shard_map/ppermute | solution.py:351
  145.9 148.5 %all-gather.10.cloned.1.call-start = ((), (), s32[]{:S(2)}) async-start(), calls=%async_computation.18 | async-start | bytes 2621440 | tf_op jit(solution)/shard_map/all_gather | solution.py:363
  150.9 76.3 %collective-permute-start.3 = (bf16[1024,1664]{1,0:T(8,128)(2,1)}, bf16[1024,1664]{1,0:T(8,128)(2,1)}, u32[]{:S(2)}, u32[]{:S(2)}) collective-permute-start(bf16[1024,1664]{1,0:T(8,128)(2,1)} %all-gather.8.cloned.1.call-done), channel_id=1, source_target_pairs={{0,4},{4,0},{8,12},{12,8},{16,20},{20,16},{24,28},{28,24},{1,5},{5... | collective-permute-start | bytes 10223624 | tf_op jit(solution)/shard_map/ppermute | solution.py:351
  179.9 198.7 %all-gather.12.cloned.1.call-start = ((), (), s32[]{:S(2)}) async-start(), calls=%async_computation.19 | async-start | bytes 7208960 | tf_op jit(solution)/shard_map/all_gather | solution.py:363
  212.7 264.5 %all-gather.14.cloned.1.call-start = ((), (), s32[]{:S(2)}) async-start(), calls=%async_computation.20 | async-start | bytes 7208960 | tf_op jit(solution)/shard_map/all_gather | solution.py:363
  228.9 77.5 %collective-permute-start.7 = (bf16[1024,1536]{1,0:T(8,128)(2,1)}, bf16[1024,1536]{1,0:T(8,128)(2,1)}, u32[]{:S(2)}, u32[]{:S(2)}) collective-permute-start(bf16[1024,1536]{1,0:T(8,128)(2,1)} %all-gather.6.cloned.1.call-done), channel_id=1, source_target_pairs={{0,4},{4,0},{8,12},{12,8},{16,20},{20,16},{24,28},{28,24},{1,5},{5... | collective-permute-start | bytes 9437192 | tf_op jit(solution)/shard_map/ppermute | solution.py:351
  297.6 73.7 %collective-permute-start.11 = (bf16[512,2048]{1,0:T(8,128)(2,1)}, bf16[512,2048]{1,0:T(8,128)(2,1)}, u32[]{:S(2)}, u32[]{:S(2)}) collective-permute-start(bf16[512,2048]{1,0:T(8,128)(2,1)} %collective-permute-done.10), channel_id=1, source_target_pairs={{0,1},{1,0},{2,3},{3,2},{4,5},{5,4},{6,7},{7,6},{8,9},{9,8},{10,11... | collective-permute-start | bytes 6291464 | tf_op jit(solution)/shard_map/ppermute | solution.py:351
  371.3 436.8 %reduce-scatter.7.cloned.1.call-start = ((), (), s32[]{:S(2)}) async-start(), calls=%async_computation.21 | async-start | bytes 3604480 | tf_op jit(solution)/shard_map/reduce_scatter | solution.py:394
  386.5 127.0 %collective-permute-start.17 = (bf16[1024,2816]{1,0:T(8,128)(2,1)}, bf16[1024,2816]{1,0:T(8,128)(2,1)}, u32[]{:S(2)}, u32[]{:S(2)}) collective-permute-start(bf16[1024,2816]{1,0:T(8,128)(2,1)} %all-gather.12.cloned.1.call-done), channel_id=1, source_target_pairs={{0,4},{4,0},{8,12},{12,8},{16,20},{20,16},{24,28},{28,24},{1,5},{5... | collective-permute-start | bytes 17301512 | tf_op jit(solution)/shard_map/ppermute | solution.py:351
  443.7 74.5 %collective-permute-start.18 = (bf16[512,2048]{1,0:T(8,128)(2,1)S(1)}, bf16[512,2048]{1,0:T(8,128)(2,1)}, u32[]{:S(2)}, u32[]{:S(2)}) collective-permute-start(bf16[512,2048]{1,0:T(8,128)(2,1)S(1)} %multiply_convert_fusion.6), channel_id=1, source_target_pairs={{0,2},{1,3},{2,0},{3,1},{4,6},{5,7},{6,4},{7,5},{8,10},{9,11},{10,... | collective-permute-start | bytes 6291464 | tf_op jit(solution)/shard_map/ppermute | solution.py:351
  444.2 74.0 %collective-permute-start.16 = (bf16[512,2048]{1,0:T(8,128)(2,1)S(1)}, bf16[512,2048]{1,0:T(8,128)(2,1)}, u32[]{:S(2)}, u32[]{:S(2)}) collective-permute-start(bf16[512,2048]{1,0:T(8,128)(2,1)S(1)} %multiply_convert_fusion.6), channel_id=1, source_target_pairs={{0,1},{1,0},{2,3},{3,2},{4,5},{5,4},{6,7},{7,6},{8,9},{9,8},{10,11... | collective-permute-start | bytes 6291464 | tf_op jit(solution)/shard_map/ppermute | solution.py:351
  722.1 172.2 %reduce-scatter.9.cloned.1.call-start = ((), (), s32[]{:S(2)}) async-start(), calls=%async_computation.22 | async-start | bytes 3604480 | tf_op jit(solution)/shard_map/reduce_scatter | solution.py:394
  787.3 94.9 %collective-permute-start.28 = (bf16[1024,1408]{1,0:T(8,128)(2,1)}, bf16[1024,1408]{1,0:T(8,128)(2,1)}, u32[]{:S(2)}, u32[]{:S(2)}) collective-permute-start(bf16[1024,1408]{1,0:T(8,128)(2,1)} %convolution_convert_fusion.1), channel_id=1, source_target_pairs={{0,4},{4,0},{8,12},{12,8},{16,20},{20,16},{24,28},{28,24},{1,5},{5... | collective-permute-start | bytes 8650760 | tf_op jit(solution)/shard_map/ppermute | solution.py:351
  850.1 85.0 %collective-permute-start.29 = (bf16[1024,1024]{1,0:T(8,128)(2,1)}, bf16[1024,1024]{1,0:T(8,128)(2,1)S(1)}, u32[]{:S(2)}, u32[]{:S(2)}) collective-permute-start(bf16[1024,1024]{1,0:T(8,128)(2,1)} %fusion.66), channel_id=1, source_target_pairs={{0,4},{4,0},{8,12},{12,8},{16,20},{20,16},{24,28},{28,24},{1,5},{5... | collective-permute-start | bytes 6291464 | tf_op jit(solution)/shard_map/ppermute | solution.py:351
  882.1 77.6 %reduce-scatter.11.cloned.1.call-start = ((), (), s32[]{:S(2)}) async-start(), calls=%async_computation.23 | async-start | bytes 3604480 | tf_op jit(solution)/shard_map/reduce_scatter | solution.py:394
  905.9 96.8 %collective-permute-start.31 = (bf16[1024,1536]{1,0:T(8,128)(2,1)}, bf16[1024,1536]{1,0:T(8,128)(2,1)}, u32[]{:S(2)}, u32[]{:S(2)}) collective-permute-start(bf16[1024,1536]{1,0:T(8,128)(2,1)} %convolution_convert_fusion), channel_id=1, source_target_pairs={{0,4},{4,0},{8,12},{12,8},{16,20},{20,16},{24,28},{28,24},{1,5},{5... | collective-permute-start | bytes 9437192 | tf_op jit(solution)/shard_map/ppermute | solution.py:351
  946.8 98.1 %reduce-scatter.13.cloned.1.call-start = ((), (), s32[]{:S(2)}) async-start(), calls=%async_computation.24 | async-start | bytes 2621440 | tf_op jit(solution)/shard_map/reduce_scatter | solution.py:394
  993.0 76.2 %collective-permute-start.33 = (bf16[1024,1664]{1,0:T(8,128)(2,1)}, bf16[1024,1664]{1,0:T(8,128)(2,1)}, u32[]{:S(2)}, u32[]{:S(2)}) collective-permute-start(bf16[1024,1664]{1,0:T(8,128)(2,1)} %convolution_convert_fusion.3), channel_id=1, source_target_pairs={{0,4},{4,0},{8,12},{12,8},{16,20},{20,16},{24,28},{28,24},{1,5},{5... | collective-permute-start | bytes 10223624 | tf_op jit(solution)/shard_map/ppermute | solution.py:351
  997.8 108.0 %reduce-scatter.15.cloned.1.call-start = ((), (), s32[]{:S(2)}) async-start(), calls=%async_computation.25 | async-start | bytes 3932160 | tf_op jit(solution)/shard_map/reduce_scatter | solution.py:394
  1050.7 152.5 %reduce-scatter.17.cloned.1.call-start = ((), (), s32[]{:S(2)}) async-start(), calls=%async_computation.26 | async-start | bytes 4259840 | tf_op jit(solution)/shard_map/reduce_scatter | solution.py:394
  1060.7 116.8 %collective-permute-start.37 = (bf16[512,2048]{1,0:T(8,128)(2,1)}, bf16[512,2048]{1,0:T(8,128)(2,1)}, u32[]{:S(2)}, u32[]{:S(2)}) collective-permute-start(bf16[512,2048]{1,0:T(8,128)(2,1)} %fusion.19), channel_id=1, source_target_pairs={{0,2},{1,3},{2,0},{3,1},{4,6},{5,7},{6,4},{7,5},{8,10},{9,11},{10,... | collective-permute-start | bytes 6291464 | tf_op jit(solution)/shard_map/ppermute | solution.py:351
  1066.0 87.2 %collective-permute-start.35 = (bf16[512,2048]{1,0:T(8,128)(2,1)}, bf16[512,2048]{1,0:T(8,128)(2,1)}, u32[]{:S(2)}, u32[]{:S(2)}) collective-permute-start(bf16[512,2048]{1,0:T(8,128)(2,1)} %fusion.18), channel_id=1, source_target_pairs={{0,2},{1,3},{2,0},{3,1},{4,6},{5,7},{6,4},{7,5},{8,10},{9,11},{10,... | collective-permute-start | bytes 6291464 | tf_op jit(solution)/shard_map/ppermute | solution.py:351
  (135 other events, 3691.0 us)
Sparse Core Ops, SparseCore 0:
  55.4 69.8 all-gather.7
  127.5 62.1 all-gather.5
  191.8 44.5 all-gather.9
  238.4 105.3 all-gather.11
  371.4 105.6 all-gather.13
  722.2 55.4 reduce-scatter.6
  796.5 55.8 reduce-scatter.8
  894.4 56.6 reduce-scatter.10
  994.3 44.2 reduce-scatter.12
  1045.1 60.5 reduce-scatter.14
  1135.1 67.0 reduce-scatter.16

commit v6 on v5

--- a/solution.py
+++ b/solution.py
@@ -264,27 +264,23 @@
     return pl.CostEstimate(flops=int(us * 1.1e9), bytes_accessed=int(us * 1e6), transcendentals=0)
 
 
-def mixer_fwd(proj, first, pos, taps, gain, prm, dims, half, mixed=None):
+def mixer_fwd(proj, first, pos, taps, gain, prm, dims, half, part=None, filled=()):
     tok = pos.shape[0]
     nh, dk, dv = dims
     hs = nh // SPLIT
     ns = tok // SEQ
     wv = hs * dv
-    row = pl.BlockSpec((ROWS, wv), lambda i: (i, 0))
-    specs = shared_specs(dims)
-    args = [proj, proj, proj, proj, first, pos, taps, gain, prm]
-    alias = {}
-    if mixed is not None:
-        alias = {len(args): 0}
-        args.append(mixed)
-        specs.append(pl.BlockSpec(memory_space=pl.ANY))
+    steps = ns // PAIR if part is None else ns // PAIR // 2
+    off = part * steps if part else 0
+    row = pl.BlockSpec((ROWS, wv), lambda i: (i + off, 0))
+    args = [proj, proj, proj, proj, first, pos, taps, gain, prm, *filled]
     return pl.pallas_call(
         functools.partial(fwd_kernel, dims, half),
-        grid=(ns // PAIR,),
-        in_specs=specs,
+        grid=(steps,),
+        in_specs=shared_specs(dims, off) + [pl.BlockSpec(memory_space=pl.ANY)] * len(filled),
         out_specs=[
-            pl.BlockSpec((ROWS, wv), lambda i: (i, half)),
-            pl.BlockSpec((PAIR * hs, SEQ, SEQ), lambda i: (i, 0, 0)),
+            pl.BlockSpec((ROWS, wv), lambda i: (i + off, half)),
+            pl.BlockSpec((PAIR * hs, SEQ, SEQ), lambda i: (i + off, 0, 0)),
             row,
             row,
         ],
@@ -294,8 +290,8 @@
             jax.ShapeDtypeStruct((tok, wv), f32),
             jax.ShapeDtypeStruct((tok, wv), f32),
         ],
-        input_output_aliases=alias,
-        cost_estimate=cost(4),
+        input_output_aliases={9 + i: i for i in range(len(filled))},
+        cost_estimate=cost(4 if part is None else 12),
         compiler_params=pltpu.CompilerParams(vmem_limit_bytes=48 << 20),
     )(*args)
 
@@ -413,15 +409,16 @@
     return around(rows), around(beyond), beyond
 
 
-def sum_tokens(far, near, size, *needs):
+def sum_tokens(far, near, size, *needs, last=False):
     half = size // 2
 
-    def around(part):
+    def around(part, *first):
         held = jnp.split(part, half, axis=0)
         step = 1
         while step < half:
             for j in range(0, half, 2 * step):
-                held[j] = held[j] + xor_send(held[j + step].astype(bf16), "rep", size, step).astype(f32)
+                low = held[j + step].astype(bf16)
+                held[j] = held[j] + xor_send(after(low, *first) if first else low, "rep", size, step).astype(f32)
             step *= 2
         return held[0]
 
@@ -430,7 +427,7 @@
     if needs:
         beyond = after(beyond, *needs)
     got = xor_send(beyond, "rep", size, half)
-    return around(part) + got.astype(f32), got
+    return around(part, *([got] if last else [])) + got.astype(f32), got
 
 
 def rms(values):
@@ -496,8 +493,11 @@
         def quarter(arrays):
             return jnp.concatenate([a.reshape(shard, R, -1) for a in arrays], axis=2)
 
-        def spread(packed):
-            return lax.all_to_all(packed.transpose(1, 0, 2), "rep", 0, 0).reshape(R * shard, -1)
+        def spread(packed, *needs):
+            packed = packed.transpose(1, 0, 2)
+            if needs:
+                packed = after(packed, *needs)
+            return lax.all_to_all(packed, "rep", 0, 0).reshape(R * shard, -1)
 
         extra = jnp.concatenate(
             [gain_one[:, None], gain_two[:, None], conv_q.T, conv_k.T,
@@ -522,7 +522,7 @@
         every_near, every_far, every_got = join_tokens(own, R)
         every = jnp.concatenate([every_near, every_far], axis=0)
         ids_all = jnp.concatenate(join_tokens(segments[:, None], R)[:2], axis=0).reshape(ns, SEQ)
-        part_r = spread(quarter([after(w_out.T, extra_all, every_got, line_1), w_ffgate, w_ffup, w_down.T]))
+        part_r = spread(quarter([w_out.T, w_ffgate, w_ffup, w_down.T]), extra_all, every_got, line_1)
         part_b, part_gu, part_d = part_r[:, :wv], part_r[:, wv : wv + 2 * ffq], part_r[:, wv + 2 * ffq :]
         line_2 = gather_line(after(part_2, extra_all), F)
         wa1, side_1 = gather_side(line_1, F)
@@ -552,36 +552,43 @@
         mixed, x_1, u_1, o_1 = mixer_fwd(proj_1, proj_1, pos, taps[0], gain_out, prm, dims, 0)
         wa2, side_2 = gather_side(line_2, F, side_1)
         proj_2 = dot(after(normed_one, mixed, line_b), wa2)
-        mixed, x_2, u_2, o_2 = mixer_fwd(proj_2, proj_1, pos, taps[1], gain_out, prm, dims, 1, mixed)
+        mixed, *saved_2 = mixer_fwd(proj_2, proj_1, pos, taps[1], gain_out, prm, dims, 1, 1, [mixed])
         wd, line_d, got_d = gather_side_first(part_d, F, side_2)
         wb, side_b = gather_side(line_b, F, side_2)
-        mixed = after(mixed, line_gu, got_d, cot_near, cot_far)
         side_gu = xor_send(after(line_gu, side_b), "fsdp", F, 1)
         wg, wu = (jnp.concatenate([line_gu[:, at : at + ffq], side_gu[:, at : at + ffq]], axis=0) for at in (0, ffq))
         own32 = own.astype(f32)
         mid = tok // 2
-        added, unused = sum_tokens(lambda: dot(mixed[mid:], wb, NT), lambda part: dot(after(mixed, part)[:mid], wb, NT), R)
+        mixed = after(mixed, line_gu, got_d, cot_near, cot_far)
+        out_far = dot(mixed[mid:], wb, NT)
+        kept = {}
+
+        def keep(name, value):
+            kept[name] = value
+            return value
+
+        def near_mixed(part):
+            kept["mixed"], *kept["saved"] = mixer_fwd(
+                proj_2, proj_1, after(pos, part), taps[1], gain_out, prm, dims, 1, 0, [mixed, *saved_2])
+            return dot(kept["mixed"][:mid], wb, NT)
+
+        added, unused = sum_tokens(lambda: out_far, near_mixed, R, last=True)
+        mixed, saved_2 = kept["mixed"], kept["saved"]
         middle = own32 + added
         r2 = rms(middle)
         n2 = middle * r2
         normed_own = (n2 * gain_second).astype(bf16)
         two = join_tokens(normed_own, R)[:2]
         gates, ups, acts, sigs, hiddens = [], [], [], [], []
-        for normed in (two[0], after(two[1], line_d)):
+        for normed in two:
             gates.append(dot(normed, wg))
-            ups.append(dot(normed, wu))
+            ups.append(dot(after(normed, gates[-1], line_d) if ups else normed, wu))
             sigs.append(jax.nn.sigmoid(gates[-1]))
             acts.append(gates[-1] * sigs[-1])
             hiddens.append((acts[-1] * ups[-1]).astype(bf16))
         hidden = jnp.concatenate(hiddens, axis=0)
         normed_two = jnp.concatenate(two, axis=0)
         cot_all = jnp.concatenate([cot_near, cot_far], axis=0)
-
-        kept = {}
-
-        def keep(name, value):
-            kept[name] = value
-            return value
 
         g_down = Summed(cot_all, hidden, F)
         dgates, dups = [None, None], [None, None]
@@ -600,7 +607,7 @@
         dmiddle_own = dmiddle.astype(bf16)
         dlow = join_tokens(dmiddle_own, R)[:2]
         dm_near = dot(dlow[0], wb)
-        args_2 = (proj_2, proj_1, pos, taps[1], gain_out, prm, x_2, u_2, o_2)
+        args_2 = (proj_2, proj_1, pos, taps[1], gain_out, prm, *saved_2)
         args_1 = (proj_1, proj_1, pos, taps[0], gain_out, prm, x_1, u_1, o_1)
         dp_2, dba, dt_2, dg_2, dr_2 = mixer_bwd(*args_2, dm_near, dims, 1, 0)
         g_up = Summed(normed_two, after(jnp.concatenate(dups, axis=0), dba), F, g_gate.got)
@@ -625,21 +632,15 @@
         t_out = g_out.total(R)
 
         def near_one(part):
-            g_2.side(part, before=(g_out.sum,))
-
-            def far_out():
-                return keep("far", dot(after(hiddens[1], g_2.low, t_up), wd, NT))
-
-            def near_out(held):
-                g_1.side(kept["far"], held, before=(g_2.sum,))
-                return keep("last", dot(after(hiddens[0], g_1.low), wd, NT))
-
-            kept["out"], unused = sum_tokens(far_out, near_out, R)
-            return back_one(0, mid, kept["last"], t_out, g_2.sum)
+            g_2.side(part, g_out.sum)
+
+            keep("far", dot(after(hiddens[1], g_2.low, t_up), wd, NT))
+            return keep("one", back_one(0, mid, kept["far"]))
 
         dnormed_one, far_one = sum_tokens(lambda: back_one(mid, tok, g_1.sent, g_up.sum, t_gate), near_one, R)
-        added = kept["out"]
-        layer_out = (middle + added).astype(bf16)
+        g_1.side(kept["one"], before=(g_2.sum,))
+        added, unused = sum_tokens(lambda: kept["far"], lambda part: dot(after(hiddens[0], g_1.low, t_out), wd, NT), R)
+        layer_out = (middle + after(added, g_1.sum)).astype(bf16)
         dprm = dr_1 + dr_2 + er_1 + er_2
         dgain_out = dg_1 + dg_2 + eg_1 + eg_2
         dtaps = [dt_1 + et_1, dt_2 + et_2]

time: 1240 us -> 1240 us (level)
  waiting for transfers between devices: 256 us -> 229 us
    ppermute x38, waiting for transfers between devices: 168 us -> 115 us  [xor_send(): return lax.ppermute(value, axis, [(i, i ^ step) for i in range(size)])]
    all_to_all x1, waiting for transfers between devices: 1.02 us -> 26.4 us  [on_device(): summed = jnp.sum(lax.all_to_all(packed, both, 0, 0, tiled=True), axis=0)]
    pallas_call x2 -> x3, Pallas kernels: 68.4 us -> 72.2 us  [mixer_fwd(): pl.pallas_call(functools.partial(fwd_kernel, dims, half), grid=(steps,),...]
    unnamed x271 -> x321, local copies, waits for them, and re-layouts: 94.7 us -> 98 us
where the time goes in v6:
time: 1240 us; the launch traced here: 1230 us
  matrix products  383 us (31%)
  local copies, waits for them, and re-layouts  230 us (19%)
  waiting for transfers between devices  229 us (18%)
  Pallas kernels  183 us (15%)
  other arithmetic  126 us (10%)
  starting transfers between devices  61.1 us (5%)
  between operations  16.2 us (1%)
    dot_general x34, matrix products, dot(): lax.dot_general(left, right, dims, preferred_element_type=f32).astype(out)  383 us
    ppermute x38, waiting for transfers between devices, xor_send(): return lax.ppermute(value, axis, [(i, i ^ step) for i in range(size)])  115 us
    pallas_call x4, Pallas kernels, mixer_bwd(): pl.pallas_call(functools.partial(bwd_kernel, dims, half, before is not No...  111 us
    unnamed x321, local copies, waits for them, and re-layouts  98 us
    pallas_call x3, Pallas kernels, mixer_fwd(): pl.pallas_call(functools.partial(fwd_kernel, dims, half), grid=(steps,),...  72.2 us
    all_gather x5, waiting for transfers between devices, gather_line(): lax.all_gather(rows, 'fsdp', axis=0, tiled=True, axis_index_groups=lines(...  35.8 us
    all_to_all x2, waiting for transfers between devices, spread(): return lax.all_to_all(packed, 'rep', 0, 0).reshape(R * shard, -1)  26.8 us
    all_to_all x1, waiting for transfers between devices, on_device(): summed = jnp.sum(lax.all_to_all(packed, both, 0, 0, tiled=True), axis=0)  26.4 us
  transfers between devices with their start and end apart: 59, of which 20 were waited for; matrix products, arithmetic and copies ran while one was open for 47% of the time, Pallas kernels for 15%

profile of v6, /device:TPU:0, one launch (start us, length us, event | category | flops | bytes accessed | tf_op | source)
XLA Modules:
  0.0 1228.4 jit_solution(3852601845805334954)
XLA Ops:
  94.1 29.3 %collective-permute-done.5 = s32[512,1]{0,1:T(1,128)S(1)} collective-permute-done((s32[512,1]{0,1:T(1,128)S(1)}, s32[512,1]{0,1:T(1,128)S(1)}, u32[]{:S(2)}, u32[]{:S(2)}) %collective-permute-start.5) | collective-permute-done | bytes 2080 | tf_op jit(solution)/shard_map/ppermute | solution.py:347
  153.5 25.4 %all-to-all-done.2 = bf16[4,64,5248]{2,1,0:T(8,128)(2,1)} async-done(((bf16[4,64,5248]{2,1,0:T(8,128)(2,1)}), bf16[4,64,5248]{2,1,0:T(8,128)(2,1)}, u32[]{:S(2)}, u32[]{:S(2)}) %all-to-all-start.2) | async-done | bytes 2687008 | tf_op jit(solution)/shard_map/all_to_all | solution.py:500
  214.0 14.0 %collective-permute-done.3 = bf16[1024,1664]{1,0:T(8,128)(2,1)} collective-permute-done((bf16[1024,1664]{1,0:T(8,128)(2,1)}, bf16[1024,1664]{1,0:T(8,128)(2,1)}, u32[]{:S(2)}, u32[]{:S(2)}) %collective-permute-start.3) | collective-permute-done | bytes 3407904 | tf_op jit(solution)/shard_map/ppermute | solution.py:347
  234.2 21.2 %fusion.93.refs_0_.refs_1_.refs_2_.refs_3_.refs_4_ = f32[2048,1664]{1,0:T(8,128)} fusion(bf16[2048,2048]{1,0:T(8,128)(2,1)} %fusion.2, bf16[2048,1664]{1,0:T(8,128)(2,1)} %constant_dynamic-update-slice_fusion.13), kind=kOutput, calls=%fused_computation.287 | convolution fusion | flops 13958643712 | bytes 28835840 | tf_op jit(solution)/shard_map/dot_general | solution.py:375
  257.8 34.2 %shard_map.356 = (bf16[2048,1024]{1,0:T(8,128)(2,1)S(1)}, f32[16,256,256]{2,1,0:T(8,128)}, f32[2048,512]{1,0:T(8,128)}, f32[2048,512]{1,0:T(8,128)}) custom-call(f32[2048,1664]{1,0:T(8,128)} %fusion.93.refs_0_.refs_1_.refs_2_.refs_3_.refs_4_, f32[2048,1664]{1,0:T(8,128)} %fusion.93.refs_0_.refs_1_.refs_2_.refs_3_.refs_4_, ...), custom_call_target="tpu_custom_call" | custom-call | flops 4400000000 | bytes 4000000 | tf_op jit(solution)/shard_map/pallas_call | solution.py:277
  312.7 15.8 %fusion.94.refs_0_.refs_1_.refs_2_.refs_3_ = f32[2048,1536]{1,0:T(8,128)} fusion(bf16[2048,2048]{1,0:T(8,128)(2,1)S(1)} %bitcast.167, bf16[2048,1536]{1,0:T(8,128)(2,1)S(1)} %constant_dynamic-update-slice_fusion.15), kind=kOutput, calls=%fused_computation.288 | convolution fusion | flops 12884901888 | bytes 27262976 | tf_op jit(solution)/shard_map/dot_general | solution.py:375
  328.5 19.0 %shard_map.357 = (bf16[2048,1024]{1,0:T(8,128)(2,1)S(1)}, f32[16,256,256]{2,1,0:T(8,128)}, f32[2048,512]{1,0:T(8,128)}, f32[2048,512]{1,0:T(8,128)}) custom-call(f32[2048,1536]{1,0:T(8,128)} %fusion.94.refs_0_.refs_1_.refs_2_.refs_3_, f32[2048,1536]{1,0:T(8,128)} %fusion.94.refs_0_.refs_1_.refs_2_.refs_3_, ...), custom_call_target="tpu_custom_call", output_to_operand_aliasing={{0}: (9, {})} | custom-call | flops 13200000000 | bytes 12000000 | tf_op jit(solution)/shard_map/pallas_call | solution.py:277
  394.3 19.0 %shard_map.358 = (bf16[2048,1024]{1,0:T(8,128)(2,1)S(1)}, f32[16,256,256]{2,1,0:T(8,128)}, f32[2048,512]{1,0:T(8,128)}, f32[2048,512]{1,0:T(8,128)}) custom-call(f32[2048,1536]{1,0:T(8,128)} %fusion.94.refs_0_.refs_1_.refs_2_.refs_3_, ...), custom_call_target="tpu_custom_call", output_to_operand_aliasing={{0}: (9, {}), {1}: (10, {}), {2}: (11, {}), {3}: (12, {})} | custom-call | flops 13200000000 | bytes 12000000 | tf_op jit(solution)/shard_map/pallas_call | solution.py:277
  421.5 18.0 %collective-permute-done.14 = bf16[512,2048]{1,0:T(8,128)(2,1)S(1)} collective-permute-done((bf16[512,2048]{1,0:T(8,128)(2,1)}, bf16[512,2048]{1,0:T(8,128)(2,1)S(1)}, u32[]{:S(2)}, u32[]{:S(2)}) %collective-permute-start.14) | collective-permute-done | bytes 2097184 | tf_op jit(solution)/shard_map/ppermute | solution.py:347
  451.4 35.7 %all-gather.14.cloned.1.call-done = bf16[2048,1408]{1,0:T(8,128)(2,1)} async-done(((bf16[512,1408]{1,0:T(8,128)(2,1)}), bf16[2048,1408]{1,0:T(8,128)(2,1)}) %all-gather.14.cloned.1.call-update) | async-done | bytes 5767184 | tf_op jit(solution)/shard_map/all_gather | solution.py:359
  490.2 19.7 %collective-permute-done.17 = bf16[1024,2816]{1,0:T(8,128)(2,1)} collective-permute-done((bf16[1024,2816]{1,0:T(8,128)(2,1)}, bf16[1024,2816]{1,0:T(8,128)(2,1)}, u32[]{:S(2)}, u32[]{:S(2)}) %collective-permute-start.17) | collective-permute-done | bytes 5767200 | tf_op jit(solution)/shard_map/ppermute | solution.py:347
  526.5 14.2 %multiply_convert_fusion.5 = (bf16[1024,1408]{1,0:T(8,128)(2,1)S(1)}, f32[1024,1408]{1,0:T(8,128)}) fusion(f32[1024,1408]{1,0:T(8,128)} %fusion.57, bf16[1024,1408]{1,0:T(8,128)(2,1)} %get-tuple-element.183, bf16[1024,1408]{1,0:T(8,128)(2,1)} %get-tuple-element.181, bf16[512,2048]{1,0:T(8,128)(2,1)} %collective-permute-done.16, ...), kind=kOutput, calls=%fused_computation.31 | convolution fusion | flops 5934153728 | bytes 24379392 | tf_op jit(solution)/shard_map/dot_general | solution.py:375
  554.8 12.1 multiply_convert_fusion.4
  577.9 13.9 %multiply_convert_fusion.3 = (bf16[1024,1408]{1,0:T(8,128)(2,1)}, bf16[1024,1408]{1,0:T(8,128)(2,1)S(1)}) fusion(f32[1024,1408]{1,0:T(8,128)} %fusion.77, f32[1024,1408]{1,0:T(8,128)} %get-tuple-element.244, bf16[1024,2048]{1,0:T(8,128)(2,1)} %get-tuple-element.118, bf16[2048,1408]{1,0:T(8,128)(2,1)S(1)} %bitcast.172), kind=kOutput, calls=%fused_computation.27 | convolution fusion | flops 5924323328 | bytes 27262976 | tf_op jit(solution)/shard_map/dot_general | solution.py:375
  638.1 14.3 %multiply_convert_fusion.1 = (bf16[1024,1408]{1,0:T(8,128)(2,1)}, bf16[1024,1408]{1,0:T(8,128)(2,1)S(1)}) fusion(f32[1024,1408]{1,0:T(8,128)} %fusion.57, f32[1024,1408]{1,0:T(8,128)} %get-tuple-element.242, bf16[1024,2048]{1,0:T(8,128)(2,1)} %get-tuple-element.119, bf16[2048,1408]{1,0:T(8,128)(2,1)S(1)} %bitcast.177), kind=kOutput, calls=%fused_computation.25 | convolution fusion | flops 5924323328 | bytes 27262976 | tf_op jit(solution)/shard_map/dot_general | solution.py:375
  732.5 27.6 %shard_map.359 = (bf16[2048,1536]{1,0:T(8,128)(2,1)}, f32[2048,128]{1,0:T(8,128)}, f32[4,1024]{1,0:T(4,128)}, f32[1,256]{1,0:T(1,128)}, f32[8,128]{1,0:T(8,128)}) custom-call(f32[2048,1536]{1,0:T(8,128)} %fusion.94.refs_0_.refs_1_.refs_2_.refs_3_, f32[2048,1536]{1,0:T(8,128)} %fusion.94.refs_0_.refs_1_.refs_2_.refs_3_, ...), custom_call_target="tpu_custom_call" | custom-call | flops 28600000512 | bytes 26000000 | tf_op jit(solution)/shard_map/pallas_call | solution.py:322
  806.1 27.9 %shard_map.360 = (bf16[2048,1664]{1,0:T(8,128)(2,1)}, f32[2048,128]{1,0:T(8,128)}, f32[4,1024]{1,0:T(4,128)}, f32[1,256]{1,0:T(1,128)}, f32[8,128]{1,0:T(8,128)}) custom-call(f32[2048,1664]{1,0:T(8,128)} %fusion.93.refs_0_.refs_1_.refs_2_.refs_3_.refs_4_, f32[2048,1664]{1,0:T(8,128)} %fusion.93.refs_0_.refs_1_.refs_2_.refs_3_.refs_4_, ...), custom_call_target="tpu_custom_call" | custom-call | flops 28600000512 | bytes 26000000 | tf_op jit(solution)/shard_map/pallas_call | solution.py:322
  850.9 27.6 %shard_map.361 = (bf16[2048,1536]{1,0:T(8,128)(2,1)}, f32[2048,128]{1,0:T(8,128)}, f32[4,1024]{1,0:T(4,128)}, f32[1,256]{1,0:T(1,128)}, f32[8,128]{1,0:T(8,128)}) custom-call(f32[2048,1536]{1,0:T(8,128)} %fusion.94.refs_0_.refs_1_.refs_2_.refs_3_, ...), custom_call_target="tpu_custom_call", output_to_operand_aliasing={{0}: (13, {}), {1}: (14, {})} | custom-call | flops 28600000512 | bytes 26000000 | tf_op jit(solution)/shard_map/pallas_call | solution.py:322
  909.1 28.1 %shard_map.362 = (bf16[2048,1664]{1,0:T(8,128)(2,1)}, f32[2048,128]{1,0:T(8,128)}, f32[4,1024]{1,0:T(4,128)}, f32[1,256]{1,0:T(1,128)}, f32[8,128]{1,0:T(8,128)}) custom-call(f32[2048,1664]{1,0:T(8,128)} %fusion.93.refs_0_.refs_1_.refs_2_.refs_3_.refs_4_, ...), custom_call_target="tpu_custom_call", output_to_operand_aliasing={{0}: (14, {}), {1}: (15, {})} | custom-call | flops 28600000512 | bytes 26000000 | tf_op jit(solution)/shard_map/pallas_call | solution.py:322
  949.2 12.9 %convolution_convert_fusion.3 = bf16[1024,1664]{1,0:T(8,128)(2,1)} fusion(bf16[2048,1664]{1,0:T(8,128)(2,1)} %get-tuple-element.152, bf16[2048,2048]{1,0:T(8,128)(2,1)} %fusion.2), kind=kOutput, calls=%fused_computation.92 | convolution fusion | flops 6981025792 | bytes 14417920 | tf_op jit(solution)/shard_map/dot_general | solution.py:375
  974.6 12.3 convolution_add_fusion.1
  1033.6 12.1 add_convert_fusion.1
  1071.7 14.3 %convolution_add_fusion = f32[1024,2048]{1,0:T(8,128)} fusion(f32[1024,2048]{1,0:T(8,128)} %fusion.52, bf16[2048,1664]{1,0:T(8,128)(2,1)} %constant_dynamic-update-slice_fusion.13, bf16[2048,1664]{1,0:T(8,128)(2,1)} %get-tuple-element.152), kind=kOutput, calls=%fused_computation.84 | convolution fusion | flops 6981419008 | bytes 27000832 | tf_op jit(solution)/shard_map/dot_general | solution.py:375
  1141.8 26.4 %all-to-all-done.7 = f32[32,1,1192]{2,1,0:T(1,128)S(1)} async-done(((f32[32,1,1192]{2,1,0:T(1,128)}), f32[32,1,1192]{2,1,0:T(1,128)S(1)}, u32[]{:S(2)}, u32[]{:S(2)}) %all-to-all-start.7) | async-done | bytes 152608 | tf_op jit(solution)/shard_map/all_to_all | solution.py:686
  (657 shorter events, 717.4 us)
Async XLA Ops:
  31.6 107.0 %all-gather.8.cloned.1.call-start = ((), (), s32[]{:S(2)}) async-start(), calls=%async_computation.17 | async-start | bytes 4259840 | tf_op jit(solution)/shard_map/all_gather | solution.py:359
  63.3 139.5 %all-gather.6.cloned.1.call-start = ((), (), s32[]{:S(2)}) async-start(), calls=%async_computation.16 | async-start | bytes 3932160 | tf_op jit(solution)/shard_map/all_gather | solution.py:359
  75.8 105.0 %collective-permute-start = (bf16[512,2048]{1,0:T(8,128)(2,1)}, bf16[512,2048]{1,0:T(8,128)(2,1)}, u32[]{:S(2)}, u32[]{:S(2)}) collective-permute-start(bf16[512,2048]{1,0:T(8,128)(2,1)} %pad_maximum_fusion.12), channel_id=1, source_target_pairs={{0,1},{1,0},{2,3},{3,2},{4,5},{5,4},{6,7},{7,6},{8,9},{9,8},{10,11... | collective-permute-start | bytes 6291464 | tf_op jit(solution)/shard_map/ppermute | solution.py:347
  146.8 147.2 %all-gather.10.cloned.1.call-start = ((), (), s32[]{:S(2)}) async-start(), calls=%async_computation.18 | async-start | bytes 2621440 | tf_op jit(solution)/shard_map/all_gather | solution.py:359
  151.7 76.3 %collective-permute-start.3 = (bf16[1024,1664]{1,0:T(8,128)(2,1)}, bf16[1024,1664]{1,0:T(8,128)(2,1)}, u32[]{:S(2)}, u32[]{:S(2)}) collective-permute-start(bf16[1024,1664]{1,0:T(8,128)(2,1)} %all-gather.8.cloned.1.call-done), channel_id=1, source_target_pairs={{0,4},{4,0},{8,12},{12,8},{16,20},{20,16},{24,28},{28,24},{1,5},{5... | collective-permute-start | bytes 10223624 | tf_op jit(solution)/shard_map/ppermute | solution.py:347
  180.8 188.8 %all-gather.12.cloned.1.call-start = ((), (), s32[]{:S(2)}) async-start(), calls=%async_computation.19 | async-start | bytes 7208960 | tf_op jit(solution)/shard_map/all_gather | solution.py:359
  213.5 273.6 %all-gather.14.cloned.1.call-start = ((), (), s32[]{:S(2)}) async-start(), calls=%async_computation.20 | async-start | bytes 7208960 | tf_op jit(solution)/shard_map/all_gather | solution.py:359
  228.1 69.2 %collective-permute-start.9 = (bf16[512,2048]{1,0:T(8,128)(2,1)S(1)}, bf16[512,2048]{1,0:T(8,128)(2,1)}, u32[]{:S(2)}, u32[]{:S(2)}) collective-permute-start(bf16[512,2048]{1,0:T(8,128)(2,1)S(1)} %copy-done.23), channel_id=1, source_target_pairs={{0,1},{1,0},{2,3},{3,2},{4,5},{5,4},{6,7},{7,6},{8,9},{9,8},{10,11... | collective-permute-start | bytes 6291464 | tf_op jit(solution)/shard_map/ppermute | solution.py:347
  228.1 69.2 %collective-permute-start.10 = (bf16[512,2048]{1,0:T(8,128)(2,1)S(1)}, bf16[512,2048]{1,0:T(8,128)(2,1)}, u32[]{:S(2)}, u32[]{:S(2)}) collective-permute-start(bf16[512,2048]{1,0:T(8,128)(2,1)S(1)} %copy-done.23), channel_id=1, source_target_pairs={{0,2},{1,3},{2,0},{3,1},{4,6},{5,7},{6,4},{7,5},{8,10},{9,11},{10,... | collective-permute-start | bytes 6291464 | tf_op jit(solution)/shard_map/ppermute | solution.py:347
  229.7 76.2 %collective-permute-start.7 = (bf16[1024,1536]{1,0:T(8,128)(2,1)}, bf16[1024,1536]{1,0:T(8,128)(2,1)}, u32[]{:S(2)}, u32[]{:S(2)}) collective-permute-start(bf16[1024,1536]{1,0:T(8,128)(2,1)} %all-gather.6.cloned.1.call-done), channel_id=1, source_target_pairs={{0,4},{4,0},{8,12},{12,8},{16,20},{20,16},{24,28},{28,24},{1,5},{5... | collective-permute-start | bytes 9437192 | tf_op jit(solution)/shard_map/ppermute | solution.py:347
  382.8 423.3 %reduce-scatter.7.cloned.1.call-start = ((), (), s32[]{:S(2)}) async-start(), calls=%async_computation.21 | async-start | bytes 3604480 | tf_op jit(solution)/shard_map/reduce_scatter | solution.py:390
  382.8 127.1 %collective-permute-start.17 = (bf16[1024,2816]{1,0:T(8,128)(2,1)}, bf16[1024,2816]{1,0:T(8,128)(2,1)}, u32[]{:S(2)}, u32[]{:S(2)}) collective-permute-start(bf16[1024,2816]{1,0:T(8,128)(2,1)} %all-gather.12.cloned.1.call-done), channel_id=1, source_target_pairs={{0,4},{4,0},{8,12},{12,8},{16,20},{20,16},{24,28},{28,24},{1,5},{5... | collective-permute-start | bytes 17301512 | tf_op jit(solution)/shard_map/ppermute | solution.py:347
  448.1 66.5 %collective-permute-start.18 = (bf16[512,2048]{1,0:T(8,128)(2,1)S(1)}, bf16[512,2048]{1,0:T(8,128)(2,1)}, u32[]{:S(2)}, u32[]{:S(2)}) collective-permute-start(bf16[512,2048]{1,0:T(8,128)(2,1)S(1)} %multiply_convert_fusion.6), channel_id=1, source_target_pairs={{0,2},{1,3},{2,0},{3,1},{4,6},{5,7},{6,4},{7,5},{8,10},{9,11},{10,... | collective-permute-start | bytes 6291464 | tf_op jit(solution)/shard_map/ppermute | solution.py:347
  448.4 66.1 %collective-permute-start.16 = (bf16[512,2048]{1,0:T(8,128)(2,1)S(1)}, bf16[512,2048]{1,0:T(8,128)(2,1)}, u32[]{:S(2)}, u32[]{:S(2)}) collective-permute-start(bf16[512,2048]{1,0:T(8,128)(2,1)S(1)} %multiply_convert_fusion.6), channel_id=1, source_target_pairs={{0,1},{1,0},{2,3},{3,2},{4,5},{5,4},{6,7},{7,6},{8,9},{9,8},{10,11... | collective-permute-start | bytes 6291464 | tf_op jit(solution)/shard_map/ppermute | solution.py:347
  637.8 68.3 %collective-permute-start.22 = (bf16[512,2048]{1,0:T(8,128)(2,1)}, bf16[512,2048]{1,0:T(8,128)(2,1)}, u32[]{:S(2)}, u32[]{:S(2)}) collective-permute-start(bf16[512,2048]{1,0:T(8,128)(2,1)} %fusion.24), channel_id=1, source_target_pairs={{0,2},{1,3},{2,0},{3,1},{4,6},{5,7},{6,4},{7,5},{8,10},{9,11},{10,... | collective-permute-start | bytes 6291464 | tf_op jit(solution)/shard_map/ppermute | solution.py:347
  719.3 177.0 %reduce-scatter.9.cloned.1.call-start = ((), (), s32[]{:S(2)}) async-start(), calls=%async_computation.22 | async-start | bytes 3604480 | tf_op jit(solution)/shard_map/reduce_scatter | solution.py:390
  783.3 99.5 %collective-permute-start.28 = (bf16[1024,1408]{1,0:T(8,128)(2,1)}, bf16[1024,1408]{1,0:T(8,128)(2,1)}, u32[]{:S(2)}, u32[]{:S(2)}) collective-permute-start(bf16[1024,1408]{1,0:T(8,128)(2,1)} %convolution_convert_fusion.1), channel_id=1, source_target_pairs={{0,4},{4,0},{8,12},{12,8},{16,20},{20,16},{24,28},{28,24},{1,5},{5... | collective-permute-start | bytes 8650760 | tf_op jit(solution)/shard_map/ppermute | solution.py:347
  842.1 95.1 %collective-permute-start.29 = (bf16[1024,1024]{1,0:T(8,128)(2,1)}, bf16[1024,1024]{1,0:T(8,128)(2,1)S(1)}, u32[]{:S(2)}, u32[]{:S(2)}) collective-permute-start(bf16[1024,1024]{1,0:T(8,128)(2,1)} %fusion.64), channel_id=1, source_target_pairs={{0,4},{4,0},{8,12},{12,8},{16,20},{20,16},{24,28},{28,24},{1,5},{5... | collective-permute-start | bytes 6291464 | tf_op jit(solution)/shard_map/ppermute | solution.py:347
  882.0 80.7 %reduce-scatter.11.cloned.1.call-start = ((), (), s32[]{:S(2)}) async-start(), calls=%async_computation.23 | async-start | bytes 3604480 | tf_op jit(solution)/shard_map/reduce_scatter | solution.py:390
  907.6 126.1 %collective-permute-start.31 = (bf16[1024,1536]{1,0:T(8,128)(2,1)}, bf16[1024,1536]{1,0:T(8,128)(2,1)}, u32[]{:S(2)}, u32[]{:S(2)}) collective-permute-start(bf16[1024,1536]{1,0:T(8,128)(2,1)} %convolution_convert_fusion), channel_id=1, source_target_pairs={{0,4},{4,0},{8,12},{12,8},{16,20},{20,16},{24,28},{28,24},{1,5},{5... | collective-permute-start | bytes 9437192 | tf_op jit(solution)/shard_map/ppermute | solution.py:347
  949.2 65.9 %reduce-scatter.13.cloned.1.call-start = ((), (), s32[]{:S(2)}) async-start(), calls=%async_computation.24 | async-start | bytes 2621440 | tf_op jit(solution)/shard_map/reduce_scatter | solution.py:390
  962.1 123.9 %collective-permute-start.32 = (bf16[1024,1664]{1,0:T(8,128)(2,1)}, bf16[1024,1664]{1,0:T(8,128)(2,1)}, u32[]{:S(2)}, u32[]{:S(2)}) collective-permute-start(bf16[1024,1664]{1,0:T(8,128)(2,1)} %convolution_convert_fusion.3), channel_id=1, source_target_pairs={{0,4},{4,0},{8,12},{12,8},{16,20},{20,16},{24,28},{28,24},{1,5},{5... | collective-permute-start | bytes 10223624 | tf_op jit(solution)/shard_map/ppermute | solution.py:347
  1018.5 101.5 %reduce-scatter.15.cloned.1.call-start = ((), (), s32[]{:S(2)}) async-start(), calls=%async_computation.25 | async-start | bytes 3932160 | tf_op jit(solution)/shard_map/reduce_scatter | solution.py:390
  1059.3 128.4 %reduce-scatter.17.cloned.1.call-start = ((), (), s32[]{:S(2)}) async-start(), calls=%async_computation.26 | async-start | bytes 4259840 | tf_op jit(solution)/shard_map/reduce_scatter | solution.py:390
  (161 other events, 3950.2 us)
Sparse Core Ops, SparseCore 0:
  55.4 69.8 all-gather.7
  126.8 62.0 all-gather.5
  191.1 44.5 all-gather.9
  237.7 105.4 all-gather.11
  382.9 104.2 all-gather.13
  719.4 53.5 reduce-scatter.6
  794.8 53.2 reduce-scatter.8
  895.0 54.8 reduce-scatter.10
  962.8 42.5 reduce-scatter.12
  1059.4 57.5 reduce-scatter.14
  1120.2 66.1 reduce-scatter.16

commit v7 on v6

--- a/solution.py
+++ b/solution.py
@@ -523,16 +523,22 @@
         every = jnp.concatenate([every_near, every_far], axis=0)
         ids_all = jnp.concatenate(join_tokens(segments[:, None], R)[:2], axis=0).reshape(ns, SEQ)
         part_r = spread(quarter([w_out.T, w_ffgate, w_ffup, w_down.T]), extra_all, every_got, line_1)
-        part_b, part_gu, part_d = part_r[:, :wv], part_r[:, wv : wv + 2 * ffq], part_r[:, wv + 2 * ffq :]
+        gains = mix(extra_all[:2], 1)
+        gain_first, gain_second = gains[0:1], gains[1:2]
+        every32 = every.astype(f32)
+        normed_one = (every32 * rms(every32) * gain_first).astype(bf16)
+        part_r = after(part_r, normed_one)
+        part_b, part_g, part_u, part_d = (
+            part_r[:, :wv], part_r[:, wv : wv + ffq], part_r[:, wv + ffq : wv + 2 * ffq], part_r[:, wv + 2 * ffq :])
         line_2 = gather_line(after(part_2, extra_all), F)
         wa1, side_1 = gather_side(line_1, F)
         cot = mix(cotangent, 1)
         cot_near, cot_far, unused = join_tokens(after(cot, side_1), R)
         line_b = gather_line(part_b, F)
-        line_gu = gather_line(part_gu, F)
-
-        gains = mix(extra_all[:2], 1)
-        gain_first, gain_second = gains[0:1], gains[1:2]
+        line_g = gather_line(after(part_g, side_1), F)
+        wu, line_u, got_u = gather_side_first(part_u, F, side_1)
+        line_d = gather_line(after(part_d, side_1), F)
+
         cq = lax.dynamic_slice_in_dim(extra_all[2:6], r * wq, wq, axis=1)
         ck = lax.dynamic_slice_in_dim(extra_all[6:10], r * wq, wq, axis=1)
         cv = extra_all[10 : 10 + 4 * per].reshape(4, per, D).transpose(0, 2, 1).reshape(4, D * per)
@@ -546,20 +552,17 @@
         same = (ids_all[:, :, None] == ids_all[:, None, :]) & (place[:, None] >= place[None, :])[None]
         pos = (jnp.sum(same.astype(f32), axis=2) - 1.0).reshape(tok, 1)
 
-        every32 = every.astype(f32)
-        normed_one = (every32 * rms(every32) * gain_first).astype(bf16)
-        proj_1 = dot(after(normed_one, line_2, part_r), wa1)
+        proj_1 = dot(after(normed_one, part_r), wa1)
         mixed, x_1, u_1, o_1 = mixer_fwd(proj_1, proj_1, pos, taps[0], gain_out, prm, dims, 0)
         wa2, side_2 = gather_side(line_2, F, side_1)
-        proj_2 = dot(after(normed_one, mixed, line_b), wa2)
+        proj_2 = dot(after(normed_one, mixed, line_b, got_u), wa2)
         mixed, *saved_2 = mixer_fwd(proj_2, proj_1, pos, taps[1], gain_out, prm, dims, 1, 1, [mixed])
-        wd, line_d, got_d = gather_side_first(part_d, F, side_2)
         wb, side_b = gather_side(line_b, F, side_2)
-        side_gu = xor_send(after(line_gu, side_b), "fsdp", F, 1)
-        wg, wu = (jnp.concatenate([line_gu[:, at : at + ffq], side_gu[:, at : at + ffq]], axis=0) for at in (0, ffq))
+        wg, side_g = gather_side(line_g, F, side_b)
+        wd, side_d = gather_side(line_d, F, side_g)
         own32 = own.astype(f32)
         mid = tok // 2
-        mixed = after(mixed, line_gu, got_d, cot_near, cot_far)
+        mixed = after(mixed, line_g, cot_near, cot_far)
         out_far = dot(mixed[mid:], wb, NT)
         kept = {}
 
@@ -574,15 +577,15 @@
 
         added, unused = sum_tokens(lambda: out_far, near_mixed, R, last=True)
         mixed, saved_2 = kept["mixed"], kept["saved"]
-        middle = own32 + added
+        middle = own32 + after(added, side_g)
         r2 = rms(middle)
         n2 = middle * r2
         normed_own = (n2 * gain_second).astype(bf16)
         two = join_tokens(normed_own, R)[:2]
         gates, ups, acts, sigs, hiddens = [], [], [], [], []
-        for normed in two:
+        for normed in (after(two[0], line_u), two[1]):
             gates.append(dot(normed, wg))
-            ups.append(dot(after(normed, gates[-1], line_d) if ups else normed, wu))
+            ups.append(dot(after(normed, gates[-1], side_d) if ups else normed, wu))
             sigs.append(jax.nn.sigmoid(gates[-1]))
             acts.append(gates[-1] * sigs[-1])
             hiddens.append((acts[-1] * ups[-1]).astype(bf16))
@@ -632,9 +635,9 @@
         t_out = g_out.total(R)
 
         def near_one(part):
-            g_2.side(part, g_out.sum)
-
-            keep("far", dot(after(hiddens[1], g_2.low, t_up), wd, NT))
+            g_2.side(part, before=(g_out.sum,))
+
+            keep("far", dot(after(hiddens[1], g_2.low, g_out.sum, t_up), wd, NT))
             return keep("one", back_one(0, mid, kept["far"]))
 
         dnormed_one, far_one = sum_tokens(lambda: back_one(mid, tok, g_1.sent, g_up.sum, t_gate), near_one, R)

time: 1240 us -> 1250 us (level)
  waiting for transfers between devices: 229 us -> 267 us
  local copies, waits for them, and re-layouts: 230 us -> 215 us
  matrix products: 383 us -> 369 us
    ppermute x38 -> x39, waiting for transfers between devices: 115 us -> 161 us  [xor_send(): return lax.ppermute(value, axis, [(i, i ^ step) for i in range(size)])]
    all_to_all x1, waiting for transfers between devices: 5.18 us -> 23.1 us  [on_device(): lax.all_to_all(jnp.broadcast_to(after(extra, part_a)[None], (N, *extra.sh...]
    all_to_all x2, waiting for transfers between devices: 26.8 us -> 9.3 us  [spread(): return lax.all_to_all(packed, 'rep', 0, 0).reshape(R * shard, -1)]
    dot_general x34, matrix products: 383 us -> 369 us  [dot(): lax.dot_general(left, right, dims, preferred_element_type=f32).astype(out)]
    all_gather x5 -> x6, waiting for transfers between devices: 35.8 us -> 32.8 us  [gather_line(): lax.all_gather(rows, 'fsdp', axis=0, tiled=True, axis_index_groups=lines(...]
    unnamed x321 -> x307, local copies, waits for them, and re-layouts: 98 us -> 97.1 us
  transfers between devices with their start and end apart: 59 -> 61, of which waited for: 20 -> 21; matrix products, arithmetic and copies ran while one was open for 47% -> 46% of each run, Pallas kernels for 15% -> 15%
where the time goes in v7:
time: 1250 us; the launch traced here: 1240 us
  matrix products  369 us (30%)
  waiting for transfers between devices  267 us (21%)
  local copies, waits for them, and re-layouts  215 us (17%)
  Pallas kernels  184 us (15%)
  other arithmetic  124 us (10%)
  starting transfers between devices  65.1 us (5%)
  between operations  16.5 us (1%)
    dot_general x34, matrix products, dot(): lax.dot_general(left, right, dims, preferred_element_type=f32).astype(out)  369 us
    ppermute x39, waiting for transfers between devices, xor_send(): return lax.ppermute(value, axis, [(i, i ^ step) for i in range(size)])  161 us
    pallas_call x4, Pallas kernels, mixer_bwd(): pl.pallas_call(functools.partial(bwd_kernel, dims, half, before is not No...  111 us
    unnamed x307, local copies, waits for them, and re-layouts  97.1 us
    pallas_call x3, Pallas kernels, mixer_fwd(): pl.pallas_call(functools.partial(fwd_kernel, dims, half), grid=(steps,),...  72.7 us
    all_gather x6, waiting for transfers between devices, gather_line(): lax.all_gather(rows, 'fsdp', axis=0, tiled=True, axis_index_groups=lines(...  32.8 us
    all_to_all x1, waiting for transfers between devices, on_device(): summed = jnp.sum(lax.all_to_all(packed, both, 0, 0, tiled=True), axis=0)  26 us
  transfers between devices with their start and end apart: 61, of which 21 were waited for; matrix products, arithmetic and copies ran while one was open for 46% of the time, Pallas kernels for 15%

profile of v7, /device:TPU:0, one launch (start us, length us, event | category | flops | bytes accessed | tf_op | source)
XLA Modules:
  0.0 1240.9 jit_solution(17981164717120227142)
XLA Ops:
  70.1 23.1 %all-to-all-done.1 = bf16[32,2,608]{2,1,0:T(2,128)(2,1)S(1)} async-done(((bf16[32,2,608]{2,1,0:T(2,128)(2,1)}), bf16[32,2,608]{2,1,0:T(2,128)(2,1)S(1)}, u32[]{:S(2)}, u32[]{:S(2)}) %all-to-all-start.1) | async-done | bytes 77856 | tf_op jit(solution)/shard_map/all_to_all | solution.py:519
  104.1 12.0 all-gather.7.cloned.1.call-done
  161.3 50.5 %collective-permute-done.3 = bf16[1024,1664]{1,0:T(8,128)(2,1)} collective-permute-done((bf16[1024,1664]{1,0:T(8,128)(2,1)}, bf16[1024,1664]{1,0:T(8,128)(2,1)}, u32[]{:S(2)}, u32[]{:S(2)}) %collective-permute-start.3) | collective-permute-done | bytes 3407904 | tf_op jit(solution)/shard_map/ppermute | solution.py:347
  239.6 21.2 %fusion.84.refs_0_.refs_1_.refs_2_.refs_3_.refs_4_ = f32[2048,1664]{1,0:T(8,128)} fusion(bf16[2048,2048]{1,0:T(8,128)(2,1)} %fusion.2, bf16[2048,1664]{1,0:T(8,128)(2,1)} %constant_dynamic-update-slice_fusion.13), kind=kOutput, calls=%fused_computation.280 | convolution fusion | flops 13958643712 | bytes 28835840 | tf_op jit(solution)/shard_map/dot_general | solution.py:375
  263.3 34.4 %shard_map.356 = (bf16[2048,1024]{1,0:T(8,128)(2,1)S(1)}, f32[16,256,256]{2,1,0:T(8,128)}, f32[2048,512]{1,0:T(8,128)}, f32[2048,512]{1,0:T(8,128)}) custom-call(f32[2048,1664]{1,0:T(8,128)} %fusion.84.refs_0_.refs_1_.refs_2_.refs_3_.refs_4_, f32[2048,1664]{1,0:T(8,128)} %fusion.84.refs_0_.refs_1_.refs_2_.refs_3_.refs_4_, ...), custom_call_target="tpu_custom_call" | custom-call | flops 4400000000 | bytes 4000000 | tf_op jit(solution)/shard_map/pallas_call | solution.py:277
  324.6 17.5 %fusion.85.refs_0_.refs_1_.refs_2_.refs_3_ = f32[2048,1536]{1,0:T(8,128)} fusion(bf16[2048,2048]{1,0:T(8,128)(2,1)S(1)} %bitcast.177, bf16[2048,1536]{1,0:T(8,128)(2,1)} %constant_dynamic-update-slice_fusion.15), kind=kOutput, calls=%fused_computation.281 | convolution fusion | flops 12884901888 | bytes 27262976 | tf_op jit(solution)/shard_map/dot_general | solution.py:375
  342.2 18.8 %shard_map.357 = (bf16[2048,1024]{1,0:T(8,128)(2,1)S(1)}, f32[16,256,256]{2,1,0:T(8,128)}, f32[2048,512]{1,0:T(8,128)}, f32[2048,512]{1,0:T(8,128)}) custom-call(f32[2048,1536]{1,0:T(8,128)} %fusion.85.refs_0_.refs_1_.refs_2_.refs_3_, f32[2048,1536]{1,0:T(8,128)} %fusion.85.refs_0_.refs_1_.refs_2_.refs_3_, ...), custom_call_target="tpu_custom_call", output_to_operand_aliasing={{0}: (9, {})} | custom-call | flops 13200000000 | bytes 12000000 | tf_op jit(solution)/shard_map/pallas_call | solution.py:277
  393.0 19.5 %shard_map.358 = (bf16[2048,1024]{1,0:T(8,128)(2,1)S(1)}, f32[16,256,256]{2,1,0:T(8,128)}, f32[2048,512]{1,0:T(8,128)}, f32[2048,512]{1,0:T(8,128)}) custom-call(f32[2048,1536]{1,0:T(8,128)} %fusion.85.refs_0_.refs_1_.refs_2_.refs_3_, ...), custom_call_target="tpu_custom_call", output_to_operand_aliasing={{0}: (9, {}), {1}: (10, {}), {2}: (11, {}), {3}: (12, {})} | custom-call | flops 13200000000 | bytes 12000000 | tf_op jit(solution)/shard_map/pallas_call | solution.py:277
  421.1 16.4 %collective-permute-done.14 = bf16[512,2048]{1,0:T(8,128)(2,1)} collective-permute-done((bf16[512,2048]{1,0:T(8,128)(2,1)}, bf16[512,2048]{1,0:T(8,128)(2,1)}, u32[]{:S(2)}, u32[]{:S(2)}) %collective-permute-start.14) | collective-permute-done | bytes 2097184 | tf_op jit(solution)/shard_map/ppermute | solution.py:347
  467.1 20.7 %all-gather.15.cloned.1.call-done = bf16[2048,1408]{1,0:T(8,128)(2,1)} async-done(((bf16[512,1408]{1,0:T(8,128)(2,1)}), bf16[2048,1408]{1,0:T(8,128)(2,1)}) %all-gather.15.cloned.1.call-update) | async-done | bytes 5767184 | tf_op jit(solution)/shard_map/all_gather | solution.py:359
  491.0 20.6 %collective-permute-done.20 = bf16[1024,1408]{1,0:T(8,128)(2,1)} collective-permute-done((bf16[1024,1408]{1,0:T(8,128)(2,1)}, bf16[1024,1408]{1,0:T(8,128)(2,1)}, u32[]{:S(2)}, u32[]{:S(2)}) %collective-permute-start.20) | collective-permute-done | bytes 2883616 | tf_op jit(solution)/shard_map/ppermute | solution.py:347
  526.8 33.9 %collective-permute-done.18 = bf16[512,2048]{1,0:T(8,128)(2,1)S(1)} collective-permute-done((bf16[512,2048]{1,0:T(8,128)(2,1)S(1)}, bf16[512,2048]{1,0:T(8,128)(2,1)S(1)}, u32[]{:S(2)}, u32[]{:S(2)}) %collective-permute-start.18) | collective-permute-done | bytes 2097184 | tf_op jit(solution)/shard_map/ppermute | solution.py:347
  584.2 12.0 multiply_convert_fusion.4
  607.2 13.0 %multiply_convert_fusion.3 = (bf16[1024,1408]{1,0:T(8,128)(2,1)S(1)}, bf16[1024,1408]{1,0:T(8,128)(2,1)S(1)}) fusion(f32[1024,1408]{1,0:T(8,128)} %copy-done.98, f32[1024,1408]{1,0:T(8,128)} %get-tuple-element.257, bf16[1024,2048]{1,0:T(8,128)(2,1)} %get-tuple-element.131, bf16[2048,1408]{1,0:T(8,128)(2,1)S(1)} %bitcast.198), kind=kOutput, calls=%fused_computation.25 | convolution fusion | flops 5924323328 | bytes 27262976 | tf_op jit(solution)/shard_map/dot_general | solution.py:375
  660.5 14.3 %multiply_convert_fusion.1 = (bf16[1024,1408]{1,0:T(8,128)(2,1)S(1)}, bf16[1024,1408]{1,0:T(8,128)(2,1)S(1)}) fusion(f32[1024,1408]{1,0:T(8,128)} %copy-done.97, f32[1024,1408]{1,0:T(8,128)} %get-tuple-element.255, bf16[1024,2048]{1,0:T(8,128)(2,1)} %get-tuple-element.132, bf16[2048,1408]{1,0:T(8,128)(2,1)} %constant_dynamic-update-slice_fusion.31), kind=kOutput, calls=%fused_computation.23 | convolution fusion | flops 5924323328 | bytes 27262976 | tf_op jit(solution)/shard_map/dot_general | solution.py:375
  758.6 27.7 %shard_map.359 = (bf16[2048,1536]{1,0:T(8,128)(2,1)}, f32[2048,128]{1,0:T(8,128)}, f32[4,1024]{1,0:T(4,128)}, f32[1,256]{1,0:T(1,128)}, f32[8,128]{1,0:T(8,128)}) custom-call(f32[2048,1536]{1,0:T(8,128)} %fusion.85.refs_0_.refs_1_.refs_2_.refs_3_, f32[2048,1536]{1,0:T(8,128)} %fusion.85.refs_0_.refs_1_.refs_2_.refs_3_, ...), custom_call_target="tpu_custom_call" | custom-call | flops 28600000512 | bytes 26000000 | tf_op jit(solution)/shard_map/pallas_call | solution.py:322
  835.9 27.9 %shard_map.360 = (bf16[2048,1664]{1,0:T(8,128)(2,1)}, f32[2048,128]{1,0:T(8,128)}, f32[4,1024]{1,0:T(4,128)}, f32[1,256]{1,0:T(1,128)}, f32[8,128]{1,0:T(8,128)}) custom-call(f32[2048,1664]{1,0:T(8,128)} %fusion.84.refs_0_.refs_1_.refs_2_.refs_3_.refs_4_, f32[2048,1664]{1,0:T(8,128)} %fusion.84.refs_0_.refs_1_.refs_2_.refs_3_.refs_4_, ...), custom_call_target="tpu_custom_call" | custom-call | flops 28600000512 | bytes 26000000 | tf_op jit(solution)/shard_map/pallas_call | solution.py:322
  879.0 27.6 %shard_map.361 = (bf16[2048,1536]{1,0:T(8,128)(2,1)}, f32[2048,128]{1,0:T(8,128)}, f32[4,1024]{1,0:T(4,128)}, f32[1,256]{1,0:T(1,128)}, f32[8,128]{1,0:T(8,128)}) custom-call(f32[2048,1536]{1,0:T(8,128)} %fusion.85.refs_0_.refs_1_.refs_2_.refs_3_, ...), custom_call_target="tpu_custom_call", output_to_operand_aliasing={{0}: (13, {}), {1}: (14, {})} | custom-call | flops 28600000512 | bytes 26000000 | tf_op jit(solution)/shard_map/pallas_call | solution.py:322
  936.6 27.9 %shard_map.362 = (bf16[2048,1664]{1,0:T(8,128)(2,1)}, f32[2048,128]{1,0:T(8,128)}, f32[4,1024]{1,0:T(4,128)}, f32[1,256]{1,0:T(1,128)}, f32[8,128]{1,0:T(8,128)}) custom-call(f32[2048,1664]{1,0:T(8,128)} %fusion.84.refs_0_.refs_1_.refs_2_.refs_3_.refs_4_, ...), custom_call_target="tpu_custom_call", output_to_operand_aliasing={{0}: (14, {}), {1}: (15, {})} | custom-call | flops 28600000512 | bytes 26000000 | tf_op jit(solution)/shard_map/pallas_call | solution.py:322
  973.1 12.9 %convolution_convert_fusion.3 = bf16[1024,1664]{1,0:T(8,128)(2,1)} fusion(bf16[2048,1664]{1,0:T(8,128)(2,1)} %get-tuple-element.165, bf16[2048,2048]{1,0:T(8,128)(2,1)} %fusion.2), kind=kOutput, calls=%fused_computation.90 | convolution fusion | flops 6981025792 | bytes 14417920 | tf_op jit(solution)/shard_map/dot_general | solution.py:375
  997.8 12.3 convolution_add_fusion.1
  1053.6 12.1 add_convert_fusion.1
  1091.7 14.4 %convolution_add_fusion = f32[1024,2048]{1,0:T(8,128)} fusion(f32[1024,2048]{1,0:T(8,128)} %fusion.52, bf16[2048,1664]{1,0:T(8,128)(2,1)} %constant_dynamic-update-slice_fusion.13, bf16[2048,1664]{1,0:T(8,128)(2,1)} %get-tuple-element.165), kind=kOutput, calls=%fused_computation.82 | convolution fusion | flops 6981419008 | bytes 27000832 | tf_op jit(solution)/shard_map/dot_general | solution.py:375
  1162.0 26.0 %all-to-all-done.7 = f32[32,1,1192]{2,1,0:T(1,128)S(1)} async-done(((f32[32,1,1192]{2,1,0:T(1,128)}), f32[32,1,1192]{2,1,0:T(1,128)S(1)}, u32[]{:S(2)}, u32[]{:S(2)}) %all-to-all-start.7) | async-done | bytes 152608 | tf_op jit(solution)/shard_map/all_to_all | solution.py:689
  (648 shorter events, 707.5 us)
Async XLA Ops:
  20.9 95.3 %all-gather.7.cloned.1.call-start = ((), (), s32[]{:S(2)}) async-start(), calls=%async_computation.16 | async-start | bytes 4259840 | tf_op jit(solution)/shard_map/all_gather | solution.py:359
  46.5 78.4 %collective-permute-start = (bf16[512,2048]{1,0:T(8,128)(2,1)}, bf16[512,2048]{1,0:T(8,128)(2,1)}, u32[]{:S(2)}, u32[]{:S(2)}) collective-permute-start(bf16[512,2048]{1,0:T(8,128)(2,1)} %pad_maximum_fusion.8), channel_id=1, source_target_pairs={{0,1},{1,0},{2,3},{3,2},{4,5},{5,4},{6,7},{7,6},{8,9},{9,8},{10,11... | collective-permute-start | bytes 6291464 | tf_op jit(solution)/shard_map/ppermute | solution.py:347
  62.9 160.7 %all-gather.11.cloned.1.call-start = ((), (), s32[]{:S(2)}) async-start(), calls=%async_computation.18 | async-start | bytes 3932160 | tf_op jit(solution)/shard_map/all_gather | solution.py:359
  124.3 175.6 %all-gather.9.cloned.1.call-start = ((), (), s32[]{:S(2)}) async-start(), calls=%async_computation.17 | async-start | bytes 2621440 | tf_op jit(solution)/shard_map/all_gather | solution.py:359
  135.4 76.4 %collective-permute-start.3 = (bf16[1024,1664]{1,0:T(8,128)(2,1)}, bf16[1024,1664]{1,0:T(8,128)(2,1)}, u32[]{:S(2)}, u32[]{:S(2)}) collective-permute-start(bf16[1024,1664]{1,0:T(8,128)(2,1)} %all-gather.7.cloned.1.call-done), channel_id=1, source_target_pairs={{0,4},{4,0},{8,12},{12,8},{16,20},{20,16},{24,28},{28,24},{1,5},{5... | collective-permute-start | bytes 10223624 | tf_op jit(solution)/shard_map/ppermute | solution.py:347
  158.3 208.8 %all-gather.13.cloned.1.call-start = ((), (), s32[]{:S(2)}) async-start(), calls=%async_computation.19 | async-start | bytes 3604480 | tf_op jit(solution)/shard_map/all_gather | solution.py:359
  211.9 225.6 %all-gather.17.cloned.1.call-start = ((), (), s32[]{:S(2)}) async-start(), calls=%async_computation.21 | async-start | bytes 3604480 | tf_op jit(solution)/shard_map/all_gather | solution.py:359
  231.5 71.5 %collective-permute-start.10 = (bf16[512,2048]{1,0:T(8,128)(2,1)S(1)}, bf16[512,2048]{1,0:T(8,128)(2,1)}, u32[]{:S(2)}, u32[]{:S(2)}) collective-permute-start(bf16[512,2048]{1,0:T(8,128)(2,1)S(1)} %copy-done.25), channel_id=1, source_target_pairs={{0,2},{1,3},{2,0},{3,1},{4,6},{5,7},{6,4},{7,5},{8,10},{9,11},{10,... | collective-permute-start | bytes 6291464 | tf_op jit(solution)/shard_map/ppermute | solution.py:347
  233.2 69.8 %collective-permute-start.9 = (bf16[512,2048]{1,0:T(8,128)(2,1)S(1)}, bf16[512,2048]{1,0:T(8,128)(2,1)}, u32[]{:S(2)}, u32[]{:S(2)}) collective-permute-start(bf16[512,2048]{1,0:T(8,128)(2,1)S(1)} %copy-done.25), channel_id=1, source_target_pairs={{0,1},{1,0},{2,3},{3,2},{4,5},{5,4},{6,7},{7,6},{8,9},{9,8},{10,11... | collective-permute-start | bytes 6291464 | tf_op jit(solution)/shard_map/ppermute | solution.py:347
  234.6 84.8 %collective-permute-start.8 = (bf16[1024,1536]{1,0:T(8,128)(2,1)}, bf16[1024,1536]{1,0:T(8,128)(2,1)}, u32[]{:S(2)}, u32[]{:S(2)}) collective-permute-start(bf16[1024,1536]{1,0:T(8,128)(2,1)} %all-gather.11.cloned.1.call-done), channel_id=1, source_target_pairs={{0,4},{4,0},{8,12},{12,8},{16,20},{20,16},{24,28},{28,24},{1,5},{5... | collective-permute-start | bytes 9437192 | tf_op jit(solution)/shard_map/ppermute | solution.py:347
  235.2 252.6 %all-gather.15.cloned.1.call-start = ((), (), s32[]{:S(2)}) async-start(), calls=%async_computation.20 | async-start | bytes 7208960 | tf_op jit(solution)/shard_map/all_gather | solution.py:359
  383.4 449.0 %reduce-scatter.7.cloned.1.call-start = ((), (), s32[]{:S(2)}) async-start(), calls=%async_computation.22 | async-start | bytes 3604480 | tf_op jit(solution)/shard_map/reduce_scatter | solution.py:390
  660.1 72.2 %collective-permute-start.23 = (bf16[512,2048]{1,0:T(8,128)(2,1)}, bf16[512,2048]{1,0:T(8,128)(2,1)}, u32[]{:S(2)}, u32[]{:S(2)}) collective-permute-start(bf16[512,2048]{1,0:T(8,128)(2,1)} %fusion.24), channel_id=1, source_target_pairs={{0,2},{1,3},{2,0},{3,1},{4,6},{5,7},{6,4},{7,5},{8,10},{9,11},{10,... | collective-permute-start | bytes 6291464 | tf_op jit(solution)/shard_map/ppermute | solution.py:347
  745.5 174.5 %reduce-scatter.9.cloned.1.call-start = ((), (), s32[]{:S(2)}) async-start(), calls=%async_computation.23 | async-start | bytes 3604480 | tf_op jit(solution)/shard_map/reduce_scatter | solution.py:390
  809.8 98.1 %collective-permute-start.29 = (bf16[1024,1408]{1,0:T(8,128)(2,1)}, bf16[1024,1408]{1,0:T(8,128)(2,1)}, u32[]{:S(2)}, u32[]{:S(2)}) collective-permute-start(bf16[1024,1408]{1,0:T(8,128)(2,1)} %convolution_convert_fusion.1), channel_id=1, source_target_pairs={{0,4},{4,0},{8,12},{12,8},{16,20},{20,16},{24,28},{28,24},{1,5},{5... | collective-permute-start | bytes 8650760 | tf_op jit(solution)/shard_map/ppermute | solution.py:347
  832.4 86.4 %all-to-all-start.3 = ((bf16[4,64,1408]{2,1,0:T(8,128)(2,1)}), bf16[4,64,1408]{2,1,0:T(8,128)(2,1)S(1)}, u32[]{:S(2)}, u32[]{:S(2)}) async-start(bf16[4,64,1408]{2,1,0:T(8,128)(2,1)} %bitcast.206), calls=%async_computation.5 | async-start | bytes 1441792 | tf_op jit(solution)/shard_map/all_to_all | solution.py:393
  835.9 150.1 %reduce-scatter.11.cloned.1.call-start = ((), (), s32[]{:S(2)}) async-start(), calls=%async_computation.24 | async-start | bytes 3604480 | tf_op jit(solution)/shard_map/reduce_scatter | solution.py:390
  872.0 92.4 %collective-permute-start.30 = (bf16[1024,1024]{1,0:T(8,128)(2,1)}, bf16[1024,1024]{1,0:T(8,128)(2,1)}, u32[]{:S(2)}, u32[]{:S(2)}) collective-permute-start(bf16[1024,1024]{1,0:T(8,128)(2,1)} %fusion.62), channel_id=1, source_target_pairs={{0,4},{4,0},{8,12},{12,8},{16,20},{20,16},{24,28},{28,24},{1,5},{5... | collective-permute-start | bytes 6291464 | tf_op jit(solution)/shard_map/ppermute | solution.py:347
  923.6 111.2 %reduce-scatter.13.cloned.1.call-start = ((), (), s32[]{:S(2)}) async-start(), calls=%async_computation.25 | async-start | bytes 2621440 | tf_op jit(solution)/shard_map/reduce_scatter | solution.py:390
  935.1 118.5 %collective-permute-start.32 = (bf16[1024,1536]{1,0:T(8,128)(2,1)}, bf16[1024,1536]{1,0:T(8,128)(2,1)}, u32[]{:S(2)}, u32[]{:S(2)}) collective-permute-start(bf16[1024,1536]{1,0:T(8,128)(2,1)} %convolution_convert_fusion), channel_id=1, source_target_pairs={{0,4},{4,0},{8,12},{12,8},{16,20},{20,16},{24,28},{28,24},{1,5},{5... | collective-permute-start | bytes 9437192 | tf_op jit(solution)/shard_map/ppermute | solution.py:347
  1013.9 92.2 %collective-permute-start.33 = (bf16[1024,1664]{1,0:T(8,128)(2,1)}, bf16[1024,1664]{1,0:T(8,128)(2,1)}, u32[]{:S(2)}, u32[]{:S(2)}) collective-permute-start(bf16[1024,1664]{1,0:T(8,128)(2,1)} %convolution_convert_fusion.3), channel_id=1, source_target_pairs={{0,4},{4,0},{8,12},{12,8},{16,20},{20,16},{24,28},{28,24},{1,5},{5... | collective-permute-start | bytes 10223624 | tf_op jit(solution)/shard_map/ppermute | solution.py:347
  1038.2 101.5 %reduce-scatter.15.cloned.1.call-start = ((), (), s32[]{:S(2)}) async-start(), calls=%async_computation.26 | async-start | bytes 3932160 | tf_op jit(solution)/shard_map/reduce_scatter | solution.py:390
  1053.2 86.6 %collective-permute-start.38 = (bf16[512,2048]{1,0:T(8,128)(2,1)}, bf16[512,2048]{1,0:T(8,128)(2,1)}, u32[]{:S(2)}, u32[]{:S(2)}) collective-permute-start(bf16[512,2048]{1,0:T(8,128)(2,1)} %fusion.17), channel_id=1, source_target_pairs={{0,2},{1,3},{2,0},{3,1},{4,6},{5,7},{6,4},{7,5},{8,10},{9,11},{10,... | collective-permute-start | bytes 6291464 | tf_op jit(solution)/shard_map/ppermute | solution.py:347
  1079.4 128.2 %reduce-scatter.17.cloned.1.call-start = ((), (), s32[]{:S(2)}) async-start(), calls=%async_computation.27 | async-start | bytes 4259840 | tf_op jit(solution)/shard_map/reduce_scatter | solution.py:390
  (155 other events, 3865.8 us)
Sparse Core Ops, SparseCore 0:
  44.7 71.4 all-gather.6
  117.7 62.0 all-gather.10
  181.9 44.5 all-gather.8
  228.6 57.8 all-gather.12
  287.9 57.8 all-gather.16
  383.5 104.2 all-gather.14
  745.7 53.7 reduce-scatter.6
  821.1 53.0 reduce-scatter.8
  918.9 54.7 reduce-scatter.10
  976.4 43.6 reduce-scatter.12
  1079.5 58.7 reduce-scatter.14
  1140.6 66.9 reduce-scatter.16

commit v8 on v7

--- a/solution.py
+++ b/solution.py
@@ -389,11 +389,12 @@
         ready = after(self.low, *before) if before else self.low
         self.sum = lax.psum_scatter(ready, "fsdp", scatter_dimension=0, tiled=True, axis_index_groups=lines(self.size))
 
-    def total(self, ranks):
-        return lax.all_to_all(self.sum.reshape(ranks, -1, self.sum.shape[1]), "rep", 0, 0)
-
-
-def join_tokens(rows, size):
+    def total(self, ranks, *needs):
+        ready = after(self.sum, *needs) if needs else self.sum
+        return lax.all_to_all(ready.reshape(ranks, -1, ready.shape[1]), "rep", 0, 0)
+
+
+def join_tokens(rows, size, meanwhile=None):
     half = size // 2
 
     def around(block):
@@ -406,7 +407,10 @@
         return jnp.concatenate([held[j] for j in range(half)], axis=0)
 
     beyond = xor_send(rows, "rep", size, half)
-    return around(rows), around(beyond), beyond
+    near = around(rows)
+    if meanwhile is not None:
+        return near, around(after(beyond, meanwhile(near))), beyond
+    return near, around(beyond), beyond
 
 
 def sum_tokens(far, near, size, *needs, last=False):
@@ -527,12 +531,12 @@
         gain_first, gain_second = gains[0:1], gains[1:2]
         every32 = every.astype(f32)
         normed_one = (every32 * rms(every32) * gain_first).astype(bf16)
-        part_r = after(part_r, normed_one)
+        cot = mix(cotangent, 1)
+        part_r = after(part_r, normed_one, cot)
         part_b, part_g, part_u, part_d = (
             part_r[:, :wv], part_r[:, wv : wv + ffq], part_r[:, wv + ffq : wv + 2 * ffq], part_r[:, wv + 2 * ffq :])
         line_2 = gather_line(after(part_2, extra_all), F)
         wa1, side_1 = gather_side(line_1, F)
-        cot = mix(cotangent, 1)
         cot_near, cot_far, unused = join_tokens(after(cot, side_1), R)
         line_b = gather_line(part_b, F)
         line_g = gather_line(after(part_g, side_1), F)
@@ -559,7 +563,7 @@
         mixed, *saved_2 = mixer_fwd(proj_2, proj_1, pos, taps[1], gain_out, prm, dims, 1, 1, [mixed])
         wb, side_b = gather_side(line_b, F, side_2)
         wg, side_g = gather_side(line_g, F, side_b)
-        wd, side_d = gather_side(line_d, F, side_g)
+        side_d = xor_send(after(line_d, side_g), "fsdp", F, 1)
         own32 = own.astype(f32)
         mid = tok // 2
         mixed = after(mixed, line_g, cot_near, cot_far)
@@ -577,18 +581,25 @@
 
         added, unused = sum_tokens(lambda: out_far, near_mixed, R, last=True)
         mixed, saved_2 = kept["mixed"], kept["saved"]
-        middle = own32 + after(added, side_g)
+        middle = own32 + after(added, side_g, line_u, line_d)
         r2 = rms(middle)
         n2 = middle * r2
         normed_own = (n2 * gain_second).astype(bf16)
-        two = join_tokens(normed_own, R)[:2]
         gates, ups, acts, sigs, hiddens = [], [], [], [], []
-        for normed in (after(two[0], line_u), two[1]):
+
+        def gate(normed):
             gates.append(dot(normed, wg))
-            ups.append(dot(after(normed, gates[-1], side_d) if ups else normed, wu))
-            sigs.append(jax.nn.sigmoid(gates[-1]))
-            acts.append(gates[-1] * sigs[-1])
-            hiddens.append((acts[-1] * ups[-1]).astype(bf16))
+            return gates[-1]
+
+        *two, beyond = join_tokens(normed_own, R, gate)
+        gate(two[1])
+        side_d = after(side_d, gates[1])
+        wd = jnp.concatenate([after(line_d, gates[0]), side_d], axis=0)
+        for t, normed in enumerate(two):
+            ups.append(dot(after(normed, gates[1]) if t else after(normed, beyond), wu))
+            sigs.append(jax.nn.sigmoid(gates[t]))
+            acts.append(gates[t] * sigs[t])
+            hiddens.append((acts[t] * ups[t]).astype(bf16))
         hidden = jnp.concatenate(hiddens, axis=0)
         normed_two = jnp.concatenate(two, axis=0)
         cot_all = jnp.concatenate([cot_near, cot_far], axis=0)
@@ -627,20 +638,20 @@
             *args_1, after(dm_far, g_2.sent, t_down), dims, 0, 1, dba, [dp_1, dba_1])
         g_out.side(dp_1)
         g_1 = Summed(normed_one, after(dp_1, g_out.low), F)
-        t_up = g_up.total(R)
 
         def back_one(lo, hi, *needs):
             return dot(after(dp_1, *needs)[lo:hi], wa1, NT) + dot(after(dp_2, *needs)[lo:hi], wa2, NT)
 
-        t_out = g_out.total(R)
 
         def near_one(part):
-            g_2.side(part, before=(g_out.sum,))
-
-            keep("far", dot(after(hiddens[1], g_2.low, g_out.sum, t_up), wd, NT))
-            return keep("one", back_one(0, mid, kept["far"]))
+            g_2.side(part, g_out.sum)
+
+            kept["t_up"], kept["t_out"] = g_up.total(R, g_2.low), g_out.total(R, g_2.low)
+            keep("far", dot(after(hiddens[1], g_2.low, g_out.sum), wd, NT))
+            return keep("one", back_one(0, mid, kept["far"], kept["t_up"]))
 
         dnormed_one, far_one = sum_tokens(lambda: back_one(mid, tok, g_1.sent, g_up.sum, t_gate), near_one, R)
+        t_up, t_out = kept["t_up"], kept["t_out"]
         g_1.side(kept["one"], before=(g_2.sum,))
         added, unused = sum_tokens(lambda: kept["far"], lambda part: dot(after(hiddens[0], g_1.low, t_out), wd, NT), R)
         layer_out = (middle + after(added, g_1.sum)).astype(bf16)

time: 1250 us -> 1230 us (0.984)
  local copies, waits for them, and re-layouts: 215 us -> 183 us
    all_to_all x6, waiting for transfers between devices: 14.4 us -> 45.7 us  [total(): return lax.all_to_all(ready.reshape(ranks, -1, ready.shape[1]), 'rep', 0, 0)]
    ppermute x39, waiting for transfers between devices: 161 us -> 140 us  [xor_send(): return lax.ppermute(value, axis, [(i, i ^ step) for i in range(size)])]
    unnamed x307 -> x301, local copies, waits for them, and re-layouts: 97.1 us -> 89 us
  transfers between devices with their start and end apart: 61 -> 61, of which waited for: 21 -> 22; matrix products, arithmetic and copies ran while one was open for 46% -> 45% of each run, Pallas kernels for 15% -> 15%
where the time goes in v8:
time: 1230 us; the launch traced here: 1220 us
  matrix products  371 us (30%)
  waiting for transfers between devices  277 us (23%)
  local copies, waits for them, and re-layouts  183 us (15%)
  Pallas kernels  183 us (15%)
  other arithmetic  119 us (10%)
  starting transfers between devices  69 us (6%)
  between operations  16.5 us (1%)
    dot_general x34, matrix products, dot(): lax.dot_general(left, right, dims, preferred_element_type=f32).astype(out)  371 us
    ppermute x39, waiting for transfers between devices, xor_send(): return lax.ppermute(value, axis, [(i, i ^ step) for i in range(size)])  140 us
    pallas_call x4, Pallas kernels, mixer_bwd(): pl.pallas_call(functools.partial(bwd_kernel, dims, half, before is not No...  111 us
    unnamed x301, local copies, waits for them, and re-layouts  89 us
    pallas_call x3, Pallas kernels, mixer_fwd(): pl.pallas_call(functools.partial(fwd_kernel, dims, half), grid=(steps,),...  71.9 us
    all_to_all x6, waiting for transfers between devices, total(): return lax.all_to_all(ready.reshape(ranks, -1, ready.shape[1]), 'rep', 0, 0)  45.7 us
    all_gather x6, waiting for transfers between devices, gather_line(): lax.all_gather(rows, 'fsdp', axis=0, tiled=True, axis_index_groups=lines(...  34.1 us
    ppermute x39, starting transfers between devices, xor_send(): return lax.ppermute(value, axis, [(i, i ^ step) for i in range(size)])  29.5 us
  transfers between devices with their start and end apart: 61, of which 22 were waited for; matrix products, arithmetic and copies ran while one was open for 45% of the time, Pallas kernels for 15%

profile of v8, /device:TPU:0, one launch (start us, length us, event | category | flops | bytes accessed | tf_op | source)
XLA Modules:
  0.0 1218.5 jit_solution(16994374547165660416)
XLA Ops:
  72.9 20.3 %all-to-all-done.1 = bf16[32,2,608]{2,1,0:T(2,128)(2,1)S(1)} async-done(((bf16[32,2,608]{2,1,0:T(2,128)(2,1)}), bf16[32,2,608]{2,1,0:T(2,128)(2,1)S(1)}, u32[]{:S(2)}, u32[]{:S(2)}) %all-to-all-start.1) | async-done | bytes 77856 | tf_op jit(solution)/shard_map/all_to_all | solution.py:523
  94.7 21.5 %all-gather.7.cloned.1.call-done = bf16[1024,1664]{1,0:T(8,128)(2,1)} async-done(((bf16[256,1664]{1,0:T(8,128)(2,1)}), bf16[1024,1664]{1,0:T(8,128)(2,1)}) %all-gather.7.cloned.1.call-update) | async-done | bytes 3407888 | tf_op jit(solution)/shard_map/all_gather | solution.py:359
  161.2 50.4 %collective-permute-done.3 = bf16[1024,1664]{1,0:T(8,128)(2,1)} collective-permute-done((bf16[1024,1664]{1,0:T(8,128)(2,1)}, bf16[1024,1664]{1,0:T(8,128)(2,1)}, u32[]{:S(2)}, u32[]{:S(2)}) %collective-permute-start.3) | collective-permute-done | bytes 3407904 | tf_op jit(solution)/shard_map/ppermute | solution.py:347
  237.9 21.2 %fusion.85.refs_0_.refs_1_.refs_2_.refs_3_.refs_4_ = f32[2048,1664]{1,0:T(8,128)} fusion(bf16[2048,2048]{1,0:T(8,128)(2,1)} %fusion.2, bf16[2048,1664]{1,0:T(8,128)(2,1)} %constant_dynamic-update-slice_fusion.13), kind=kOutput, calls=%fused_computation.281 | convolution fusion | flops 13958643712 | bytes 28835840 | tf_op jit(solution)/shard_map/dot_general | solution.py:375
  261.6 34.2 %shard_map.356 = (bf16[2048,1024]{1,0:T(8,128)(2,1)S(1)}, f32[16,256,256]{2,1,0:T(8,128)}, f32[2048,512]{1,0:T(8,128)}, f32[2048,512]{1,0:T(8,128)}) custom-call(f32[2048,1664]{1,0:T(8,128)} %fusion.85.refs_0_.refs_1_.refs_2_.refs_3_.refs_4_, f32[2048,1664]{1,0:T(8,128)} %fusion.85.refs_0_.refs_1_.refs_2_.refs_3_.refs_4_, ...), custom_call_target="tpu_custom_call" | custom-call | flops 4400000000 | bytes 4000000 | tf_op jit(solution)/shard_map/pallas_call | solution.py:277
  322.7 17.6 %fusion.86.refs_0_.refs_1_.refs_2_.refs_3_ = f32[2048,1536]{1,0:T(8,128)} fusion(bf16[2048,2048]{1,0:T(8,128)(2,1)S(1)} %bitcast.176, bf16[2048,1536]{1,0:T(8,128)(2,1)} %constant_dynamic-update-slice_fusion.15), kind=kOutput, calls=%fused_computation.282 | convolution fusion | flops 12884901888 | bytes 27262976 | tf_op jit(solution)/shard_map/dot_general | solution.py:375
  340.3 18.8 %shard_map.357 = (bf16[2048,1024]{1,0:T(8,128)(2,1)S(1)}, f32[16,256,256]{2,1,0:T(8,128)}, f32[2048,512]{1,0:T(8,128)}, f32[2048,512]{1,0:T(8,128)}) custom-call(f32[2048,1536]{1,0:T(8,128)} %fusion.86.refs_0_.refs_1_.refs_2_.refs_3_, f32[2048,1536]{1,0:T(8,128)} %fusion.86.refs_0_.refs_1_.refs_2_.refs_3_, ...), custom_call_target="tpu_custom_call", output_to_operand_aliasing={{0}: (9, {})} | custom-call | flops 13200000000 | bytes 12000000 | tf_op jit(solution)/shard_map/pallas_call | solution.py:277
  384.5 18.8 %shard_map.358 = (bf16[2048,1024]{1,0:T(8,128)(2,1)S(1)}, f32[16,256,256]{2,1,0:T(8,128)}, f32[2048,512]{1,0:T(8,128)}, f32[2048,512]{1,0:T(8,128)}) custom-call(f32[2048,1536]{1,0:T(8,128)} %fusion.86.refs_0_.refs_1_.refs_2_.refs_3_, ...), custom_call_target="tpu_custom_call", output_to_operand_aliasing={{0}: (9, {}), {1}: (10, {}), {2}: (11, {}), {3}: (12, {})} | custom-call | flops 13200000000 | bytes 12000000 | tf_op jit(solution)/shard_map/pallas_call | solution.py:277
  411.6 18.1 %collective-permute-done.14 = bf16[512,2048]{1,0:T(8,128)(2,1)} collective-permute-done((bf16[512,2048]{1,0:T(8,128)(2,1)}, bf16[512,2048]{1,0:T(8,128)(2,1)}, u32[]{:S(2)}, u32[]{:S(2)}) %collective-permute-start.14) | collective-permute-done | bytes 2097184 | tf_op jit(solution)/shard_map/ppermute | solution.py:347
  440.7 12.6 %all-gather.15.cloned.1.call-done = bf16[2048,1408]{1,0:T(8,128)(2,1)} async-done(((bf16[512,1408]{1,0:T(8,128)(2,1)}), bf16[2048,1408]{1,0:T(8,128)(2,1)}) %all-gather.15.cloned.1.call-update) | async-done | bytes 5767184 | tf_op jit(solution)/shard_map/all_gather | solution.py:359
  468.5 36.5 %collective-permute-done.18 = bf16[512,2048]{1,0:T(8,128)(2,1)S(1)} collective-permute-done((bf16[512,2048]{1,0:T(8,128)(2,1)S(1)}, bf16[512,2048]{1,0:T(8,128)(2,1)S(1)}, u32[]{:S(2)}, u32[]{:S(2)}) %collective-permute-start.18) | collective-permute-done | bytes 2097184 | tf_op jit(solution)/shard_map/ppermute | solution.py:347
  564.5 12.5 %multiply_convert_fusion.3 = (bf16[1024,1408]{1,0:T(8,128)(2,1)S(1)}, bf16[1024,1408]{1,0:T(8,128)(2,1)S(1)}) fusion(f32[1024,1408]{1,0:T(8,128)S(1)} %copy-done.93, f32[1024,1408]{1,0:T(8,128)} %get-tuple-element.265, bf16[1024,2048]{1,0:T(8,128)(2,1)} %get-tuple-element.135, bf16[2048,1408]{1,0:T(8,128)(2,1)} %copy-done.55), kind=kOutput, calls=%fused_computation.25 | convolution fusion | flops 5924323328 | bytes 27262976 | tf_op jit(solution)/shard_map/dot_general | solution.py:375
  618.8 14.2 %multiply_convert_fusion.1 = (bf16[1024,1408]{1,0:T(8,128)(2,1)S(1)}, bf16[1024,1408]{1,0:T(8,128)(2,1)S(1)}) fusion(f32[1024,1408]{1,0:T(8,128)} %fusion.70, f32[1024,1408]{1,0:T(8,128)} %get-tuple-element.263, bf16[1024,2048]{1,0:T(8,128)(2,1)} %get-tuple-element.139, bf16[2048,1408]{1,0:T(8,128)(2,1)} %copy-done.55), kind=kOutput, calls=%fused_computation.23 | convolution fusion | flops 5924323328 | bytes 27262976 | tf_op jit(solution)/shard_map/dot_general | solution.py:375
  715.9 27.4 %shard_map.359 = (bf16[2048,1536]{1,0:T(8,128)(2,1)}, f32[2048,128]{1,0:T(8,128)}, f32[4,1024]{1,0:T(4,128)}, f32[1,256]{1,0:T(1,128)}, f32[8,128]{1,0:T(8,128)}) custom-call(f32[2048,1536]{1,0:T(8,128)} %fusion.86.refs_0_.refs_1_.refs_2_.refs_3_, f32[2048,1536]{1,0:T(8,128)} %fusion.86.refs_0_.refs_1_.refs_2_.refs_3_, ...), custom_call_target="tpu_custom_call" | custom-call | flops 28600000512 | bytes 26000000 | tf_op jit(solution)/shard_map/pallas_call | solution.py:322
  791.1 28.4 %shard_map.360 = (bf16[2048,1664]{1,0:T(8,128)(2,1)}, f32[2048,128]{1,0:T(8,128)}, f32[4,1024]{1,0:T(4,128)}, f32[1,256]{1,0:T(1,128)}, f32[8,128]{1,0:T(8,128)}) custom-call(f32[2048,1664]{1,0:T(8,128)} %fusion.85.refs_0_.refs_1_.refs_2_.refs_3_.refs_4_, f32[2048,1664]{1,0:T(8,128)} %fusion.85.refs_0_.refs_1_.refs_2_.refs_3_.refs_4_, ...), custom_call_target="tpu_custom_call" | custom-call | flops 28600000512 | bytes 26000000 | tf_op jit(solution)/shard_map/pallas_call | solution.py:322
  834.6 27.2 %shard_map.361 = (bf16[2048,1536]{1,0:T(8,128)(2,1)}, f32[2048,128]{1,0:T(8,128)}, f32[4,1024]{1,0:T(4,128)}, f32[1,256]{1,0:T(1,128)}, f32[8,128]{1,0:T(8,128)}) custom-call(f32[2048,1536]{1,0:T(8,128)} %fusion.86.refs_0_.refs_1_.refs_2_.refs_3_, ...), custom_call_target="tpu_custom_call", output_to_operand_aliasing={{0}: (13, {}), {1}: (14, {})} | custom-call | flops 28600000512 | bytes 26000000 | tf_op jit(solution)/shard_map/pallas_call | solution.py:322
  889.3 27.9 %shard_map.362 = (bf16[2048,1664]{1,0:T(8,128)(2,1)}, f32[2048,128]{1,0:T(8,128)}, f32[4,1024]{1,0:T(4,128)}, f32[1,256]{1,0:T(1,128)}, f32[8,128]{1,0:T(8,128)}) custom-call(f32[2048,1664]{1,0:T(8,128)} %fusion.85.refs_0_.refs_1_.refs_2_.refs_3_.refs_4_, ...), custom_call_target="tpu_custom_call", output_to_operand_aliasing={{0}: (14, {}), {1}: (15, {})} | custom-call | flops 28600000512 | bytes 26000000 | tf_op jit(solution)/shard_map/pallas_call | solution.py:322
  925.9 12.9 %convolution_convert_fusion.3 = bf16[1024,1664]{1,0:T(8,128)(2,1)} fusion(bf16[2048,1664]{1,0:T(8,128)(2,1)} %get-tuple-element.173, bf16[2048,2048]{1,0:T(8,128)(2,1)} %fusion.2), kind=kOutput, calls=%fused_computation.90 | convolution fusion | flops 6981025792 | bytes 14417920 | tf_op jit(solution)/shard_map/dot_general | solution.py:375
  950.6 12.3 %convolution_add_fusion.1 = f32[1024,2048]{1,0:T(8,128)S(1)} fusion(f32[1024,2048]{1,0:T(8,128)} %fusion.54, bf16[2048,1664]{1,0:T(8,128)(2,1)} %constant_dynamic-update-slice_fusion.13, bf16[2048,1664]{1,0:T(8,128)(2,1)} %get-tuple-element.173), kind=kOutput, calls=%fused_computation.83 | convolution fusion | flops 6981419008 | bytes 27000832 | tf_op jit(solution)/shard_map/dot_general | solution.py:375
  979.2 11.9 add_convert_fusion.1
  1023.7 32.5 %all-to-all-done.5 = bf16[4,64,1408]{2,1,0:T(8,128)(2,1)S(1)} async-done(((bf16[4,64,1408]{2,1,0:T(8,128)(2,1)}), bf16[4,64,1408]{2,1,0:T(8,128)(2,1)S(1)}, u32[]{:S(2)}, u32[]{:S(2)}) %all-to-all-start.5) | async-done | bytes 720928 | tf_op jit(solution)/shard_map/all_to_all | solution.py:394
  1056.1 11.9 fusion.52
  1068.0 14.3 %convolution_add_fusion = f32[1024,2048]{1,0:T(8,128)} fusion(f32[1024,2048]{1,0:T(8,128)} %fusion.52, bf16[2048,1664]{1,0:T(8,128)(2,1)} %constant_dynamic-update-slice_fusion.13, bf16[2048,1664]{1,0:T(8,128)(2,1)} %get-tuple-element.173), kind=kOutput, calls=%fused_computation.82 | convolution fusion | flops 6981419008 | bytes 27000832 | tf_op jit(solution)/shard_map/dot_general | solution.py:375
  1138.6 27.5 %all-to-all-done.7 = f32[32,1,1192]{2,1,0:T(1,128)S(1)} async-done(((f32[32,1,1192]{2,1,0:T(1,128)}), f32[32,1,1192]{2,1,0:T(1,128)S(1)}, u32[]{:S(2)}, u32[]{:S(2)}) %all-to-all-start.7) | async-done | bytes 152608 | tf_op jit(solution)/shard_map/all_to_all | solution.py:700
  (642 shorter events, 671.1 us)
Async XLA Ops:
  20.9 95.3 %all-gather.7.cloned.1.call-start = ((), (), s32[]{:S(2)}) async-start(), calls=%async_computation.16 | async-start | bytes 4259840 | tf_op jit(solution)/shard_map/all_gather | solution.py:359
  46.5 78.1 %collective-permute-start = (bf16[512,2048]{1,0:T(8,128)(2,1)}, bf16[512,2048]{1,0:T(8,128)(2,1)}, u32[]{:S(2)}, u32[]{:S(2)}) collective-permute-start(bf16[512,2048]{1,0:T(8,128)(2,1)} %pad_maximum_fusion.8), channel_id=1, source_target_pairs={{0,1},{1,0},{2,3},{3,2},{4,5},{5,4},{6,7},{7,6},{8,9},{9,8},{10,11... | collective-permute-start | bytes 6291464 | tf_op jit(solution)/shard_map/ppermute | solution.py:347
  68.0 153.6 %all-gather.11.cloned.1.call-start = ((), (), s32[]{:S(2)}) async-start(), calls=%async_computation.18 | async-start | bytes 3932160 | tf_op jit(solution)/shard_map/all_gather | solution.py:359
  124.3 176.1 %all-gather.9.cloned.1.call-start = ((), (), s32[]{:S(2)}) async-start(), calls=%async_computation.17 | async-start | bytes 2621440 | tf_op jit(solution)/shard_map/all_gather | solution.py:359
  135.2 76.4 %collective-permute-start.3 = (bf16[1024,1664]{1,0:T(8,128)(2,1)}, bf16[1024,1664]{1,0:T(8,128)(2,1)}, u32[]{:S(2)}, u32[]{:S(2)}) collective-permute-start(bf16[1024,1664]{1,0:T(8,128)(2,1)} %all-gather.7.cloned.1.call-done), channel_id=1, source_target_pairs={{0,4},{4,0},{8,12},{12,8},{16,20},{20,16},{24,28},{28,24},{1,5},{5... | collective-permute-start | bytes 10223624 | tf_op jit(solution)/shard_map/ppermute | solution.py:347
  158.3 206.9 %all-gather.13.cloned.1.call-start = ((), (), s32[]{:S(2)}) async-start(), calls=%async_computation.19 | async-start | bytes 3604480 | tf_op jit(solution)/shard_map/all_gather | solution.py:359
  211.6 226.9 %all-gather.17.cloned.1.call-start = ((), (), s32[]{:S(2)}) async-start(), calls=%async_computation.21 | async-start | bytes 3604480 | tf_op jit(solution)/shard_map/all_gather | solution.py:359
  229.6 74.0 %collective-permute-start.10 = (bf16[512,2048]{1,0:T(8,128)(2,1)S(1)}, bf16[512,2048]{1,0:T(8,128)(2,1)}, u32[]{:S(2)}, u32[]{:S(2)}) collective-permute-start(bf16[512,2048]{1,0:T(8,128)(2,1)S(1)} %copy-done.24), channel_id=1, source_target_pairs={{0,2},{1,3},{2,0},{3,1},{4,6},{5,7},{6,4},{7,5},{8,10},{9,11},{10,... | collective-permute-start | bytes 6291464 | tf_op jit(solution)/shard_map/ppermute | solution.py:347
  232.6 84.9 %collective-permute-start.8 = (bf16[1024,1536]{1,0:T(8,128)(2,1)}, bf16[1024,1536]{1,0:T(8,128)(2,1)}, u32[]{:S(2)}, u32[]{:S(2)}) collective-permute-start(bf16[1024,1536]{1,0:T(8,128)(2,1)} %all-gather.11.cloned.1.call-done), channel_id=1, source_target_pairs={{0,4},{4,0},{8,12},{12,8},{16,20},{20,16},{24,28},{28,24},{1,5},{5... | collective-permute-start | bytes 9437192 | tf_op jit(solution)/shard_map/ppermute | solution.py:347
  233.3 220.0 %all-gather.15.cloned.1.call-start = ((), (), s32[]{:S(2)}) async-start(), calls=%async_computation.20 | async-start | bytes 7208960 | tf_op jit(solution)/shard_map/all_gather | solution.py:359
  300.3 487.2 %reduce-scatter.7.cloned.1.call-start = ((), (), s32[]{:S(2)}) async-start(), calls=%async_computation.22 | async-start | bytes 3604480 | tf_op jit(solution)/shard_map/reduce_scatter | solution.py:390
  461.3 76.8 %collective-permute-start.20 = (bf16[1024,1408]{1,0:T(8,128)(2,1)S(1)}, bf16[1024,1408]{1,0:T(8,128)(2,1)}, u32[]{:S(2)}, u32[]{:S(2)}) collective-permute-start(bf16[1024,1408]{1,0:T(8,128)(2,1)S(1)} %copy-done.40), channel_id=1, source_target_pairs={{0,4},{4,0},{8,12},{12,8},{16,20},{20,16},{24,28},{28,24},{1,5},{5... | collective-permute-start | bytes 8650760 | tf_op jit(solution)/shard_map/ppermute | solution.py:347
  702.2 170.7 %reduce-scatter.9.cloned.1.call-start = ((), (), s32[]{:S(2)}) async-start(), calls=%async_computation.23 | async-start | bytes 3604480 | tf_op jit(solution)/shard_map/reduce_scatter | solution.py:390
  766.1 95.7 %collective-permute-start.29 = (bf16[1024,1408]{1,0:T(8,128)(2,1)}, bf16[1024,1408]{1,0:T(8,128)(2,1)}, u32[]{:S(2)}, u32[]{:S(2)}) collective-permute-start(bf16[1024,1408]{1,0:T(8,128)(2,1)} %convolution_convert_fusion.1), channel_id=1, source_target_pairs={{0,4},{4,0},{8,12},{12,8},{16,20},{20,16},{24,28},{28,24},{1,5},{5... | collective-permute-start | bytes 8650760 | tf_op jit(solution)/shard_map/ppermute | solution.py:347
  787.5 98.2 %all-to-all-start.3 = ((bf16[4,64,1408]{2,1,0:T(8,128)(2,1)}), bf16[4,64,1408]{2,1,0:T(8,128)(2,1)S(1)}, u32[]{:S(2)}, u32[]{:S(2)}) async-start(bf16[4,64,1408]{2,1,0:T(8,128)(2,1)} %bitcast.206), calls=%async_computation.5 | async-start | bytes 1441792 | tf_op jit(solution)/shard_map/all_to_all | solution.py:394
  791.0 147.8 %reduce-scatter.11.cloned.1.call-start = ((), (), s32[]{:S(2)}) async-start(), calls=%async_computation.24 | async-start | bytes 3604480 | tf_op jit(solution)/shard_map/reduce_scatter | solution.py:390
  833.9 83.3 %collective-permute-start.30 = (bf16[1024,1024]{1,0:T(8,128)(2,1)}, bf16[1024,1024]{1,0:T(8,128)(2,1)}, u32[]{:S(2)}, u32[]{:S(2)}) collective-permute-start(bf16[1024,1024]{1,0:T(8,128)(2,1)} %fusion.62), channel_id=1, source_target_pairs={{0,4},{4,0},{8,12},{12,8},{16,20},{20,16},{24,28},{28,24},{1,5},{5... | collective-permute-start | bytes 6291464 | tf_op jit(solution)/shard_map/ppermute | solution.py:347
  884.4 94.8 %collective-permute-start.32 = (bf16[1024,1536]{1,0:T(8,128)(2,1)}, bf16[1024,1536]{1,0:T(8,128)(2,1)}, u32[]{:S(2)}, u32[]{:S(2)}) collective-permute-start(bf16[1024,1536]{1,0:T(8,128)(2,1)} %convolution_convert_fusion), channel_id=1, source_target_pairs={{0,4},{4,0},{8,12},{12,8},{16,20},{20,16},{24,28},{28,24},{1,5},{5... | collective-permute-start | bytes 9437192 | tf_op jit(solution)/shard_map/ppermute | solution.py:347
  889.3 90.0 %reduce-scatter.13.cloned.1.call-start = ((), (), s32[]{:S(2)}) async-start(), calls=%async_computation.25 | async-start | bytes 2621440 | tf_op jit(solution)/shard_map/reduce_scatter | solution.py:390
  972.4 110.0 %collective-permute-start.33 = (bf16[1024,1664]{1,0:T(8,128)(2,1)}, bf16[1024,1664]{1,0:T(8,128)(2,1)}, u32[]{:S(2)}, u32[]{:S(2)}) collective-permute-start(bf16[1024,1664]{1,0:T(8,128)(2,1)} %convolution_convert_fusion.3), channel_id=1, source_target_pairs={{0,4},{4,0},{8,12},{12,8},{16,20},{20,16},{24,28},{28,24},{1,5},{5... | collective-permute-start | bytes 10223624 | tf_op jit(solution)/shard_map/ppermute | solution.py:347
  994.6 122.2 %reduce-scatter.15.cloned.1.call-start = ((), (), s32[]{:S(2)}) async-start(), calls=%async_computation.26 | async-start | bytes 3932160 | tf_op jit(solution)/shard_map/reduce_scatter | solution.py:390
  996.0 120.9 %collective-permute-start.38 = (bf16[512,2048]{1,0:T(8,128)(2,1)}, bf16[512,2048]{1,0:T(8,128)(2,1)}, u32[]{:S(2)}, u32[]{:S(2)}) collective-permute-start(bf16[512,2048]{1,0:T(8,128)(2,1)} %fusion.17), channel_id=1, source_target_pairs={{0,2},{1,3},{2,0},{3,1},{4,6},{5,7},{6,4},{7,5},{8,10},{9,11},{10,... | collective-permute-start | bytes 6291464 | tf_op jit(solution)/shard_map/ppermute | solution.py:347
  1007.4 177.6 %reduce-scatter.17.cloned.1.call-start = ((), (), s32[]{:S(2)}) async-start(), calls=%async_computation.27 | async-start | bytes 4259840 | tf_op jit(solution)/shard_map/reduce_scatter | solution.py:390
  1022.0 88.8 %collective-permute-start.35 = (bf16[512,2048]{1,0:T(8,128)(2,1)}, bf16[512,2048]{1,0:T(8,128)(2,1)}, u32[]{:S(2)}, u32[]{:S(2)}) collective-permute-start(bf16[512,2048]{1,0:T(8,128)(2,1)} %split.127), channel_id=1, source_target_pairs={{0,1},{1,0},{2,3},{3,2},{4,5},{5,4},{6,7},{7,6},{8,9},{9,8},{10,11... | collective-permute-start | bytes 6291464 | tf_op jit(solution)/shard_map/ppermute | solution.py:347
  (151 other events, 3607.0 us)
Sparse Core Ops, SparseCore 0:
  44.7 71.4 all-gather.6
  117.7 62.0 all-gather.10
  182.0 44.5 all-gather.8
  228.6 57.8 all-gather.12
  287.9 57.8 all-gather.16
  347.8 105.3 all-gather.14
  702.3 54.4 reduce-scatter.6
  776.2 53.5 reduce-scatter.8
  873.1 54.7 reduce-scatter.10
  930.0 43.7 reduce-scatter.12
  997.9 58.8 reduce-scatter.14
  1117.0 65.1 reduce-scatter.16

commit v9 on v8

--- a/solution.py
+++ b/solution.py
@@ -648,12 +648,13 @@
 
             kept["t_up"], kept["t_out"] = g_up.total(R, g_2.low), g_out.total(R, g_2.low)
             keep("far", dot(after(hiddens[1], g_2.low, g_out.sum), wd, NT))
-            return keep("one", back_one(0, mid, kept["far"], kept["t_up"]))
+            return keep("one", back_one(0, mid, kept["far"]))
 
         dnormed_one, far_one = sum_tokens(lambda: back_one(mid, tok, g_1.sent, g_up.sum, t_gate), near_one, R)
         t_up, t_out = kept["t_up"], kept["t_out"]
-        g_1.side(kept["one"], before=(g_2.sum,))
-        added, unused = sum_tokens(lambda: kept["far"], lambda part: dot(after(hiddens[0], g_1.low, t_out), wd, NT), R)
+        near_out = dot(after(hiddens[0], kept["one"]), wd, NT)
+        g_1.side(near_out, t_up, before=(g_2.sum,))
+        added, unused = sum_tokens(lambda: kept["far"], lambda part: after(near_out, t_out, g_1.low), R)
         layer_out = (middle + after(added, g_1.sum)).astype(bf16)
         dprm = dr_1 + dr_2 + er_1 + er_2
         dgain_out = dg_1 + dg_2 + eg_1 + eg_2

time: 1230 us -> 1190 us (0.967)
  waiting for transfers between devices: 277 us -> 240 us
    all_to_all x6, waiting for transfers between devices: 45.7 us -> 9.21 us  [total(): return lax.all_to_all(ready.reshape(ranks, -1, ready.shape[1]), 'rep', 0, 0)]
    unnamed x301 -> x279, local copies, waits for them, and re-layouts: 89 us -> 80.2 us
  transfers between devices with their start and end apart: 61 -> 61, of which waited for: 22 -> 21; matrix products, arithmetic and copies ran while one was open for 45% -> 47% of each run, Pallas kernels for 15% -> 15%
where the time goes in v9:
time: 1190 us; the launch traced here: 1180 us
  matrix products  375 us (32%)
  waiting for transfers between devices  240 us (20%)
  Pallas kernels  183 us (15%)
  local copies, waits for them, and re-layouts  179 us (15%)
  other arithmetic  119 us (10%)
  starting transfers between devices  70 us (6%)
  between operations  16.4 us (1%)
    dot_general x34, matrix products, dot(): lax.dot_general(left, right, dims, preferred_element_type=f32).astype(out)  375 us
    ppermute x39, waiting for transfers between devices, xor_send(): return lax.ppermute(value, axis, [(i, i ^ step) for i in range(size)])  140 us
    pallas_call x4, Pallas kernels, mixer_bwd(): pl.pallas_call(functools.partial(bwd_kernel, dims, half, before is not No...  111 us
    unnamed x279, local copies, waits for them, and re-layouts  80.2 us
    pallas_call x3, Pallas kernels, mixer_fwd(): pl.pallas_call(functools.partial(fwd_kernel, dims, half), grid=(steps,),...  71.9 us
    all_gather x6, waiting for transfers between devices, gather_line(): lax.all_gather(rows, 'fsdp', axis=0, tiled=True, axis_index_groups=lines(...  34.1 us
    ppermute x39, starting transfers between devices, xor_send(): return lax.ppermute(value, axis, [(i, i ^ step) for i in range(size)])  30.8 us
    all_to_all x1, waiting for transfers between devices, on_device(): summed = jnp.sum(lax.all_to_all(packed, both, 0, 0, tiled=True), axis=0)  26.5 us
  transfers between devices with their start and end apart: 61, of which 21 were waited for; matrix products, arithmetic and copies ran while one was open for 47% of the time, Pallas kernels for 15%

profile of v9, /device:TPU:0, one launch (start us, length us, event | category | flops | bytes accessed | tf_op | source)
XLA Modules:
  0.0 1182.6 jit_solution(9681015507908055325)
XLA Ops:
  72.9 20.2 %all-to-all-done.1 = bf16[32,2,608]{2,1,0:T(2,128)(2,1)S(1)} async-done(((bf16[32,2,608]{2,1,0:T(2,128)(2,1)}), bf16[32,2,608]{2,1,0:T(2,128)(2,1)S(1)}, u32[]{:S(2)}, u32[]{:S(2)}) %all-to-all-start.1) | async-done | bytes 77856 | tf_op jit(solution)/shard_map/all_to_all | solution.py:523
  94.6 21.6 %all-gather.7.cloned.1.call-done = bf16[1024,1664]{1,0:T(8,128)(2,1)} async-done(((bf16[256,1664]{1,0:T(8,128)(2,1)}), bf16[1024,1664]{1,0:T(8,128)(2,1)}) %all-gather.7.cloned.1.call-update) | async-done | bytes 3407888 | tf_op jit(solution)/shard_map/all_gather | solution.py:359
  161.3 50.4 %collective-permute-done.3 = bf16[1024,1664]{1,0:T(8,128)(2,1)} collective-permute-done((bf16[1024,1664]{1,0:T(8,128)(2,1)}, bf16[1024,1664]{1,0:T(8,128)(2,1)}, u32[]{:S(2)}, u32[]{:S(2)}) %collective-permute-start.3) | collective-permute-done | bytes 3407904 | tf_op jit(solution)/shard_map/ppermute | solution.py:347
  238.0 21.2 %fusion.84.refs_0_.refs_1_.refs_2_.refs_3_.refs_4_ = f32[2048,1664]{1,0:T(8,128)} fusion(bf16[2048,2048]{1,0:T(8,128)(2,1)} %fusion.2, bf16[2048,1664]{1,0:T(8,128)(2,1)} %constant_dynamic-update-slice_fusion.13), kind=kOutput, calls=%fused_computation.280 | convolution fusion | flops 13958643712 | bytes 28835840 | tf_op jit(solution)/shard_map/dot_general | solution.py:375
  261.7 34.3 %shard_map.356 = (bf16[2048,1024]{1,0:T(8,128)(2,1)S(1)}, f32[16,256,256]{2,1,0:T(8,128)}, f32[2048,512]{1,0:T(8,128)}, f32[2048,512]{1,0:T(8,128)}) custom-call(f32[2048,1664]{1,0:T(8,128)} %fusion.84.refs_0_.refs_1_.refs_2_.refs_3_.refs_4_, f32[2048,1664]{1,0:T(8,128)} %fusion.84.refs_0_.refs_1_.refs_2_.refs_3_.refs_4_, ...), custom_call_target="tpu_custom_call" | custom-call | flops 4400000000 | bytes 4000000 | tf_op jit(solution)/shard_map/pallas_call | solution.py:277
  322.8 17.6 %fusion.85.refs_0_.refs_1_.refs_2_.refs_3_ = f32[2048,1536]{1,0:T(8,128)} fusion(bf16[2048,2048]{1,0:T(8,128)(2,1)S(1)} %bitcast.176, bf16[2048,1536]{1,0:T(8,128)(2,1)} %constant_dynamic-update-slice_fusion.15), kind=kOutput, calls=%fused_computation.281 | convolution fusion | flops 12884901888 | bytes 27262976 | tf_op jit(solution)/shard_map/dot_general | solution.py:375
  340.3 18.9 %shard_map.357 = (bf16[2048,1024]{1,0:T(8,128)(2,1)S(1)}, f32[16,256,256]{2,1,0:T(8,128)}, f32[2048,512]{1,0:T(8,128)}, f32[2048,512]{1,0:T(8,128)}) custom-call(f32[2048,1536]{1,0:T(8,128)} %fusion.85.refs_0_.refs_1_.refs_2_.refs_3_, f32[2048,1536]{1,0:T(8,128)} %fusion.85.refs_0_.refs_1_.refs_2_.refs_3_, ...), custom_call_target="tpu_custom_call", output_to_operand_aliasing={{0}: (9, {})} | custom-call | flops 13200000000 | bytes 12000000 | tf_op jit(solution)/shard_map/pallas_call | solution.py:277
  384.7 18.8 %shard_map.358 = (bf16[2048,1024]{1,0:T(8,128)(2,1)S(1)}, f32[16,256,256]{2,1,0:T(8,128)}, f32[2048,512]{1,0:T(8,128)}, f32[2048,512]{1,0:T(8,128)}) custom-call(f32[2048,1536]{1,0:T(8,128)} %fusion.85.refs_0_.refs_1_.refs_2_.refs_3_, ...), custom_call_target="tpu_custom_call", output_to_operand_aliasing={{0}: (9, {}), {1}: (10, {}), {2}: (11, {}), {3}: (12, {})} | custom-call | flops 13200000000 | bytes 12000000 | tf_op jit(solution)/shard_map/pallas_call | solution.py:277
  411.7 18.1 %collective-permute-done.14 = bf16[512,2048]{1,0:T(8,128)(2,1)} collective-permute-done((bf16[512,2048]{1,0:T(8,128)(2,1)}, bf16[512,2048]{1,0:T(8,128)(2,1)}, u32[]{:S(2)}, u32[]{:S(2)}) %collective-permute-start.14) | collective-permute-done | bytes 2097184 | tf_op jit(solution)/shard_map/ppermute | solution.py:347
  440.8 12.5 %all-gather.15.cloned.1.call-done = bf16[2048,1408]{1,0:T(8,128)(2,1)} async-done(((bf16[512,1408]{1,0:T(8,128)(2,1)}), bf16[2048,1408]{1,0:T(8,128)(2,1)}) %all-gather.15.cloned.1.call-update) | async-done | bytes 5767184 | tf_op jit(solution)/shard_map/all_gather | solution.py:359
  468.5 36.5 %collective-permute-done.18 = bf16[512,2048]{1,0:T(8,128)(2,1)S(1)} collective-permute-done((bf16[512,2048]{1,0:T(8,128)(2,1)S(1)}, bf16[512,2048]{1,0:T(8,128)(2,1)S(1)}, u32[]{:S(2)}, u32[]{:S(2)}) %collective-permute-start.18) | collective-permute-done | bytes 2097184 | tf_op jit(solution)/shard_map/ppermute | solution.py:347
  564.5 12.5 %multiply_convert_fusion.3 = (bf16[1024,1408]{1,0:T(8,128)(2,1)S(1)}, bf16[1024,1408]{1,0:T(8,128)(2,1)S(1)}) fusion(f32[1024,1408]{1,0:T(8,128)S(1)} %copy-done.88, f32[1024,1408]{1,0:T(8,128)} %get-tuple-element.265, bf16[1024,2048]{1,0:T(8,128)(2,1)} %get-tuple-element.136, bf16[2048,1408]{1,0:T(8,128)(2,1)} %copy-done.53), kind=kOutput, calls=%fused_computation.25 | convolution fusion | flops 5924323328 | bytes 27262976 | tf_op jit(solution)/shard_map/dot_general | solution.py:375
  618.8 14.2 %multiply_convert_fusion.1 = (bf16[1024,1408]{1,0:T(8,128)(2,1)S(1)}, bf16[1024,1408]{1,0:T(8,128)(2,1)S(1)}) fusion(f32[1024,1408]{1,0:T(8,128)} %fusion.69, f32[1024,1408]{1,0:T(8,128)} %get-tuple-element.267, bf16[1024,2048]{1,0:T(8,128)(2,1)} %get-tuple-element.140, bf16[2048,1408]{1,0:T(8,128)(2,1)} %copy-done.53), kind=kOutput, calls=%fused_computation.23 | convolution fusion | flops 5924323328 | bytes 27262976 | tf_op jit(solution)/shard_map/dot_general | solution.py:375
  716.5 27.4 %shard_map.359 = (bf16[2048,1536]{1,0:T(8,128)(2,1)}, f32[2048,128]{1,0:T(8,128)}, f32[4,1024]{1,0:T(4,128)}, f32[1,256]{1,0:T(1,128)}, f32[8,128]{1,0:T(8,128)}) custom-call(f32[2048,1536]{1,0:T(8,128)} %fusion.85.refs_0_.refs_1_.refs_2_.refs_3_, f32[2048,1536]{1,0:T(8,128)} %fusion.85.refs_0_.refs_1_.refs_2_.refs_3_, ...), custom_call_target="tpu_custom_call" | custom-call | flops 28600000512 | bytes 26000000 | tf_op jit(solution)/shard_map/pallas_call | solution.py:322
  792.7 28.4 %shard_map.360 = (bf16[2048,1664]{1,0:T(8,128)(2,1)}, f32[2048,128]{1,0:T(8,128)}, f32[4,1024]{1,0:T(4,128)}, f32[1,256]{1,0:T(1,128)}, f32[8,128]{1,0:T(8,128)}) custom-call(f32[2048,1664]{1,0:T(8,128)} %fusion.84.refs_0_.refs_1_.refs_2_.refs_3_.refs_4_, f32[2048,1664]{1,0:T(8,128)} %fusion.84.refs_0_.refs_1_.refs_2_.refs_3_.refs_4_, ...), custom_call_target="tpu_custom_call" | custom-call | flops 28600000512 | bytes 26000000 | tf_op jit(solution)/shard_map/pallas_call | solution.py:322
  836.1 27.2 %shard_map.361 = (bf16[2048,1536]{1,0:T(8,128)(2,1)}, f32[2048,128]{1,0:T(8,128)}, f32[4,1024]{1,0:T(4,128)}, f32[1,256]{1,0:T(1,128)}, f32[8,128]{1,0:T(8,128)}) custom-call(f32[2048,1536]{1,0:T(8,128)} %fusion.85.refs_0_.refs_1_.refs_2_.refs_3_, ...), custom_call_target="tpu_custom_call", output_to_operand_aliasing={{0}: (13, {}), {1}: (14, {})} | custom-call | flops 28600000512 | bytes 26000000 | tf_op jit(solution)/shard_map/pallas_call | solution.py:322
  891.6 27.9 %shard_map.362 = (bf16[2048,1664]{1,0:T(8,128)(2,1)}, f32[2048,128]{1,0:T(8,128)}, f32[4,1024]{1,0:T(4,128)}, f32[1,256]{1,0:T(1,128)}, f32[8,128]{1,0:T(8,128)}) custom-call(f32[2048,1664]{1,0:T(8,128)} %fusion.84.refs_0_.refs_1_.refs_2_.refs_3_.refs_4_, ...), custom_call_target="tpu_custom_call", output_to_operand_aliasing={{0}: (14, {}), {1}: (15, {})} | custom-call | flops 28600000512 | bytes 26000000 | tf_op jit(solution)/shard_map/pallas_call | solution.py:322
  928.1 12.9 %convolution_convert_fusion.3 = bf16[1024,1664]{1,0:T(8,128)(2,1)} fusion(bf16[2048,1664]{1,0:T(8,128)(2,1)} %get-tuple-element.176, bf16[2048,2048]{1,0:T(8,128)(2,1)} %fusion.2), kind=kOutput, calls=%fused_computation.89 | convolution fusion | flops 6981025792 | bytes 14417920 | tf_op jit(solution)/shard_map/dot_general | solution.py:375
  952.9 12.3 %convolution_add_fusion.1 = f32[1024,2048]{1,0:T(8,128)S(1)} fusion(f32[1024,2048]{1,0:T(8,128)} %fusion.53, bf16[2048,1664]{1,0:T(8,128)(2,1)} %constant_dynamic-update-slice_fusion.13, bf16[2048,1664]{1,0:T(8,128)(2,1)} %get-tuple-element.176), kind=kOutput, calls=%fused_computation.82 | convolution fusion | flops 6981419008 | bytes 27000832 | tf_op jit(solution)/shard_map/dot_general | solution.py:375
  979.7 12.1 %add_convert_fusion.1 = bf16[1024,1536]{1,0:T(8,128)(2,1)} fusion(bf16[1024,1536]{1,0:T(8,128)(2,1)} %collective-permute-done.32, bf16[2048,1536]{1,0:T(8,128)(2,1)} %get-tuple-element.172, bf16[2048,2048]{1,0:T(8,128)(2,1)} %fusion.2), kind=kOutput, calls=%fused_computation.9 | convolution fusion | flops 6447169536 | bytes 16777216 | tf_op jit(solution)/shard_map/dot_general | solution.py:375
  1016.0 13.2 %convolution_add_fusion = f32[1024,2048]{1,0:T(8,128)} fusion(f32[1024,2048]{1,0:T(8,128)S(1)} %fusion.51, bf16[2048,1664]{1,0:T(8,128)(2,1)} %constant_dynamic-update-slice_fusion.13, bf16[2048,1664]{1,0:T(8,128)(2,1)} %get-tuple-element.176), kind=kOutput, calls=%fused_computation.81 | convolution fusion | flops 6981419008 | bytes 27000832 | tf_op jit(solution)/shard_map/dot_general | solution.py:375
  1034.8 12.1 %fusion.91 = f32[1024,2048]{1,0:T(8,128)} fusion(bf16[1024,1408]{1,0:T(8,128)(2,1)} %copy-done.39, bf16[2048,1408]{1,0:T(8,128)(2,1)} %copy-done.53), kind=kOutput, calls=%fused_computation.287 | convolution fusion | flops 5905580032 | bytes 17039360 | tf_op jit(solution)/shard_map/dot_general | solution.py:375
  1057.7 13.4 %add_convert_fusion = bf16[1024,1664]{1,0:T(8,128)(2,1)} fusion(bf16[1024,1664]{1,0:T(8,128)(2,1)} %collective-permute-done.33, bf16[2048,1664]{1,0:T(8,128)(2,1)} %get-tuple-element.176, bf16[2048,2048]{1,0:T(8,128)(2,1)} %fusion.2), kind=kOutput, calls=%fused_computation.8 | convolution fusion | flops 6984433664 | bytes 17825792 | tf_op jit(solution)/shard_map/dot_general | solution.py:375
  1103.7 26.5 %all-to-all-done.7 = f32[32,1,1192]{2,1,0:T(1,128)S(1)} async-done(((f32[32,1,1192]{2,1,0:T(1,128)}), f32[32,1,1192]{2,1,0:T(1,128)S(1)}, u32[]{:S(2)}, u32[]{:S(2)}) %all-to-all-start.7) | async-done | bytes 152608 | tf_op jit(solution)/shard_map/all_to_all | solution.py:701
  (618 shorter events, 656.3 us)
Async XLA Ops:
  20.9 95.3 %all-gather.7.cloned.1.call-start = ((), (), s32[]{:S(2)}) async-start(), calls=%async_computation.16 | async-start | bytes 4259840 | tf_op jit(solution)/shard_map/all_gather | solution.py:359
  46.4 78.2 %collective-permute-start = (bf16[512,2048]{1,0:T(8,128)(2,1)}, bf16[512,2048]{1,0:T(8,128)(2,1)}, u32[]{:S(2)}, u32[]{:S(2)}) collective-permute-start(bf16[512,2048]{1,0:T(8,128)(2,1)} %pad_maximum_fusion.8), channel_id=1, source_target_pairs={{0,1},{1,0},{2,3},{3,2},{4,5},{5,4},{6,7},{7,6},{8,9},{9,8},{10,11... | collective-permute-start | bytes 6291464 | tf_op jit(solution)/shard_map/ppermute | solution.py:347
  68.0 153.7 %all-gather.11.cloned.1.call-start = ((), (), s32[]{:S(2)}) async-start(), calls=%async_computation.18 | async-start | bytes 3932160 | tf_op jit(solution)/shard_map/all_gather | solution.py:359
  124.4 176.0 %all-gather.9.cloned.1.call-start = ((), (), s32[]{:S(2)}) async-start(), calls=%async_computation.17 | async-start | bytes 2621440 | tf_op jit(solution)/shard_map/all_gather | solution.py:359
  135.2 76.4 %collective-permute-start.3 = (bf16[1024,1664]{1,0:T(8,128)(2,1)}, bf16[1024,1664]{1,0:T(8,128)(2,1)}, u32[]{:S(2)}, u32[]{:S(2)}) collective-permute-start(bf16[1024,1664]{1,0:T(8,128)(2,1)} %all-gather.7.cloned.1.call-done), channel_id=1, source_target_pairs={{0,4},{4,0},{8,12},{12,8},{16,20},{20,16},{24,28},{28,24},{1,5},{5... | collective-permute-start | bytes 10223624 | tf_op jit(solution)/shard_map/ppermute | solution.py:347
  158.3 207.0 %all-gather.13.cloned.1.call-start = ((), (), s32[]{:S(2)}) async-start(), calls=%async_computation.19 | async-start | bytes 3604480 | tf_op jit(solution)/shard_map/all_gather | solution.py:359
  211.7 227.0 %all-gather.17.cloned.1.call-start = ((), (), s32[]{:S(2)}) async-start(), calls=%async_computation.21 | async-start | bytes 3604480 | tf_op jit(solution)/shard_map/all_gather | solution.py:359
  229.6 73.8 %collective-permute-start.10 = (bf16[512,2048]{1,0:T(8,128)(2,1)S(1)}, bf16[512,2048]{1,0:T(8,128)(2,1)}, u32[]{:S(2)}, u32[]{:S(2)}) collective-permute-start(bf16[512,2048]{1,0:T(8,128)(2,1)S(1)} %copy-done.24), channel_id=1, source_target_pairs={{0,2},{1,3},{2,0},{3,1},{4,6},{5,7},{6,4},{7,5},{8,10},{9,11},{10,... | collective-permute-start | bytes 6291464 | tf_op jit(solution)/shard_map/ppermute | solution.py:347
  231.3 72.2 %collective-permute-start.9 = (bf16[512,2048]{1,0:T(8,128)(2,1)S(1)}, bf16[512,2048]{1,0:T(8,128)(2,1)}, u32[]{:S(2)}, u32[]{:S(2)}) collective-permute-start(bf16[512,2048]{1,0:T(8,128)(2,1)S(1)} %copy-done.24), channel_id=1, source_target_pairs={{0,1},{1,0},{2,3},{3,2},{4,5},{5,4},{6,7},{7,6},{8,9},{9,8},{10,11... | collective-permute-start | bytes 6291464 | tf_op jit(solution)/shard_map/ppermute | solution.py:347
  232.7 84.8 %collective-permute-start.8 = (bf16[1024,1536]{1,0:T(8,128)(2,1)}, bf16[1024,1536]{1,0:T(8,128)(2,1)}, u32[]{:S(2)}, u32[]{:S(2)}) collective-permute-start(bf16[1024,1536]{1,0:T(8,128)(2,1)} %all-gather.11.cloned.1.call-done), channel_id=1, source_target_pairs={{0,4},{4,0},{8,12},{12,8},{16,20},{20,16},{24,28},{28,24},{1,5},{5... | collective-permute-start | bytes 9437192 | tf_op jit(solution)/shard_map/ppermute | solution.py:347
  233.3 219.9 %all-gather.15.cloned.1.call-start = ((), (), s32[]{:S(2)}) async-start(), calls=%async_computation.20 | async-start | bytes 7208960 | tf_op jit(solution)/shard_map/all_gather | solution.py:359
  300.2 488.9 %reduce-scatter.7.cloned.1.call-start = ((), (), s32[]{:S(2)}) async-start(), calls=%async_computation.22 | async-start | bytes 3604480 | tf_op jit(solution)/shard_map/reduce_scatter | solution.py:390
  461.3 76.8 %collective-permute-start.20 = (bf16[1024,1408]{1,0:T(8,128)(2,1)S(1)}, bf16[1024,1408]{1,0:T(8,128)(2,1)}, u32[]{:S(2)}, u32[]{:S(2)}) collective-permute-start(bf16[1024,1408]{1,0:T(8,128)(2,1)S(1)} %copy-done.38), channel_id=1, source_target_pairs={{0,4},{4,0},{8,12},{12,8},{16,20},{20,16},{24,28},{28,24},{1,5},{5... | collective-permute-start | bytes 8650760 | tf_op jit(solution)/shard_map/ppermute | solution.py:347
  702.2 173.0 %reduce-scatter.9.cloned.1.call-start = ((), (), s32[]{:S(2)}) async-start(), calls=%async_computation.23 | async-start | bytes 3604480 | tf_op jit(solution)/shard_map/reduce_scatter | solution.py:390
  766.2 97.9 %collective-permute-start.29 = (bf16[1024,1408]{1,0:T(8,128)(2,1)}, bf16[1024,1408]{1,0:T(8,128)(2,1)}, u32[]{:S(2)}, u32[]{:S(2)}) collective-permute-start(bf16[1024,1408]{1,0:T(8,128)(2,1)} %convolution_convert_fusion.1), channel_id=1, source_target_pairs={{0,4},{4,0},{8,12},{12,8},{16,20},{20,16},{24,28},{28,24},{1,5},{5... | collective-permute-start | bytes 8650760 | tf_op jit(solution)/shard_map/ppermute | solution.py:347
  789.1 98.9 %all-to-all-start.3 = ((bf16[4,64,1408]{2,1,0:T(8,128)(2,1)}), bf16[4,64,1408]{2,1,0:T(8,128)(2,1)S(1)}, u32[]{:S(2)}, u32[]{:S(2)}) async-start(bf16[4,64,1408]{2,1,0:T(8,128)(2,1)} %bitcast.202), calls=%async_computation.5 | async-start | bytes 1441792 | tf_op jit(solution)/shard_map/all_to_all | solution.py:394
  792.6 148.5 %reduce-scatter.11.cloned.1.call-start = ((), (), s32[]{:S(2)}) async-start(), calls=%async_computation.24 | async-start | bytes 3604480 | tf_op jit(solution)/shard_map/reduce_scatter | solution.py:390
  835.4 84.1 %collective-permute-start.30 = (bf16[1024,1024]{1,0:T(8,128)(2,1)}, bf16[1024,1024]{1,0:T(8,128)(2,1)}, u32[]{:S(2)}, u32[]{:S(2)}) collective-permute-start(bf16[1024,1024]{1,0:T(8,128)(2,1)} %fusion.61), channel_id=1, source_target_pairs={{0,4},{4,0},{8,12},{12,8},{16,20},{20,16},{24,28},{28,24},{1,5},{5... | collective-permute-start | bytes 6291464 | tf_op jit(solution)/shard_map/ppermute | solution.py:347
  886.7 93.0 %collective-permute-start.32 = (bf16[1024,1536]{1,0:T(8,128)(2,1)}, bf16[1024,1536]{1,0:T(8,128)(2,1)}, u32[]{:S(2)}, u32[]{:S(2)}) collective-permute-start(bf16[1024,1536]{1,0:T(8,128)(2,1)} %convolution_convert_fusion), channel_id=1, source_target_pairs={{0,4},{4,0},{8,12},{12,8},{16,20},{20,16},{24,28},{28,24},{1,5},{5... | collective-permute-start | bytes 9437192 | tf_op jit(solution)/shard_map/ppermute | solution.py:347
  891.5 88.1 %reduce-scatter.13.cloned.1.call-start = ((), (), s32[]{:S(2)}) async-start(), calls=%async_computation.25 | async-start | bytes 2621440 | tf_op jit(solution)/shard_map/reduce_scatter | solution.py:390
  928.1 153.9 %reduce-scatter.15.cloned.1.call-start = ((), (), s32[]{:S(2)}) async-start(), calls=%async_computation.26 | async-start | bytes 3932160 | tf_op jit(solution)/shard_map/reduce_scatter | solution.py:390
  969.7 88.0 %collective-permute-start.33 = (bf16[1024,1664]{1,0:T(8,128)(2,1)}, bf16[1024,1664]{1,0:T(8,128)(2,1)}, u32[]{:S(2)}, u32[]{:S(2)}) collective-permute-start(bf16[1024,1664]{1,0:T(8,128)(2,1)} %convolution_convert_fusion.3), channel_id=1, source_target_pairs={{0,4},{4,0},{8,12},{12,8},{16,20},{20,16},{24,28},{28,24},{1,5},{5... | collective-permute-start | bytes 10223624 | tf_op jit(solution)/shard_map/ppermute | solution.py:347
  977.6 104.4 %collective-permute-start.38 = (bf16[512,2048]{1,0:T(8,128)(2,1)}, bf16[512,2048]{1,0:T(8,128)(2,1)}, u32[]{:S(2)}, u32[]{:S(2)}) collective-permute-start(bf16[512,2048]{1,0:T(8,128)(2,1)} %fusion.16), channel_id=1, source_target_pairs={{0,2},{1,3},{2,0},{3,1},{4,6},{5,7},{6,4},{7,5},{8,10},{9,11},{10,... | collective-permute-start | bytes 6291464 | tf_op jit(solution)/shard_map/ppermute | solution.py:347
  1034.8 114.5 %reduce-scatter.17.cloned.1.call-start = ((), (), s32[]{:S(2)}) async-start(), calls=%async_computation.27 | async-start | bytes 4259840 | tf_op jit(solution)/shard_map/reduce_scatter | solution.py:390
  (141 other events, 3556.6 us)
Sparse Core Ops, SparseCore 0:
  44.6 71.4 all-gather.6
  117.7 62.0 all-gather.10
  181.9 44.5 all-gather.8
  228.6 57.8 all-gather.12
  287.9 57.8 all-gather.16
  347.8 105.3 all-gather.14
  702.3 54.4 reduce-scatter.6
  777.7 53.5 reduce-scatter.8
  875.4 54.6 reduce-scatter.10
  932.2 43.6 reduce-scatter.12
  992.0 57.4 reduce-scatter.14
  1082.2 64.0 reduce-scatter.16
